TPU v7x, 32 devices: a whole 2x2x4 slice. The times are simulated.
32 devices in a mesh: dp: 8 (over y, x, core), tensor: 4 (over z).
Axes of the slice: x: 2, y: 2, z: 4, core: 2. Of those that a mesh axis runs over, the one named last changes fastest.
Arguments:
- layer_input: bfloat16 [16384, 768], P('dp'), may hold values from -6 to 6
- segment_ids: int32 [16384], P('dp'), may hold values from -1 to 3, as said below
- w_qkv: bfloat16 [768, 12, 192], P(None, 'tensor'), may hold values from -0.21875 to 0.21875
- qv_bias: bfloat16 [12, 128], P('tensor'), may hold values from -3 to 3
- w_out: bfloat16 [768, 768], P('tensor'), may hold values from -0.875 to 0.875
- out_bias: bfloat16 [768], replicated, may hold values from -2 to 2
- norm1_gain: bfloat16 [768], replicated, may hold values from 0.25 to 1.75
- norm1_bias: bfloat16 [768], replicated, may hold values from -2 to 2
- w_up: bfloat16 [768, 3072], P(None, 'tensor'), may hold values from -0.21875 to 0.21875
- up_bias: bfloat16 [3072], P('tensor'), may hold values from -3 to 3
- w_down: bfloat16 [3072, 768], P('tensor'), may hold values from -0.109375 to 0.109375
- down_bias: bfloat16 [768], replicated, may hold values from -2 to 2
- norm2_gain: bfloat16 [768], replicated, may hold values from 0.25 to 1.75
- norm2_bias: bfloat16 [768], replicated, may hold values from -2 to 2
- out_cotangent: bfloat16 [16384, 768], P(('dp', 'tensor')), may hold values from -6 to 6
Outputs:
- layer_output: bfloat16 [16384, 768], P(('dp', 'tensor'))
- input_grad: float32 [16384, 768], P(('dp', 'tensor'))
- grad_qkv: float32 [768, 12, 192], P(None, 'tensor')
- grad_qv_bias: float32 [12, 128], P('tensor')
- grad_out: float32 [768, 768], P('tensor')
- grad_out_bias: float32 [768], replicated
- grad_norm1_gain: float32 [768], replicated
- grad_norm1_bias: float32 [768], replicated
- grad_up: float32 [768, 3072], P(None, 'tensor')
- grad_up_bias: float32 [3072], P('tensor')
- grad_down: float32 [3072, 768], P('tensor')
- grad_down_bias: float32 [768], replicated
- grad_norm2_gain: float32 [768], replicated
- grad_norm2_bias: float32 [768], replicated
Inputs may be any that keep to these rules, and one draw needn't show every extreme that they name: `segment_ids`: the 8 blocks of 2048 consecutive tokens (those of one index of dp) each hold their live rows first: some wholly live rows, then one row whose live tokens form a prefix of 256 tokens or more, then wholly padded rows (-1). One block is wholly live; every other block has padding. In a live row the segment numbers start at 0 and never fall; a wholly live row has exactly 4 segments.
All inputs are finite; a program needn't handle non-finite values.
Results may differ from a plain program's by a relative error of at most 0.02.
Values may be sent and summed in bfloat16 or wider, within the bound.
A program may use at most 128 MiB of HBM per device.

v0:
```python
import jax
import jax.numpy as jnp
from jax import lax
from jax.sharding import PartitionSpec as P

SEQ = 1024


EPSILON = 1e-06
MASKED = -1e30


def layer_norm(summed, norm_gain, norm_shift):
    row_mean = jnp.mean(summed, axis=-1, keepdims=True)
    centred = summed - row_mean
    spread = jnp.mean(centred * centred, axis=-1, keepdims=True)
    return centred * lax.rsqrt(spread + EPSILON) * norm_gain + norm_shift


def gelu_exact(inputs):
    return jax.nn.gelu(inputs, approximate=False)


def contract_rows(left_side, right_side):
    return lax.dot_general(
        left_side, right_side, (((0,), (0,)), ((), ())), preferred_element_type=jnp.float32
    )


def contract_cols(left_side, right_side):
    return lax.dot_general(
        left_side, right_side, (((1,), (1,)), ((), ())), preferred_element_type=jnp.float32
    )


def row_scores(queries, keys_row, segment, score_scale):
    raw_scores = jnp.einsum("qhd,khd->hqk", queries, keys_row, preferred_element_type=jnp.float32)
    allowed = segment[:, None] == segment[None, :]
    return jnp.where(allowed[None], raw_scores * score_scale, MASKED)


def on_device(
    layer_input,
    segment_ids,
    w_qkv,
    qv_bias,
    w_out,
    out_bias,
    norm1_gain,
    norm1_bias,
    w_up,
    up_bias,
    w_down,
    down_bias,
    norm2_gain,
    norm2_bias,
    out_cotangent,
):
    tensor_count = lax.axis_size("tensor")
    tensor_place = lax.axis_index("tensor")
    token_count, feature_count = layer_input.shape
    share_rows = token_count // tensor_count
    local_heads = qv_bias.shape[0]
    head_dim = qv_bias.shape[1] // 2
    score_scale = float(head_dim) ** (-0.5)
    row_length = SEQ
    row_count = token_count // row_length
    first_row = tensor_place * share_rows

    def own_rows(matrix):
        return lax.dynamic_slice_in_dim(matrix, first_row, share_rows, 0)

    def attend_forward(packed):
        queries, keys_row, values_row, segment = packed
        scores = row_scores(queries, keys_row, segment, score_scale)
        row_top = jnp.max(scores, axis=-1, keepdims=True)
        exponent = jnp.exp(scores - row_top)
        row_total = jnp.sum(exponent, axis=-1, keepdims=True)
        probability = exponent / row_total
        attended_row = jnp.einsum(
            "hqk,khd->qhd",
            probability.astype(jnp.bfloat16),
            values_row,
            preferred_element_type=jnp.float32,
        )
        return (attended_row, (row_top + jnp.log(row_total))[..., 0])

    def attend_backward(packed):
        queries, keys_row, values_row, segment, grad_row, log_total = packed
        scores = row_scores(queries, keys_row, segment, score_scale)
        probability = jnp.exp(scores - log_total[..., None])
        grad_values = jnp.einsum(
            "hqk,qhd->khd",
            probability.astype(jnp.bfloat16),
            grad_row,
            preferred_element_type=jnp.float32,
        )
        grad_probs = jnp.einsum(
            "qhd,khd->hqk", grad_row, values_row, preferred_element_type=jnp.float32
        )
        inner_sum = jnp.sum(probability * grad_probs, axis=-1, keepdims=True)
        grad_raw = (probability * (grad_probs - inner_sum) * score_scale).astype(jnp.bfloat16)
        grad_queries = jnp.einsum(
            "hqk,khd->qhd", grad_raw, keys_row, preferred_element_type=jnp.float32
        )
        grad_keys = jnp.einsum(
            "hqk,qhd->khd", grad_raw, queries, preferred_element_type=jnp.float32
        )
        return jnp.concatenate([grad_queries, grad_keys, grad_values], axis=-1).astype(jnp.bfloat16)

    gain_first = norm1_gain.astype(jnp.float32)
    shift_first = norm1_bias.astype(jnp.float32)
    gain_second = norm2_gain.astype(jnp.float32)
    shift_second = norm2_bias.astype(jnp.float32)
    joined_weight = w_qkv.reshape(feature_count, local_heads * 3 * head_dim)
    key_zeros = jnp.zeros((local_heads, head_dim), jnp.float32)
    joined_bias = jnp.concatenate(
        [
            qv_bias[:, :head_dim].astype(jnp.float32),
            key_zeros,
            qv_bias[:, head_dim:].astype(jnp.float32),
        ],
        axis=1,
    )
    projected = (
        jnp.dot(layer_input, joined_weight, preferred_element_type=jnp.float32).reshape(
            token_count, local_heads, 3 * head_dim
        )
        + joined_bias
    )
    projected = projected.astype(jnp.bfloat16).reshape(
        row_count, row_length, local_heads, 3 * head_dim
    )
    queries_all = projected[..., :head_dim]
    keys_all = projected[..., head_dim : 2 * head_dim]
    values_all = projected[..., 2 * head_dim :]
    segments = segment_ids.reshape(row_count, row_length)
    attended, log_totals = lax.map(attend_forward, (queries_all, keys_all, values_all, segments))
    attended = attended.reshape(token_count, local_heads * head_dim).astype(jnp.bfloat16)
    attn_part = jnp.dot(attended, w_out, preferred_element_type=jnp.float32)
    attn_full = lax.psum(attn_part.astype(jnp.bfloat16), "tensor").astype(jnp.float32)
    first_full = layer_input.astype(jnp.float32) + attn_full + out_bias.astype(jnp.float32)
    hidden_full = layer_norm(first_full, gain_first, shift_first)
    hidden_low = hidden_full.astype(jnp.bfloat16)
    first_sum = own_rows(first_full)
    hidden_own = own_rows(hidden_full)
    up_pre = jnp.dot(hidden_low, w_up, preferred_element_type=jnp.float32) + up_bias.astype(
        jnp.float32
    )
    activation = gelu_exact(up_pre).astype(jnp.bfloat16)
    ffn_part = jnp.dot(activation, w_down, preferred_element_type=jnp.float32)
    ffn_full = lax.psum(ffn_part.astype(jnp.bfloat16), "tensor").astype(jnp.float32)
    ffn_own = own_rows(ffn_full)
    second_sum = hidden_own + ffn_own + down_bias.astype(jnp.float32)
    result, second_back = jax.vjp(layer_norm, second_sum, gain_second, shift_second)
    output = result.astype(jnp.bfloat16)
    live_own = (own_rows(segment_ids) >= 0).astype(jnp.float32)
    cotangent = out_cotangent.astype(jnp.float32) * live_own[:, None]
    grad_second, grad_gain_second, grad_shift_second = second_back(cotangent)
    grad_down_bias = jnp.sum(grad_second, axis=0)
    second_low = lax.all_gather(grad_second.astype(jnp.bfloat16), "tensor", axis=0, tiled=True)
    grad_down = contract_rows(activation, second_low)
    grad_activation = contract_cols(second_low, w_down)
    gelu_value, gelu_back = jax.vjp(gelu_exact, up_pre)
    grad_up_pre = gelu_back(grad_activation)[0].astype(jnp.bfloat16)
    grad_up = contract_rows(hidden_low, grad_up_pre)
    grad_up_bias = jnp.sum(grad_up_pre.astype(jnp.float32), axis=0)
    hidden_part = contract_cols(grad_up_pre, w_up)
    grad_hidden = (
        lax.psum_scatter(
            hidden_part.astype(jnp.bfloat16), "tensor", scatter_dimension=0, tiled=True
        ).astype(jnp.float32)
        + grad_second
    )
    first_value, first_back = jax.vjp(layer_norm, first_sum, gain_first, shift_first)
    grad_first, grad_gain_first, grad_shift_first = first_back(grad_hidden)
    grad_out_bias = jnp.sum(grad_first, axis=0)
    first_low = lax.all_gather(grad_first.astype(jnp.bfloat16), "tensor", axis=0, tiled=True)
    grad_out = contract_rows(attended, first_low)
    grad_attended = (
        contract_cols(first_low, w_out)
        .astype(jnp.bfloat16)
        .reshape(row_count, row_length, local_heads, head_dim)
    )
    grad_projected = lax.map(
        attend_backward, (queries_all, keys_all, values_all, segments, grad_attended, log_totals)
    )
    grad_projected = grad_projected.reshape(token_count, local_heads * 3 * head_dim)
    grad_joined = contract_rows(layer_input, grad_projected).reshape(
        feature_count, local_heads, 3 * head_dim
    )
    bias_sums = jnp.sum(grad_projected.astype(jnp.float32), axis=0).reshape(
        local_heads, 3 * head_dim
    )
    grad_qv_bias = jnp.concatenate([bias_sums[:, :head_dim], bias_sums[:, 2 * head_dim :]], axis=1)
    input_part = contract_cols(grad_projected, joined_weight)
    input_grad = (
        lax.psum_scatter(
            input_part.astype(jnp.bfloat16), "tensor", scatter_dimension=0, tiled=True
        ).astype(jnp.float32)
        + grad_first
    )
    grad_joined, grad_qv_bias, grad_out, grad_up, grad_up_bias, grad_down = lax.psum(
        (grad_joined, grad_qv_bias, grad_out, grad_up, grad_up_bias, grad_down), "dp"
    )
    norm_sums = lax.psum(
        (
            grad_gain_first,
            grad_shift_first,
            grad_out_bias,
            grad_gain_second,
            grad_shift_second,
            grad_down_bias,
        ),
        ("dp", "tensor"),
    )
    return (
        output,
        input_grad,
        grad_joined,
        grad_qv_bias,
        grad_out,
        norm_sums[2],
        norm_sums[0],
        norm_sums[1],
        grad_up,
        grad_up_bias,
        grad_down,
        norm_sums[5],
        norm_sums[3],
        norm_sums[4],
    )


def solution(mesh):
    return jax.shard_map(
        on_device,
        mesh=mesh,
        in_specs=(
            P("dp", None),
            P("dp"),
            P(None, "tensor", None),
            P("tensor", None),
            P("tensor", None),
            P(),
            P(),
            P(),
            P(None, "tensor"),
            P("tensor"),
            P("tensor", None),
            P(),
            P(),
            P(),
            P(("dp", "tensor"), None),
        ),
        out_specs=(
            P(("dp", "tensor"), None),
            P(("dp", "tensor"), None),
            P(None, "tensor", None),
            P("tensor", None),
            P("tensor", None),
            P(),
            P(),
            P(),
            P(None, "tensor"),
            P("tensor"),
            P("tensor", None),
            P(),
            P(),
            P(),
        ),
        check_vma=False,
    )
```

profile of v0, /device:TPU:0, one launch (start us, length us, event | category | flops | bytes accessed | tf_op | source)
XLA Modules:
  0.0 894.1 jit_solution(5119119623418682610)
XLA Ops:
  8.9 5.5 add_convert_fusion.1
  14.5 5.6 reshape.268
  20.0 1.9 fusion.123
  22.2 1.1 copy.52
  24.3 50.1 %while.22 = (s32[]{:T(128)}, bf16[2,1024,3,64]{1,3,2,0:T(8,128)(2,1)}, f32[2,3,1024]{2,1,0:T(4,128)}, bf16[2,1024,3,64]{1,3,2,0:T(8,128)(2,1)}, s32[2,1024]{1,0:...) while((s32[]{:T(128)}, ...), condition=%wide.region_3.4_spmd, body=%wide.region_0.3_spmd.sunk | while | flops 844100608 | bytes 50530516 | solution.py:138
  25.0 6.9 fusion.168
  31.9 7.4 fusion.169
  39.3 8.5 fusion.170
  50.0 6.9 fusion.168
  56.9 7.4 fusion.169
  64.3 8.5 fusion.170
  74.4 1.9 copy.44
  77.5 2.7 convolution_convert_fusion.3
  80.4 123.8 %all-reduce.7.cloned.1.call-done = bf16[2048,768]{1,0:T(8,128)(2,1)} async-done(((bf16[2048,768]{1,0:T(8,128)(2,1)}), bf16[2048,768]{1,0:T(8,128)(2,1)}) %all-reduce.7.cloned.1.call-update) | async-done | bytes 3145744 | tf_op jit(solution)/shard_map/psum | solution.py:141
  204.2 3.9 fusion.122
  209.0 1.1 multiply_add_fusion
  210.8 17.3 %multiply_convert_fusion.1 = (bf16[2048,768]{1,0:T(8,128)(2,1)S(1)}, f32[2048,768]{1,0:T(8,128)}, f32[2048,768]{1,0:T(8,128)}) fusion(f32[768]{0:T(1024)S(1)} %convert_element_type.126, bf16[768,768]{1,0:T(8,128)(2,1)S(1)} %copy-done, f32[2048,768]{1,0:T(8,128)S(1)} %multiply_add_fusion), kind=kOutput, calls=%fused_computation.83 | convolution fusion | flops 2521300992 | bytes 23202816 | tf_op jit(solution)/shard_map/dot_general | solution.py:147
  228.1 1.6 copy-done.44
  229.7 4.0 convolution_convert_fusion.1
  235.2 118.8 %all-reduce.9.cloned.1.call-done = bf16[2048,768]{1,0:T(8,128)(2,1)} async-done(((bf16[2048,768]{1,0:T(8,128)(2,1)}), bf16[2048,768]{1,0:T(8,128)(2,1)}) %all-reduce.9.cloned.1.call-update) | async-done | bytes 3145744 | tf_op jit(solution)/shard_map/psum | solution.py:152
  354.0 1.9 fusion.120
  356.3 1.3 multiply_reduce_fusion.2
  357.6 2.9 fusion.119
  362.0 62.2 %all-gather.3.cloned.1.call-done = bf16[2048,768]{1,0:T(8,128)(2,1)} async-done(((bf16[512,768]{1,0:T(8,128)(2,1)}), bf16[2048,768]{1,0:T(8,128)(2,1)}) %all-gather.3.cloned.1.call-update) | async-done | bytes 3145744 | tf_op jit(solution)/shard_map/all_gather | solution.py:161
  424.2 11.0 %convert_reduce_fusion = (f32[768]{0:T(1024)}, bf16[2048,768]{1,0:T(8,128)(2,1)S(1)}) fusion(f32[2048,768]{1,0:T(8,128)} %get-tuple-element.171, f32[2048,768]{1,0:T(8,128)} %get-tuple-element.186, f32[768]{0:T(1024)} %copy-done.34, bf16[2048,768]{1,0:T(8,128)(2,1)} %all-gather.3.cloned.1.call-done, bf16[768,768]{1,0:T(8,128)(2,1)} %param.29), kind=kOutput, calls=%fused_computation.81 | convolution fusion | flops 2442657024 | bytes 20060160 | tf_op jit(solution)/shard_map/dot_general | solution.py:31
  435.2 1.6 copy-done.11
  436.9 4.1 convolution_convert_fusion
  441.0 1.6 dynamic-slice_reduce_fusion
  442.6 1.7 multiply_reduce_fusion.5
  444.3 55.7 %reduce-scatter.3.cloned.1.call-done = bf16[512,768]{1,0:T(8,128)(2,1)} async-done(((bf16[2048,768]{1,0:T(8,128)(2,1)}), bf16[512,768]{1,0:T(8,128)(2,1)}) %reduce-scatter.3.cloned.1.call-update) | async-done | bytes 786448 | tf_op jit(solution)/shard_map/reduce_scatter | solution.py:170
  500.0 3.1 multiply_reduce_fusion.3
  503.1 2.4 fusion.118
  505.6 1.1 copy-done.5
  506.7 1.7 add_reduce_fusion
  508.5 63.6 %all-gather.5.cloned.1.call-done = bf16[2048,768]{1,0:T(8,128)(2,1)} async-done(((bf16[512,768]{1,0:T(8,128)(2,1)}), bf16[2048,768]{1,0:T(8,128)(2,1)}) %all-gather.5.cloned.1.call-update) | async-done | bytes 3145744 | tf_op jit(solution)/shard_map/all_gather | solution.py:178
  572.1 3.1 convolution_convert_fusion.4
  576.8 114.7 %while.23 = (s32[]{:T(128)}, bf16[2,1024,3,192]{1,3,2,0:T(8,128)(2,1)}, bf16[2,1024,3,64]{1,3,2,0:T(8,128)(2,1)S(1)}, s32[2,1024]{1,0:T(2,128)S(1)}, bf16[2,1024...) while((s32[]{:T(128)}, ...), condition=%wide.region_19.20_spmd, body=%wide.region_17.19_spmd.sunk | while | flops 2100240384 | bytes 201443472 | solution.py:185
  577.7 2.8 fusion.181
  580.5 5.1 fusion.182
  585.6 7.5 fusion.183
  593.1 19.8 %fusion.185 = bf16[1,1024,3,64]{1,3,2,0:T(8,128)(2,1)S(1)} fusion(f32[3,1024,1024]{1,2,0:T(8,128)} %fusion.183, f32[3,1024,1024]{1,2,0:T(8,128)} %copy-done.2, f32[3,1024]{1,0:T(4,128)S(1)} %dynamic-slice_bitcast_fusion.2, pred[1024,1024]{0,1:T(8,128)(4,1)S(1)} %broadcast_compare_fusion.5, bf16[2,1024,3,64]{1,3,2,0:T(8,128)(2,1)S(1)} %get-tuple-element.327, ...), kind=kOutput, calls=%fused_computation.46.clone.1 | convolution fusion | flops 437456896 | bytes 53248004 | tf_op jit(solution)/shard_map/while/body/eval_jaxpr/hqk,khd->qhd/dot_general | solution.py:103
  613.0 20.1 %fusion.184 = bf16[1,1024,3,64]{1,3,2,0:T(8,128)(2,1)S(1)} fusion(f32[3,1024,1024]{1,2,0:T(8,128)} %fusion.183, f32[3,1024,1024]{1,2,0:T(8,128)} %copy-done.2, f32[3,1024]{1,0:T(4,128)S(1)} %dynamic-slice_bitcast_fusion.2, pred[1024,1024]{0,1:T(8,128)(4,1)S(1)} %broadcast_compare_fusion.5, bf16[2,1024,3,64]{1,3,2,0:T(8,128)(2,1)} %get-tuple-element.329, ...), kind=kOutput, calls=%fused_computation.45.clone.1 | convolution fusion | flops 437456896 | bytes 53248004 | tf_op jit(solution)/shard_map/while/body/eval_jaxpr/hqk,qhd->khd/dot_general | solution.py:106
  633.1 1.1 maximum_dynamic-update-slice_fusion.2
  634.9 2.8 fusion.181
  637.7 5.1 fusion.182
  642.8 7.5 fusion.183
  650.3 19.8 %fusion.185 = bf16[1,1024,3,64]{1,3,2,0:T(8,128)(2,1)S(1)} fusion(f32[3,1024,1024]{1,2,0:T(8,128)} %fusion.183, f32[3,1024,1024]{1,2,0:T(8,128)} %copy-done.2, f32[3,1024]{1,0:T(4,128)S(1)} %dynamic-slice_bitcast_fusion.2, pred[1024,1024]{0,1:T(8,128)(4,1)S(1)} %broadcast_compare_fusion.5, bf16[2,1024,3,64]{1,3,2,0:T(8,128)(2,1)S(1)} %get-tuple-element.327, ...), kind=kOutput, calls=%fused_computation.46.clone.1 | convolution fusion | flops 437456896 | bytes 53248004 | tf_op jit(solution)/shard_map/while/body/eval_jaxpr/hqk,khd->qhd/dot_general | solution.py:103
  670.2 20.1 %fusion.184 = bf16[1,1024,3,64]{1,3,2,0:T(8,128)(2,1)S(1)} fusion(f32[3,1024,1024]{1,2,0:T(8,128)} %fusion.183, f32[3,1024,1024]{1,2,0:T(8,128)} %copy-done.2, f32[3,1024]{1,0:T(4,128)S(1)} %dynamic-slice_bitcast_fusion.2, pred[1024,1024]{0,1:T(8,128)(4,1)S(1)} %broadcast_compare_fusion.5, bf16[2,1024,3,64]{1,3,2,0:T(8,128)(2,1)} %get-tuple-element.329, ...), kind=kOutput, calls=%fused_computation.45.clone.1 | convolution fusion | flops 437456896 | bytes 53248004 | tf_op jit(solution)/shard_map/while/body/eval_jaxpr/hqk,qhd->khd/dot_general | solution.py:106
  690.3 1.1 maximum_dynamic-update-slice_fusion.2
  691.6 4.2 copy.46
  696.5 4.0 convolution_convert_fusion.2
  700.6 7.1 fusion.127
  707.7 7.1 fusion.109
  714.8 1.6 fusion.126
  716.4 3.2 fusion.125
  720.4 45.0 %all-reduce = (f32[768]{0:T(1024)}, f32[768]{0:T(1024)}, f32[768]{0:T(1024)}, f32[768]{0:T(1024)}, f32[768]{0:T(1024)}, /*index=5*/f32[768]{0:T(1024)}) all-reduce(f32[768]{0:T(1024)S(1)} %copy-done.28, f32[768]{0:T(1024)S(1)} %copy-done.30, f32[768]{0:T(1024)S(1)} %copy-done.31, ...), channel_id=1, replica_groups=mesh['dp'=8,'tensor'=4] {'dp','tensor'}, use_global_device_ids=true, to_apply=%region_26.27 | all-reduce | flops 4608 | bytes 36864 | tf_op jit(solution)/shard_map/psum | solution.py:206
  765.4 2.1 convert_reduce_fusion.1
  767.5 14.5 %all-reduce.1 = (f32[3,128]{1,0:T(4,128)}, f32[768]{0:T(1024)}) all-reduce(f32[3,128]{1,0:T(4,128)S(1)} %pad_maximum_fusion.1, f32[768]{0:T(1024)S(1)} %copy-done.33), channel_id=1, replica_groups=mesh['dp'=8,'tensor'=4] {'dp'}, use_global_device_ids=true, to_apply=%region_23.24 | all-reduce | flops 1152 | bytes 9216 | tf_op jit(solution)/shard_map/psum | solution.py:203
  782.0 2.5 convert_add_fusion
  784.5 94.6 %all-reduce.11.cloned.1.call-done = (f32[768,3,192]{0,2,1:T(8,128)}, f32[192,768]{1,0:T(8,128)}, f32[768,768]{1,0:T(8,128)}, f32[768,768]{1,0:T(8,128)}) async-done(((f32[768,3,192]{0,2,1:T(8,128)}, f32[192,768]{1,0:T(8,128)}, f32[768,768]{1,0:T(8,128)}, f32[768,768]{1,0:T(8,128)}), (f32[768,3,192]{0,2,1:T(8,128)}, f32[192,768]{1,0:T(8,128)}, f32[768,768]{1,0:T(8,128)}, ...) | async-done | bytes 7077904 | tf_op jit(solution)/shard_map/psum | solution.py:203
  879.2 2.9 copy.82
  882.1 1.9 copy.83
  884.0 1.4 copy.84
  885.4 1.4 copy.85
  (161 shorter events, 18.0 us)
Async XLA Ops:
  7.2 203.6 %copy-start = (bf16[768,768]{1,0:T(8,128)(2,1)S(1)}, bf16[768,768]{1,0:T(8,128)(2,1)}, u32[]{:S(2)}) copy-start(bf16[768,768]{1,0:T(8,128)(2,1)} %param.27) | copy-start | bytes 3538948
  7.2 197.0 %all-reduce.7.cloned.1.call-start = ((), (), s32[]{:S(2)}) async-start(), calls=%async_computation.2 | async-start | bytes 6291456 | tf_op jit(solution)/shard_map/psum | solution.py:141
  24.3 53.2 %copy-start.18 = (bf16[192,768]{1,0:T(8,128)(2,1)S(1)}, bf16[192,768]{1,0:T(8,128)(2,1)}, u32[]{:S(2)}) copy-start(bf16[192,768]{1,0:T(8,128)(2,1)} %param.23) | copy-start | bytes 884740
  31.9 7.4 copy-start.16
  39.3 8.5 copy-start.20
  47.8 0.9 copy-start.17
  48.7 0.6 copy-start.21
  56.9 7.4 copy-start.16
  64.2 8.5 copy-start.20
  72.7 0.9 copy-start.17
  73.6 0.6 copy-start.21
  76.4 4.0 copy-start.35
  76.4 4.0 copy-start.36
  76.4 4.0 copy-start.37
  76.4 4.0 copy-start.38
  76.6 0.9 copy-start.7
  80.3 273.7 %all-reduce.9.cloned.1.call-start = ((), (), s32[]{:S(2)}) async-start(), calls=%async_computation.3 | async-start | bytes 6291456 | tf_op jit(solution)/shard_map/psum | solution.py:152
  80.4 129.8 %copy-start.34 = (f32[768]{0:T(1024)}, f32[768]{0:T(1024)S(1)}, u32[]{:S(2)}) copy-start(f32[768]{0:T(1024)S(1)} %convert_element_type.126) | copy-start | bytes 9220
  208.2 2.7 copy-start.3
  210.8 17.3 %copy-start.4 = (f32[2048,768]{1,0:T(8,128)}, f32[2048,768]{1,0:T(8,128)S(1)}, u32[]{:S(2)}) copy-start(f32[2048,768]{1,0:T(8,128)S(1)} %multiply_add_fusion) | copy-start | bytes 18874372
  210.8 18.9 %copy-start.42 = (bf16[768,768]{1,0:T(8,128)(2,1)S(1)}, bf16[768,768]{1,0:T(8,128)(2,1)}, u32[]{:S(2)}) copy-start(bf16[768,768]{1,0:T(8,128)(2,1)} %param.29) | copy-start | bytes 3538948
  228.1 1.6 copy-start.44
  229.7 4.1 copy-start.39
  229.7 4.1 copy-start.40
  229.7 4.1 copy-start.41
  233.7 122.5 %copy-start.13 = (bf16[512,768]{1,0:T(8,128)(2,1)S(1)}, bf16[512,768]{1,0:T(8,128)(2,1)}, u32[]{:S(2)}) copy-start(bf16[512,768]{1,0:T(8,128)(2,1)} %param.33) | copy-start | bytes 2359300
  233.7 190.5 %all-gather.3.cloned.1.call-start = ((), (), s32[]{:S(2)}) async-start(), calls=%async_computation.4 | async-start | bytes 3932160 | tf_op jit(solution)/shard_map/all_gather | solution.py:161
  235.2 122.4 %copy-start.25 = (f32[512]{0:T(512)}, f32[512]{0:T(512)S(1)}, u32[]{:S(2)}) copy-start(f32[512]{0:T(512)S(1)} %fusion.114) | copy-start | bytes 6148
  354.0 3.6 copy-start.29
  361.6 138.5 %reduce-scatter.3.cloned.1.call-start = ((), (), s32[]{:S(2)}) async-start(), calls=%async_computation.5 | async-start | bytes 3932160 | tf_op jit(solution)/shard_map/reduce_scatter | solution.py:170
  435.2 1.6 copy-start.11
  441.0 131.1 %all-gather.5.cloned.1.call-start = ((), (), s32[]{:S(2)}) async-start(), calls=%async_computation.6 | async-start | bytes 3932160 | tf_op jit(solution)/shard_map/all_gather | solution.py:178
  444.3 127.8 %copy-start.19 = (bf16[192,768]{1,0:T(8,128)(2,1)S(1)}, bf16[192,768]{1,0:T(8,128)(2,1)}, u32[]{:S(2)}) copy-start(bf16[192,768]{1,0:T(8,128)(2,1)} %param.23) | copy-start | bytes 884740
  505.6 1.1 copy-start.5
  505.6 71.2 %copy-start.23 = (f32[512]{0:T(512)}, f32[512]{0:T(512)S(1)}, u32[]{:S(2)}) copy-start(f32[512]{0:T(512)S(1)} %negate_multiply_fusion.1) | copy-start | bytes 6148
  506.7 70.1 %copy-start.22 = (f32[2,3,1024]{2,1,0:T(4,128)S(1)}, f32[2,3,1024]{2,1,0:T(4,128)}, u32[]{:S(2)}) copy-start(f32[2,3,1024]{2,1,0:T(4,128)} %get-tuple-element.312) | copy-start | bytes 73732
  508.4 273.6 %reduce-scatter.5.cloned.1.call-start = ((), (), s32[]{:S(2)}) async-start(), calls=%async_computation.7 | async-start | bytes 3932160 | tf_op jit(solution)/shard_map/reduce_scatter | solution.py:198
  580.5 5.1 copy-start.2
  637.7 5.1 copy-start.2
  691.6 4.9 copy-start.43
  700.5 178.6 %all-reduce.11.cloned.1.call-start = ((), (), s32[]{:S(2)}) async-start(), calls=%async_computation.8 | async-start | bytes 14155776 | tf_op jit(solution)/shard_map/psum | solution.py:203
  700.6 7.1 copy-start.12
  707.7 7.1 copy-start.8
  707.7 7.1 copy-start.9
  707.7 8.7 copy-start.10
  719.6 0.7 copy-start.26
  719.6 0.7 copy-start.27
  719.6 0.7 copy-start.28
  719.6 0.7 copy-start.30
  719.6 0.7 copy-start.31
  719.6 0.7 copy-start.32
  719.7 47.9 %copy-start.33 = (f32[768]{0:T(1024)S(1)}, f32[768]{0:T(1024)}, u32[]{:S(2)}) copy-start(f32[768]{0:T(1024)} %get-tuple-element.162) | copy-start | bytes 9220
  719.7 62.3 %copy-start.6 = (f32[512,768]{1,0:T(8,128)S(1)}, f32[512,768]{1,0:T(8,128)}, u32[]{:S(2)}) copy-start(f32[512,768]{1,0:T(8,128)} %copy-done.5) | copy-start | bytes 4718596
  719.7 62.3 %copy-start.24 = (f32[512]{0:T(512)S(1)}, f32[512]{0:T(512)}, u32[]{:S(2)}) copy-start(f32[512]{0:T(512)} %copy-done.23) | copy-start | bytes 6148
  879.2 4.9 copy-start.15
  879.2 6.3 copy-start.14
  879.2 7.7 copy-start.1
Sparse Core Ops, SparseCore 0:
  80.4 123.7 all-reduce.6
  233.9 120.0 all-reduce.8
  361.7 62.4 all-gather.2
  441.1 58.8 reduce-scatter.2
  508.5 63.5 all-gather.4
  700.7 59.9 reduce-scatter.4
  765.5 113.6 all-reduce.10
where the time goes:
time: 904 us; the launch traced here: 894 us
  waiting for transfers between devices  519 us (57%)
  matrix products  212 us (23%)
  blocking collectives  59.5 us (7%)
  other arithmetic  50.4 us (6%)
  local copies, waits for them, and re-layouts  36.7 us (4%)
  between operations  15 us (2%)
    psum x1, waiting for transfers between devices, on_device(): lax.psum(attn_part.astype(jnp.bfloat16), 'tensor').astype(jnp.float32)  124 us
    psum x1, waiting for transfers between devices, on_device(): lax.psum(ffn_part.astype(jnp.bfloat16), 'tensor').astype(jnp.float32)  119 us
    psum x1, waiting for transfers between devices, on_device(): lax.psum((grad_joined, grad_qv_bias, grad_out, grad_up, grad_up_bias, gra...  94.6 us
    all_gather x1, waiting for transfers between devices, on_device(): lax.all_gather(grad_first.astype(jnp.bfloat16), 'tensor', axis=0, tiled=T...  63.6 us
    all_gather x1, waiting for transfers between devices, on_device(): lax.all_gather(grad_second.astype(jnp.bfloat16), 'tensor', axis=0, tiled=...  62.2 us
    reduce_scatter x1, waiting for transfers between devices, on_device(): lax.psum_scatter(hidden_part.astype(jnp.bfloat16), 'tensor', scatter_dime...  55.7 us
    psum x1, blocking collectives, on_device(): lax.psum((grad_gain_first, grad_shift_first, grad_out_bias, grad_gain_sec...  45 us
    dot_general x2, matrix products, attend_backward(): jnp.einsum('hqk,qhd->khd', grad_raw, queries, preferred_element_type=jnp....  40.2 us
  transfers between devices with their start and end apart: 7, of which 6 were waited for; matrix products, arithmetic and copies ran while one was open for 3% of the time, Pallas kernels for 0%

commit v1 on v0

v1 whole, which is shorter than its diff:
```python
import jax
import jax.numpy as jnp
from jax import lax
from jax.sharding import PartitionSpec as P

SEQ = 1024


EPSILON = 1e-06
MASKED = -1e30
LOW = jnp.bfloat16
HIGH = jnp.float32


def dot_nn(left, right):
    return lax.dot_general(left, right, (((1,), (0,)), ((), ())), preferred_element_type=HIGH)


def dot_nt(left, right):
    return lax.dot_general(left, right, (((1,), (1,)), ((), ())), preferred_element_type=HIGH)


def dot_tn(left, right):
    return lax.dot_general(left, right, (((0,), (0,)), ((), ())), preferred_element_type=HIGH)


def norm_forward(summed):
    mean = jnp.mean(summed, axis=-1, keepdims=True)
    centred = summed - mean
    spread = jnp.mean(centred * centred, axis=-1, keepdims=True)
    inverse = lax.rsqrt(spread + EPSILON)
    return centred * inverse, inverse


def norm_backward(xhat, inverse, scaled):
    return inverse * (
        scaled
        - jnp.mean(scaled, axis=-1, keepdims=True)
        - xhat * jnp.mean(scaled * xhat, axis=-1, keepdims=True)
    )


def gelu_parts(u):
    phi_cdf = 0.5 * (1.0 + lax.erf(u * (2.0**-0.5)))
    density = jnp.exp(-0.5 * u * u) * 0.3989422804014327
    return u * phi_cdf, phi_cdf + u * density


def column_sum(values):
    return jnp.sum(values, axis=0, keepdims=True)


def on_device(
    layer_input,
    segment_ids,
    w_qkv,
    qv_bias,
    w_out,
    out_bias,
    norm1_gain,
    norm1_bias,
    w_up,
    up_bias,
    w_down,
    down_bias,
    norm2_gain,
    norm2_bias,
    out_cotangent,
):
    n_tensor = lax.axis_size("tensor")
    place = lax.axis_index("tensor")
    n_dp = lax.axis_size("dp")
    dp_place = lax.axis_index("dp")
    tokens, width = layer_input.shape
    share = tokens // n_tensor
    local_heads = qv_bias.shape[0]
    heads = local_heads * n_tensor
    head_dim = qv_bias.shape[1] // 2
    score_scale = float(head_dim) ** (-0.5)
    shares_per_row = SEQ // share
    row_start = (place // shares_per_row) * SEQ
    own_start = place * share
    in_row = (place % shares_per_row) * share

    units = w_up.shape[1]
    qkv_rows = w_qkv.reshape(width, local_heads, 3, head_dim).transpose(2, 1, 3, 0).reshape(-1, width)
    local = jnp.concatenate([qkv_rows, w_out, w_up.T, w_down], axis=0)
    slab = local.shape[0] // n_dp
    mine = lax.dynamic_slice_in_dim(local, dp_place * slab, slab, 0)
    everything = lax.all_gather(mine, ("tensor", "dp"), axis=0, tiled=True)
    everything = everything.reshape(n_tensor, local.shape[0], width)
    local_width = local_heads * head_dim
    q_rows = everything[:, :local_width].reshape(-1, width)
    k_rows = everything[:, local_width : 2 * local_width].reshape(-1, width)
    v_rows = everything[:, 2 * local_width : 3 * local_width].reshape(-1, width)
    at = 3 * local_width
    out_rows = everything[:, at : at + local_width].reshape(-1, width)
    at += local_width
    up_rows = everything[:, at : at + units].reshape(-1, width)
    at += units
    down_rows = everything[:, at : at + units].reshape(-1, width)
    small = jnp.concatenate([qv_bias.reshape(-1), up_bias])
    small = lax.all_gather(small, "tensor", axis=0, tiled=False)
    qv_full = small[:, : local_heads * 2 * head_dim].reshape(heads, 2 * head_dim).astype(HIGH)
    up_bias_full = small[:, local_heads * 2 * head_dim :].reshape(-1).astype(HIGH)
    q_bias = qv_full[:, :head_dim].reshape(-1)
    v_bias = qv_full[:, head_dim:].reshape(-1)

    row_input = lax.dynamic_slice_in_dim(layer_input, row_start, SEQ, 0)
    own_input = lax.dynamic_slice_in_dim(layer_input, own_start, share, 0)
    row_segments = lax.dynamic_slice_in_dim(segment_ids, row_start, SEQ, 0)
    own_segments = lax.dynamic_slice_in_dim(segment_ids, own_start, share, 0)

    queries = (dot_nt(own_input, q_rows) + q_bias).astype(LOW).reshape(share, heads, head_dim)
    keys = dot_nt(row_input, k_rows).astype(LOW).reshape(SEQ, heads, head_dim)
    values = (dot_nt(row_input, v_rows) + v_bias).astype(LOW).reshape(SEQ, heads, head_dim)
    allowed = own_segments[:, None] == row_segments[None, :]
    scores = jnp.einsum("qhd,khd->hqk", queries, keys, preferred_element_type=HIGH) * score_scale
    scores = jnp.where(allowed[None], scores, MASKED)
    top = jnp.max(scores, axis=-1, keepdims=True)
    total = jnp.sum(jnp.exp(scores - top), axis=-1, keepdims=True)
    probability = jnp.exp(scores - (top + jnp.log(total)))
    probability_low = probability.astype(LOW)
    attended = jnp.einsum("hqk,khd->qhd", probability_low, values, preferred_element_type=HIGH)
    attended = attended.astype(LOW).reshape(share, -1)

    first_sum = own_input.astype(HIGH) + dot_nn(attended, out_rows) + out_bias.astype(HIGH)
    gain_first = norm1_gain.astype(HIGH)
    gain_second = norm2_gain.astype(HIGH)
    xhat_first, inverse_first = norm_forward(first_sum)
    hidden = xhat_first * gain_first + norm1_bias.astype(HIGH)
    hidden_low = hidden.astype(LOW)
    up_pre = dot_nt(hidden_low, up_rows) + up_bias_full
    gelu_value, gelu_slope = gelu_parts(up_pre)
    activation = gelu_value.astype(LOW)
    second_sum = hidden + dot_nn(activation, down_rows) + down_bias.astype(HIGH)
    xhat_second, inverse_second = norm_forward(second_sum)
    output = (xhat_second * gain_second + norm2_bias.astype(HIGH)).astype(LOW)

    live = (own_segments >= 0).astype(HIGH)
    cotangent = out_cotangent.astype(HIGH) * live[:, None]
    grad_second = norm_backward(xhat_second, inverse_second, cotangent * gain_second)
    second_low = grad_second.astype(LOW)
    grad_down = dot_tn(activation, second_low)
    grad_up_pre = (dot_nt(second_low, down_rows) * gelu_slope).astype(LOW)
    grad_up = dot_tn(grad_up_pre, hidden_low)
    grad_hidden = grad_second + dot_nn(grad_up_pre, up_rows)
    grad_first = norm_backward(xhat_first, inverse_first, grad_hidden * gain_first)
    first_low = grad_first.astype(LOW)
    grad_out = dot_tn(attended, first_low)
    grad_attended = dot_nt(first_low, out_rows).astype(LOW).reshape(share, heads, head_dim)

    grad_values = jnp.einsum(
        "hqk,qhd->khd", probability_low, grad_attended, preferred_element_type=HIGH
    )
    grad_probs = jnp.einsum("qhd,khd->hqk", grad_attended, values, preferred_element_type=HIGH)
    inner = jnp.sum(probability * grad_probs, axis=-1, keepdims=True)
    grad_raw = (probability * (grad_probs - inner) * score_scale).astype(LOW)
    grad_queries = jnp.einsum("hqk,khd->qhd", grad_raw, keys, preferred_element_type=HIGH)
    grad_keys = jnp.einsum("hqk,qhd->khd", grad_raw, queries, preferred_element_type=HIGH)
    grad_queries = grad_queries.astype(LOW).reshape(share, -1)
    grad_keys = grad_keys.astype(LOW).reshape(SEQ, -1)
    grad_values = grad_values.astype(LOW).reshape(SEQ, -1)
    grad_q_rows = dot_tn(grad_queries, own_input)
    grad_k_rows = dot_tn(grad_keys, row_input)
    grad_v_rows = dot_tn(grad_values, row_input)

    row_term = dot_nn(grad_keys, k_rows) + dot_nn(grad_values, v_rows)
    row_term = row_term.reshape(shares_per_row, share, width)
    my_half = place % shares_per_row
    input_grad = grad_first + dot_nn(grad_queries, q_rows) + row_term[my_half]
    for step in range(1, shares_per_row):
        pairs = [
            (p, (p // shares_per_row) * shares_per_row + (p + step) % shares_per_row)
            for p in range(n_tensor)
        ]
        sent = row_term[(my_half + step) % shares_per_row].astype(LOW)
        input_grad = input_grad + lax.ppermute(sent, "tensor", pairs).astype(HIGH)

    def by_shard(rows):
        return rows.astype(LOW).reshape(n_tensor, -1, width)

    gradients = jnp.concatenate(
        [
            by_shard(grad_q_rows),
            by_shard(grad_k_rows),
            by_shard(grad_v_rows),
            by_shard(grad_out),
            by_shard(grad_up),
            by_shard(grad_down),
        ],
        axis=1,
    )
    rows_all = gradients.shape[1]
    slab = rows_all // n_dp
    gradients = gradients.reshape(n_tensor, n_dp, slab, width).transpose(1, 0, 2, 3)
    part = lax.psum_scatter(gradients.reshape(-1, width), "dp", scatter_dimension=0, tiled=True)
    part = lax.psum_scatter(part, "tensor", scatter_dimension=0, tiled=True)
    summed = lax.all_gather(part, "dp", axis=0, tiled=True).astype(HIGH)
    at = 3 * local_width
    grad_qkv = (
        summed[:at].reshape(3, local_heads, head_dim, width).transpose(3, 1, 0, 2)
    ).reshape(width, local_heads, 3 * head_dim)
    grad_out = summed[at : at + local_width]
    at += local_width
    grad_up = summed[at : at + units].T
    at += units
    grad_down = summed[at : at + units]

    vectors = lax.psum(
        (
            jnp.sum(grad_queries.astype(HIGH), axis=0).reshape(heads, head_dim),
            jnp.sum(grad_values.astype(HIGH), axis=0).reshape(heads, head_dim),
            jnp.sum(grad_up_pre.astype(HIGH), axis=0),
            jnp.sum(grad_first, axis=0),
            jnp.sum(grad_hidden * xhat_first, axis=0),
            jnp.sum(grad_hidden, axis=0),
            jnp.sum(grad_second, axis=0),
            jnp.sum(cotangent * xhat_second, axis=0),
            jnp.sum(cotangent, axis=0),
        ),
        ("dp", "tensor"),
    )
    grad_qv = jnp.concatenate([vectors[0], vectors[1]], axis=1)
    grad_qv_bias = lax.dynamic_slice_in_dim(grad_qv, place * local_heads, local_heads, 0)
    grad_up_bias = lax.dynamic_slice_in_dim(vectors[2], place * units, units, 0)
    return (
        output,
        input_grad,
        grad_qkv,
        grad_qv_bias,
        grad_out,
        vectors[3],
        vectors[4],
        vectors[5],
        grad_up,
        grad_up_bias,
        grad_down,
        vectors[6],
        vectors[7],
        vectors[8],
    )


def solution(mesh):
    return jax.shard_map(
        on_device,
        mesh=mesh,
        in_specs=(
            P("dp", None),
            P("dp"),
            P(None, "tensor", None),
            P("tensor", None),
            P("tensor", None),
            P(),
            P(),
            P(),
            P(None, "tensor"),
            P("tensor"),
            P("tensor", None),
            P(),
            P(),
            P(),
            P(("dp", "tensor"), None),
        ),
        out_specs=(
            P(("dp", "tensor"), None),
            P(("dp", "tensor"), None),
            P(None, "tensor", None),
            P("tensor", None),
            P("tensor", None),
            P(),
            P(),
            P(),
            P(None, "tensor"),
            P("tensor"),
            P("tensor", None),
            P(),
            P(),
            P(),
        ),
        check_vma=False,
    )
```

time: 904 us -> 559 us (0.62)
  waiting for transfers between devices: 519 us -> 226 us
  other arithmetic: 50.4 us -> 24.1 us
  matrix products: 212 us -> 187 us
    psum x3 -> x0, waiting for transfers between devices: 337 us -> none  [the longest x1 124 us: on_device(): lax.psum(attn_part.astype(jnp.bfloat16), 'tensor').astype(jnp.float32)]
    reduce_scatter x2, waiting for transfers between devices: 55.7 us -> 139 us  [the longest x1 99 us: on_device(): lax.psum_scatter(gradients.reshape(-1, width), 'dp', scatter_dimension=0,...]
    all_gather x2, waiting for transfers between devices: 126 us -> 86.1 us  [the longest x1 86.1 us: on_device(): everything = lax.all_gather(mine, ('tensor', 'dp'), axis=0, tiled=True)]
    dot_general x26 -> x24, matrix products: 212 us -> 187 us  [the longest x1 46.5 us: on_device(): jnp.einsum('hqk,qhd->khd', grad_raw, queries, preferred_element_type=HIGH)]
    reduce_sum x14 -> x6, other arithmetic: 38.5 us -> 15.7 us  [the longest x1 12.1 us: on_device(): total = jnp.sum(jnp.exp(scores - top), axis=-1, keepdims=True)]
    psum x2 -> x1, blocking collectives: 59.5 us -> 42 us  [on_device(): lax.psum((jnp.sum(grad_queries.astype(HIGH), axis=0).reshape(heads, head_...]
    all_gather x0 -> x1, blocking collectives: none -> 14.8 us  [on_device(): small = lax.all_gather(small, 'tensor', axis=0, tiled=False)]
    slice x2 -> x6, local copies, waits for them, and re-layouts: 1.9 us -> 16.1 us  [the longest x1 7.96 us: on_device(): down_rows = everything[:, at:at + units].reshape(-1, width)]
  transfers between devices with their start and end apart: 7 -> 5, of which waited for: 6 -> 3; matrix products, arithmetic and copies ran while one was open for 3% -> 3% of each run, Pallas kernels for 0% -> 0%
where the time goes in v1:
time: 559 us; the launch traced here: 549 us
  waiting for transfers between devices  226 us (40%)
  matrix products  187 us (33%)
  blocking collectives  56.9 us (10%)
  local copies, waits for them, and re-layouts  39.4 us (7%)
  other arithmetic  24.1 us (4%)
  between operations  14.9 us (3%)
    reduce_scatter x1, waiting for transfers between devices, on_device(): lax.psum_scatter(gradients.reshape(-1, width), 'dp', scatter_dimension=0,...  99 us
    all_gather x1, waiting for transfers between devices, on_device(): everything = lax.all_gather(mine, ('tensor', 'dp'), axis=0, tiled=True)  86.1 us
    dot_general x1, matrix products, on_device(): jnp.einsum('hqk,qhd->khd', grad_raw, queries, preferred_element_type=HIGH)  46.5 us
    dot_general x1, matrix products, on_device(): jnp.einsum('hqk,khd->qhd', grad_raw, keys, preferred_element_type=HIGH)  45.7 us
    psum x1, blocking collectives, on_device(): lax.psum((jnp.sum(grad_queries.astype(HIGH), axis=0).reshape(heads, head_...  42 us
    reduce_scatter x1, waiting for transfers between devices, on_device(): part = lax.psum_scatter(part, 'tensor', scatter_dimension=0, tiled=True)  40.4 us
    dot_general x6, matrix products, dot_nn(): lax.dot_general(left, right, (((1,), (0,)), ((), ())), preferred_element_...  17.1 us
    dot_general x6, matrix products, dot_nt(): lax.dot_general(left, right, (((1,), (1,)), ((), ())), preferred_element_...  17 us
  transfers between devices with their start and end apart: 5, of which 3 were waited for; matrix products, arithmetic and copies ran while one was open for 3% of the time, Pallas kernels for 0%

profile of v1, /device:TPU:0, one launch (start us, length us, event | category | flops | bytes accessed | tf_op | source)
XLA Modules:
  0.0 549.0 jit_solution(3154635445795153635)
XLA Ops:
  7.3 1.7 copy.46
  9.0 1.2 copy.45
  10.2 1.9 fusion.38
  12.2 0.7 pad_maximum_fusion
  12.9 14.8 %all-gather.1 = bf16[4,1,1152]{2,1,0:T(2,128)(2,1)S(1)} all-gather(bf16[1,1,1152]{2,1,0:T(2,128)(2,1)S(1)} %reshape.251), channel_id=2, replica_groups=mesh['dp'=8,'tensor'=4] {'tensor'}, dimensions={0}, use_global_device_ids=true | all-gather | bytes 11520 | tf_op jit(solution)/shard_map/all_gather | solution.py:103
  27.8 0.7 convert_element_type.153
  28.7 0.7 convert_element_type.155
  29.4 0.7 convert_element_type.154
  30.1 0.7 convert_element_type.161
  30.8 0.7 convert_element_type.162
  31.5 0.4 broadcast_compare_fusion
  31.9 86.1 %all-gather.5.cloned.1.call-done = bf16[9216,768]{1,0:T(8,128)(2,1)} async-done(((bf16[288,768]{1,0:T(8,128)(2,1)}), bf16[9216,768]{1,0:T(8,128)(2,1)}) %all-gather.5.cloned.1.call-update) | async-done | bytes 14155792 | tf_op jit(solution)/shard_map/all_gather | solution.py:90
  118.0 8.0 %fusion.71 = (bf16[4,768,768]{2,1,0:T(8,128)(2,1)}, bf16[4,768,768]{2,1,0:T(8,128)(2,1)}) fusion(bf16[4,2304,768]{2,1,0:T(8,128)(2,1)} %bitcast.91), kind=kLoop, calls=%fused_computation.124 | loop fusion | bytes 18874368 | tf_op jit(solution)/shard_map/slice | solution.py:101
  125.9 4.2 fusion.72
  130.1 1.1 copy-done.4
  131.2 1.9 add_convert_fusion.2
  133.4 3.4 convolution_convert_fusion.3
  136.9 10.5 %fusion.2 = (f32[12,512]{1,0:T(8,128)S(1)}, f32[12,512,1024]{2,1,0:T(8,128)}) fusion(pred[512,1024]{1,0:T(8,128)(4,1)S(1)} %broadcast_compare_fusion, bf16[512,12,64]{0,2,1:T(8,128)(2,1)S(1)} %bitcast.113, bf16[1024,12,64]{0,2,1:T(8,128)(2,1)S(1)} %bitcast.118), kind=kOutput, calls=%fused_computation.7 | convolution fusion | flops 824174592 | bytes 28073984 | tf_op jit(solution)/shard_map/qhd,khd->hqk/dot_general | solution.py:118
  147.5 12.1 %exponential_reduce_fusion = f32[12,512]{1,0:T(8,128)S(1)} fusion(f32[12,512,1024]{2,1,0:T(8,128)} %get-tuple-element.89, f32[12,512]{1,0:T(8,128)S(1)} %get-tuple-element.88, pred[512,1024]{1,0:T(8,128)(4,1)S(1)} %broadcast_compare_fusion), kind=kLoop, calls=%fused_computation.5 | loop fusion | flops 25159680 | bytes 25739264 | tf_op jit(solution)/shard_map/reduce_sum | solution.py:121
  159.6 1.4 add_convert_fusion
  161.1 11.9 %convolution_convert_fusion.9 = bf16[12,64,512]{2,1,0:T(8,128)(2,1)S(1)} fusion(bf16[1024,12,64]{0,2,1:T(8,128)(2,1)S(1)} %bitcast.96, f32[12,512]{1,0:T(8,128)S(1)} %log_add_fusion, f32[12,512,1024]{2,1,0:T(8,128)} %get-tuple-element.89, pred[512,1024]{1,0:T(8,128)(4,1)S(1)} %broadcast_compare_fusion), kind=kOutput, calls=%fused_computation.64 | convolution fusion | flops 830865408 | bytes 28073984 | tf_op jit(solution)/shard_map/hqk,khd->qhd/dot_general | solution.py:124
  173.1 2.3 fusion.74
  175.8 3.1 multiply_convert_fusion.1
  179.0 2.8 fusion.75
  182.2 0.9 multiply_reduce_fusion.1
  183.0 1.6 fusion.69
  184.7 5.3 convert_reduce_fusion
  190.0 3.6 multiply_reduce_fusion.2
  193.6 0.5 fusion.70
  194.1 0.7 copy-done.16
  194.9 1.7 convolution_convert_fusion.8
  196.6 1.4 copy.48
  198.0 11.5 %fusion.78 = f32[12,512,1024]{2,1,0:T(8,128)} fusion(bf16[512,12,64]{0,2,1:T(8,128)(2,1)S(1)} %bitcast.94, bf16[1024,12,64]{0,2,1:T(8,128)(2,1)} %bitcast.97), kind=kOutput, calls=%fused_computation.129 | convolution fusion | flops 805306368 | bytes 27525120 | tf_op jit(solution)/shard_map/qhd,khd->hqk/dot_general | solution.py:156
  209.5 13.4 %convert_reduce_fusion.1 = (f32[12,64]{1,0:T(8,128)}, bf16[12,64,1024]{2,1,0:T(8,128)(2,1)}) fusion(bf16[512,12,64]{0,2,1:T(8,128)(2,1)S(1)} %bitcast.95, f32[12,512]{1,0:T(8,128)S(1)} %log_add_fusion, f32[12,512,1024]{2,1,0:T(8,128)} %get-tuple-element.89, pred[512,1024]{1,0:T(8,128)(4,1)S(1)} %broadcast_compare_fusion), kind=kOutput, calls=%fused_computation.27 | convolution fusion | flops 832830720 | bytes 28077056 | tf_op jit(solution)/shard_map/hqk,qhd->khd/dot_general | solution.py:153
  222.9 46.5 %fusion.18 = bf16[12,64,1024]{2,1,0:T(8,128)(2,1)} fusion(bf16[512,12,64]{0,2,1:T(8,128)(2,1)} %bitcast.114, f32[12,512,1024]{2,1,0:T(8,128)} %fusion.78, f32[12,512]{1,0:T(8,128)S(1)} %log_add_fusion, f32[12,512,1024]{2,1,0:T(8,128)} %get-tuple-element.89, pred[512,1024]{1,0:T(8,128)(4,1)S(1)} %broadcast_compare_fusion), kind=kOutput, calls=%fused_computation.31 | convolution fusion | flops 875305984 | bytes 53239808 | tf_op jit(solution)/shard_map/hqk,qhd->khd/dot_general | solution.py:160
  269.4 45.7 %convert_reduce_fusion.2 = (f32[12,64]{1,0:T(8,128)}, bf16[12,64,512]{2,1,0:T(8,128)(2,1)}) fusion(bf16[1024,12,64]{0,2,1:T(8,128)(2,1)} %bitcast.119, f32[12,512,1024]{2,1,0:T(8,128)} %fusion.78, f32[12,512]{1,0:T(8,128)S(1)} %log_add_fusion, f32[12,512,1024]{2,1,0:T(8,128)} %get-tuple-element.89, pred[512,1024]{1,0:T(8,128)(4,1)S(1)} %broadcast_compare_fusion), kind=kOutput, calls=%fused_computation.38 | convolution fusion | flops 875698432 | bytes 53242880 | tf_op jit(solution)/shard_map/hqk,khd->qhd/dot_general | solution.py:159
  315.1 0.8 convolution_convert_fusion.4
  315.8 0.6 copy-done.2
  316.5 4.9 convolution_convert_fusion.1
  321.4 3.0 convolution_convert_fusion
  324.4 2.1 convolution_convert_fusion.7
  326.5 0.4 copy-done.29
  326.9 1.4 convolution_convert_fusion.6
  328.3 1.4 convolution_convert_fusion.5
  330.0 0.3 constant_dynamic-update-slice_fusion.1
  330.3 0.3 constant_dynamic-update-slice_fusion
  330.6 5.6 %copy.49 = bf16[4,8,288,768]{3,2,0,1:T(8,128)(2,1)} copy(bf16[4,8,288,768]{3,2,1,0:T(8,128)(2,1)S(1)} %bitcast.90) | data formatting | bytes 28311552 | tf_op jit(solution)/shard_map/reshape | solution.py:196
  336.3 99.0 %reduce-scatter.3.cloned.1.call-done = bf16[1152,768]{1,0:T(8,128)(2,1)} async-done(((bf16[9216,768]{1,0:T(8,128)(2,1)}), bf16[1152,768]{1,0:T(8,128)(2,1)}) %reduce-scatter.3.cloned.1.call-update) | async-done | bytes 1769488 | tf_op jit(solution)/shard_map/reduce_scatter | solution.py:197
  435.6 40.4 %reduce-scatter.5.cloned.1.call-done = bf16[288,768]{1,0:T(8,128)(2,1)} async-done(((bf16[1152,768]{1,0:T(8,128)(2,1)}), bf16[288,768]{1,0:T(8,128)(2,1)}) %reduce-scatter.5.cloned.1.call-update) | async-done | bytes 442384 | tf_op jit(solution)/shard_map/reduce_scatter | solution.py:198
  476.1 3.0 fusion.79
  479.2 1.5 convolution_add_fusion
  480.6 1.7 copy-done.8
  482.4 0.7 collective-permute-start
  483.0 42.0 %all-reduce = (f32[12,64]{1,0:T(8,128)}, f32[12,64]{1,0:T(8,128)}, f32[768]{0:T(1024)}, f32[768]{0:T(1024)}, f32[768]{0:T(1024)}, /*index=5*/f32[3072]{0:T(1024)}, f32[768]{0:T(1024)}, f32[768]{0:T(1024)}, f32[768]{0:T(1024)}) all-reduce(f32[12,64]{1,0:T(8,128)} %get-tuple-element.97, ...), channel_id=1, replica_groups=mesh['dp'=8,'tensor'=4] {'dp','tensor'}, use_global_device_ids=true, to_apply=%region_14.15 | all-reduce | flops 9216 | bytes 73728 | tf_op jit(solution)/shard_map/psum | solution.py:210
  525.1 1.4 dynamic_slice.35
  526.4 1.4 fusion.51
  527.8 3.9 fusion.21
  531.7 1.4 slice.66
  533.1 1.3 copy.50
  534.5 0.5 convert_element_type.186
  535.0 1.6 slice_bitcast_fusion
  536.6 3.0 copy.51
  539.6 0.9 slice.67
  540.5 1.6 slice.69
  (109 shorter events, 2.3 us)
Async XLA Ops:
  7.2 3.0 copy-start.17
  7.2 3.0 copy-start.21
  7.2 110.8 %all-gather.5.cloned.1.call-start = ((), (), s32[]{:S(2)}) async-start(), calls=%async_computation.2 | async-start | bytes 14598144 | tf_op jit(solution)/shard_map/all_gather | solution.py:90
  8.9 3.3 copy-start.23
  8.9 3.3 copy-start.24
  9.0 22.5 %copy-start.22 = (s32[2048]{0:T(1024)S(1)}, s32[2048]{0:T(1024)}, u32[]{:S(2)}) copy-start(s32[2048]{0:T(1024)} %param.16) | copy-start | bytes 24580
  12.1 423.2 %reduce-scatter.3.cloned.1.call-start = ((), (), s32[]{:S(2)}) async-start(), calls=%async_computation.3 | async-start | bytes 15925248 | tf_op jit(solution)/shard_map/reduce_scatter | solution.py:197
  130.1 1.1 copy-start.4
  133.4 3.5 copy-start.6
  136.9 10.6 %copy-start.11 = (bf16[1024,768]{0,1:T(8,128)(2,1)}, bf16[1024,768]{0,1:T(8,128)(2,1)S(1)}, u32[]{:S(2)}) copy-start(bf16[1024,768]{0,1:T(8,128)(2,1)S(1)} %convolution_convert_fusion.3) | copy-start | bytes 4718596
  147.5 12.1 %copy-start.12 = (bf16[4,192,768]{2,1,0:T(8,128)(2,1)S(1)}, bf16[4,192,768]{2,1,0:T(8,128)(2,1)}, u32[]{:S(2)}) copy-start(bf16[4,192,768]{2,1,0:T(8,128)(2,1)} %get-tuple-element.84) | copy-start | bytes 3538948
  147.5 12.1 %copy-start.25 = (bf16[2048,768]{1,0:T(8,128)(2,1)S(1)}, bf16[2048,768]{1,0:T(8,128)(2,1)}, u32[]{:S(2)}) copy-start(bf16[2048,768]{1,0:T(8,128)(2,1)} %param.15) | copy-start | bytes 9437188
  159.6 16.2 %slice-start = ((s8[4718592]{0:T(1024)(128)(4,1)}), s8[4194304]{0:T(1024)(128)(4,1)S(1)}, s32[]{:S(2)}) async-start(s8[4718592]{0:T(1024)(128)(4,1)} %bitcast.104), calls=%async_computation.6 | async-start | bytes 8388608
  161.1 12.0 %copy-start.3 = (bf16[1024,768]{0,1:T(8,128)(2,1)}, bf16[1024,768]{0,1:T(8,128)(2,1)S(1)}, u32[]{:S(2)}) copy-start(bf16[1024,768]{0,1:T(8,128)(2,1)S(1)} %add_convert_fusion) | copy-start | bytes 4718596
  161.1 12.0 %copy-start.15 = (bf16[4,192,768]{2,1,0:T(8,128)(2,1)S(1)}, bf16[4,192,768]{2,1,0:T(8,128)(2,1)}, u32[]{:S(2)}) copy-start(bf16[4,192,768]{2,1,0:T(8,128)(2,1)} %get-tuple-element.81) | copy-start | bytes 3538948
  161.1 14.7 %slice-start.1 = ((s8[4718592]{0:T(1024)(128)(4,1)}), s8[524288]{0:T(1024)(128)(4,1)S(1)}, s32[]{:S(2)}) async-start(s8[4718592]{0:T(1024)(128)(4,1)} %bitcast.104), calls=%async_computation.7 | async-start | bytes 1048576
  173.1 2.7 copy-start.18
  175.4 18.2 %copy-start.1 = (f32[512,768]{1,0:T(8,128)}, f32[512,768]{1,0:T(8,128)S(1)}, u32[]{:S(2)}) copy-start(f32[512,768]{1,0:T(8,128)S(1)} %get-tuple-element.91) | copy-start | bytes 4718596
  175.4 3.5 slice-start.2
  175.8 3.2 slice-start.3
  179.0 2.8 copy-start.30
  179.0 3.1 copy-start.7
  184.7 5.3 copy-start.9
  190.0 3.6 copy-start.32
  193.6 1.3 copy-start.16
  269.4 45.7 %copy-start.19 = (bf16[12,64,512]{2,1,0:T(8,128)(2,1)S(1)}, bf16[12,64,512]{2,1,0:T(8,128)(2,1)}, u32[]{:S(2)}) copy-start(bf16[12,64,512]{2,1,0:T(8,128)(2,1)} %copy-done.18) | copy-start | bytes 2359300
  315.1 1.4 copy-start.2
  316.5 4.9 copy-start.10
  316.5 4.9 copy-start.31
  321.4 3.0 copy-start.20
  324.3 2.2 copy-start.26
  324.4 2.6 copy-start.29
  326.9 1.4 copy-start.27
  336.2 139.8 %copy-start.14 = (bf16[4,192,768]{2,1,0:T(8,128)(2,1)S(1)}, bf16[4,192,768]{2,1,0:T(8,128)(2,1)}, u32[]{:S(2)}) copy-start(bf16[4,192,768]{2,1,0:T(8,128)(2,1)} %get-tuple-element.82) | copy-start | bytes 3538948
  336.3 139.8 %reduce-scatter.5.cloned.1.call-start = ((), (), s32[]{:S(2)}) async-start(), calls=%async_computation.4 | async-start | bytes 2211840 | tf_op jit(solution)/shard_map/reduce_scatter | solution.py:198
  435.3 96.3 %all-gather.7.cloned.1.call-start = ((), (), s32[]{:S(2)}) async-start(), calls=%async_computation.5 | async-start | bytes 3981312 | tf_op jit(solution)/shard_map/all_gather | solution.py:199
  476.1 3.0 copy-start.13
  476.1 3.0 copy-start.28
  479.1 48.7 %copy-start.5 = (bf16[4,192,768]{2,1,0:T(8,128)(2,1)S(1)}, bf16[4,192,768]{2,1,0:T(8,128)(2,1)}, u32[]{:S(2)}) copy-start(bf16[4,192,768]{2,1,0:T(8,128)(2,1)} %copy-done.4) | copy-start | bytes 3538948
  480.6 1.7 copy-start.8
  482.4 45.4 %collective-permute-start = (bf16[512,768]{1,0:T(8,128)(2,1)S(1)}, bf16[512,768]{1,0:T(8,128)(2,1)}, u32[]{:S(2)}, u32[]{:S(2)}) collective-permute-start(bf16[512,768]{1,0:T(8,128)(2,1)S(1)} %fusion.33), channel_id=1, source_target_pairs={{0,1},{1,0},{2,3},{3,2},{4,5},{5,4},{6,7},{7,6},{8,9},{9,8},{10,11... | collective-permute-start | bytes 2359304 | tf_op jit(solution)/shard_map/ppermute | solution.py:178
  531.7 2.8 copy-start
Sparse Core Ops, SparseCore 0:
  12.2 105.6 all-gather.4
  336.4 98.8 reduce-scatter.2
  437.6 38.3 reduce-scatter.4
  477.9 33.5 all-gather.6

commit v2 on v1

v2 whole, which is shorter than its diff:
```python
import functools

import jax
import jax.numpy as jnp
from jax import lax
from jax.experimental import pallas as pl
from jax.experimental.pallas import tpu as pltpu
from jax.sharding import PartitionSpec as P

SEQ = 1024


EPSILON = 1e-06
MASKED = -1e30
LOW = jnp.bfloat16
HIGH = jnp.float32


def dot_nn(left, right):
    return lax.dot_general(left, right, (((1,), (0,)), ((), ())), preferred_element_type=HIGH)


def dot_nt(left, right):
    return lax.dot_general(left, right, (((1,), (1,)), ((), ())), preferred_element_type=HIGH)


def dot_tn(left, right):
    return lax.dot_general(left, right, (((0,), (0,)), ((), ())), preferred_element_type=HIGH)


def norm_forward(summed):
    mean = jnp.mean(summed, axis=-1, keepdims=True)
    centred = summed - mean
    spread = jnp.mean(centred * centred, axis=-1, keepdims=True)
    inverse = lax.rsqrt(spread + EPSILON)
    return centred * inverse, inverse


def norm_backward(xhat, inverse, scaled):
    return inverse * (
        scaled
        - jnp.mean(scaled, axis=-1, keepdims=True)
        - xhat * jnp.mean(scaled * xhat, axis=-1, keepdims=True)
    )


def gelu_parts(u):
    phi_cdf = 0.5 * (1.0 + lax.erf(u * (2.0**-0.5)))
    density = jnp.exp(-0.5 * u * u) * 0.3989422804014327
    return u * phi_cdf, phi_cdf + u * density


def column_sum(values):
    return jnp.sum(values, axis=0, keepdims=True)

MESH = pl.DeviceIdType.MESH
VMEM_LIMIT = 60 * 1024 * 1024


class Place:
    def __init__(self, n_tensor):
        self.z = lax.axis_index("tensor")
        self.dp = lax.axis_index("dp")
        self.core = lax.rem(self.dp, 2)
        self.a = lax.rem(self.dp // 2, 2)
        self.b = lax.rem(self.dp // 4, 2)
        self.to_core = (self.dp + 1 - 2 * self.core, self.z)
        self.to_a = (self.dp + 2 - 4 * self.a, self.z)
        self.to_b = (self.dp + 4 - 8 * self.b, self.z)
        self.others = [lax.rem(self.z + step, n_tensor) for step in range(1, n_tensor)]
        if n_tensor == 4:
            near = self.z + 1 - 2 * lax.rem(self.z, 2)
            upper = self.z // 2
            self.others = [near, 2 - upper, 3 - 3 * upper]

    def partners(self):
        return [self.to_core, self.to_a, self.to_b] + [(self.dp, z) for z in self.others]


def meet(place):
    barrier = pltpu.get_barrier_semaphore()
    partners = place.partners()
    for partner in partners:
        pl.semaphore_signal(barrier, inc=1, device_id=partner, device_id_type=MESH)
    pl.semaphore_wait(barrier, len(partners))


def remote(src, dst, send, recv, target):
    return pltpu.make_async_remote_copy(
        src_ref=src,
        dst_ref=dst,
        send_sem=send,
        recv_sem=recv,
        device_id=target,
        device_id_type=MESH,
    )


class Gather:
    def __init__(self, place, whole, local, send, recv, group):
        self.place, self.whole, self.local = place, whole, local
        self.send, self.recv, self.group = send, recv, group
        self.quarter = whole.shape[1] // 4
        self.half = whole.shape[2] // 2

    def window(self, a, b, side):
        rows = pl.ds(pl.multiple_of((a * 2 + b) * self.quarter, 16), self.quarter)
        return rows, pl.ds(pl.multiple_of(side * self.half, 128), self.half)

    def piece(self, z, a, b, side):
        rows, columns = self.window(a, b, side)
        return self.whole.at[z, rows, columns]

    def sems(self, z, slot):
        return self.send.at[self.group, z, slot], self.recv.at[self.group, z, slot]

    def pass_on(self, z, slot, a, b, side, target):
        part = self.piece(z, a, b, side)
        return remote(part, part, *self.sems(z, slot), target)

    def along(self, z):
        p = self.place
        rows, columns = self.window(p.a, p.b, p.core)
        return remote(
            self.local.at[rows, columns],
            self.whole.at[p.z, rows, columns],
            self.send.at[self.group, z, 0],
            self.recv.at[self.group, p.z, 0],
            (p.dp, z),
        )

    def start(self):
        for z in self.place.others:
            self.along(z).start()

    def first(self, z):
        p = self.place
        self.pass_on(z, 0, p.a, p.b, p.core, p.to_core).wait_recv()
        self.pass_on(z, 1, p.a, p.b, p.core, p.to_a).start()
        self.pass_on(z, 2, p.a, p.b, p.core, p.to_b).start()
        self.pass_on(z, 4, p.a, p.b, p.core, p.to_core).start()

    def turn(self, z):
        p = self.place
        odd = lax.rem(z + self.group, 2)
        a = p.a * odd + (1 - p.a) * (1 - odd)
        b = p.b * (1 - odd) + (1 - p.b) * odd
        target = odd * p.to_a[0] + (1 - odd) * p.to_b[0]
        return self.pass_on(z, 3, a, b, p.core, (target, p.z))

    def second(self, z):
        p = self.place
        self.pass_on(z, 1, 1 - p.a, p.b, p.core, p.to_a).wait_recv()
        self.pass_on(z, 2, p.a, 1 - p.b, p.core, p.to_b).wait_recv()
        self.turn(z).start()
        self.pass_on(z, 5, 1 - p.a, p.b, p.core, p.to_core).start()
        self.pass_on(z, 6, p.a, 1 - p.b, p.core, p.to_core).start()

    def third(self, z):
        p = self.place
        self.pass_on(z, 3, 1 - p.a, 1 - p.b, p.core, p.to_a).wait_recv()
        self.pass_on(z, 7, 1 - p.a, 1 - p.b, p.core, p.to_core).start()

    def last(self, z):
        p = self.place
        side = 1 - p.core
        self.pass_on(z, 4, p.a, p.b, side, p.to_core).wait_recv()
        self.pass_on(z, 5, 1 - p.a, p.b, side, p.to_core).wait_recv()
        self.pass_on(z, 6, p.a, 1 - p.b, side, p.to_core).wait_recv()
        self.pass_on(z, 7, 1 - p.a, 1 - p.b, side, p.to_core).wait_recv()

    def finish(self):
        p = self.place
        for z in p.others:
            self.along(z).wait_send()
            self.pass_on(z, 1, p.a, p.b, p.core, p.to_a).wait_send()
            self.pass_on(z, 2, p.a, p.b, p.core, p.to_b).wait_send()
            self.turn(z).wait_send()
            self.pass_on(z, 4, p.a, p.b, p.core, p.to_core).wait_send()
            self.pass_on(z, 5, 1 - p.a, p.b, p.core, p.to_core).wait_send()
            self.pass_on(z, 6, p.a, 1 - p.b, p.core, p.to_core).wait_send()
            self.pass_on(z, 7, 1 - p.a, 1 - p.b, p.core, p.to_core).wait_send()


def segment_bias(own_segments, row_segments):
    return jnp.where(own_segments == row_segments, 0.0, MASKED)


def gather_attend(
    n_tensor,
    heads,
    scale,
    row_input,
    own_segments,
    row_segments,
    local_a,
    local_b,
    local_c,
    local_small,
    out_a,
    whole_b,
    whole_c,
    small,
    attended,
    queries,
    keys,
    values,
    log_totals,
    whole_a,
    small_land,
    bias,
    mixed,
    send,
    recv,
    small_send,
    small_recv,
    copy_sem,
):
    place = Place(n_tensor)
    share = own_segments.shape[0]
    shares_per_row = row_input.shape[0] // share
    group_rows = local_a.shape[0] // 3
    size = group_rows // heads
    in_row = pl.ds(pl.multiple_of(lax.rem(place.z, shares_per_row) * share, share), share)
    meet(place)
    gather_a = Gather(place, whole_a, local_a, send, recv, 0)
    gather_b = Gather(place, whole_b, local_b, send, recv, 1)
    gather_c = Gather(place, whole_c, local_c, send, recv, 2)

    def small_copy(z):
        return remote(
            local_small, small_land.at[place.z], small_send.at[z], small_recv.at[place.z], (place.dp, z)
        )

    def small_arrival(z):
        return remote(
            local_small, small_land.at[z], small_send.at[z], small_recv.at[z], (place.dp, z)
        )

    for z in place.others:
        small_copy(z).start()
    gather_a.start()
    own_a = pltpu.make_async_copy(local_a, whole_a.at[place.z], copy_sem.at[0])
    own_b = pltpu.make_async_copy(local_b, whole_b.at[place.z], copy_sem.at[1])
    own_c = pltpu.make_async_copy(local_c, whole_c.at[place.z], copy_sem.at[2])
    own_a.start()
    small_land[place.z] = local_small[...]
    bias[...] = segment_bias(own_segments[...], row_segments[...])
    own_a.wait()

    def save_a(z, slot):
        return pltpu.make_async_copy(whole_a.at[z], out_a.at[z], copy_sem.at[slot])

    def attend(z, between):
        weights = whole_a[z]
        q_bias = small_land[z, 0:1, :group_rows]
        v_bias = small_land[z, 1:2, :group_rows]
        q = dot_nt(row_input[in_row], weights[:group_rows]) + q_bias
        q = q.astype(LOW)
        k = dot_nt(row_input[...], weights[group_rows : 2 * group_rows]).astype(LOW)
        v = (dot_nt(row_input[...], weights[2 * group_rows :]) + v_bias).astype(LOW)
        for head in range(heads):
            part = slice(head * size, (head + 1) * size)
            queries[z, head] = q[:, part] * scale
            keys[z, head] = k[:, part]
            values[z, head] = v[:, part]

        def one_head(head, carry):
            chunk = min(256, share)
            for at in range(0, share, chunk):
                rows = pl.ds(at, chunk)
                scores = dot_nt(queries[z, head, rows], keys[z, head]) + bias[rows]
                top = jnp.max(scores, axis=-1, keepdims=True)
                raised = jnp.exp(scores - top)
                total = jnp.sum(raised, axis=-1, keepdims=True)
                summed = dot_nn(raised.astype(LOW), values[z, head])
                mixed[head, rows] = (summed / total).astype(LOW)
                log_totals[z, head, rows] = top + jnp.log(total)
            for at, service in enumerate(between):
                pl.when(head == at)(service)
            return carry

        lax.fori_loop(0, heads, one_head, 0)
        attended[z] = jnp.concatenate([mixed[head] for head in range(heads)], axis=-1)

    near, middle, far = place.others

    def services(*steps):
        def run():
            for step, z in steps:
                step(z)

        return run

    def start_b():
        gather_b.start()
        own_b.start()

    def start_c():
        gather_c.start()
        own_c.start()

    attend(place.z, [start_b, start_c])
    save_a(place.z, 3).start()
    for z in place.others:
        gather_a.first(z)
    for z in place.others:
        gather_a.second(z)
    for z in place.others:
        gather_a.third(z)
        small_arrival(z).wait_recv()
    gather_a.last(near)
    attend(
        near,
        [
            services((gather_b.first, near)),
            services((gather_b.first, middle)),
            services((gather_b.second, near), (gather_b.first, far)),
        ],
    )
    save_a(near, 4).start()
    gather_a.last(middle)
    attend(
        middle,
        [
            services((gather_b.third, near), (gather_b.second, middle), (gather_c.first, near)),
            services((gather_b.second, far), (gather_b.third, middle)),
            services((gather_b.third, far), (gather_c.first, middle), (gather_c.second, near)),
        ],
    )
    save_a(middle, 5).start()
    gather_a.last(far)
    attend(
        far,
        [
            services((gather_c.first, far)),
            services((gather_c.second, middle), (gather_c.third, near)),
            services(),
        ],
    )
    save_a(far, 6).start()
    gather_c.second(far)
    gather_c.third(middle)
    gather_c.third(far)
    small[...] = small_land[...]
    for z in place.others:
        gather_b.last(z)
        gather_c.last(z)
        small_copy(z).wait_send()
    for gather in (gather_a, gather_b, gather_c):
        gather.finish()
    own_b.wait()
    own_c.wait()
    for slot, z in enumerate([place.z] + place.others):
        save_a(z, 3 + slot).wait()


def attend_back(
    n_tensor,
    heads,
    scale,
    row_input,
    own_segments,
    row_segments,
    first_low,
    whole_a,
    whole_out,
    queries,
    keys,
    values,
    log_totals,
    grad_a,
    bias_sums,
    own_term,
    row_term,
    bias,
    grad_mixed,
    grad_q,
    grad_k,
    grad_v,
):
    z_here = lax.axis_index("tensor")
    share = own_segments.shape[0]
    shares_per_row = row_input.shape[0] // share
    group_rows = whole_a.shape[1] // 3
    size = group_rows // heads
    in_row = pl.ds(pl.multiple_of(lax.rem(z_here, shares_per_row) * share, share), share)
    bias[...] = segment_bias(own_segments[...], row_segments[...])
    own_term[...] = jnp.zeros_like(own_term)
    row_term[...] = jnp.zeros_like(row_term)

    def one_shard(z, carry):
        incoming = dot_nt(first_low[...], whole_out[z]).astype(LOW)
        for head in range(heads):
            grad_mixed[head] = incoming[:, head * size : (head + 1) * size]

        def one_head(head, inner):
            q, k, v = queries[z, head], keys[z, head], values[z, head]
            up = grad_mixed[head]
            chance = jnp.exp(dot_nt(q, k) + bias[...] - log_totals[z, head])
            change = chance * dot_nt(up, v)
            change = change - chance * jnp.sum(change, axis=-1, keepdims=True)
            change = change.astype(LOW)
            grad_q[head] = (dot_nn(change, k) * scale).astype(LOW)
            grad_k[head] = dot_nn(q.T, change).astype(LOW)
            grad_v[head] = dot_nn(up.T, chance.astype(LOW)).astype(LOW)
            return inner

        lax.fori_loop(0, heads, one_head, 0)
        dq = jnp.concatenate([grad_q[head] for head in range(heads)], axis=-1)
        dk = grad_k[...].reshape(group_rows, -1)
        dv = grad_v[...].reshape(group_rows, -1)
        x_own, x_row = row_input[in_row], row_input[...]
        grad_a[z, :group_rows] = dot_tn(dq, x_own).astype(LOW)
        grad_a[z, group_rows : 2 * group_rows] = dot_nn(dk, x_row).astype(LOW)
        grad_a[z, 2 * group_rows :] = dot_nn(dv, x_row).astype(LOW)
        weights = whole_a[z]
        own_term[...] += dot_nn(dq, weights[:group_rows])
        row_term[...] += dot_tn(
            jnp.concatenate([dk, dv], axis=0), weights[group_rows:]
        )
        ones = jnp.ones((8, x_row.shape[0]), LOW)
        bias_sums[z, 0:8, :group_rows] = dot_nn(ones[:, :share], dq)
        bias_sums[z, 8:16, :group_rows] = dot_nt(ones, dv)
        return carry

    lax.fori_loop(0, n_tensor, one_shard, 0)


def on_device(
    layer_input,
    segment_ids,
    w_qkv,
    qv_bias,
    w_out,
    out_bias,
    norm1_gain,
    norm1_bias,
    w_up,
    up_bias,
    w_down,
    down_bias,
    norm2_gain,
    norm2_bias,
    out_cotangent,
):
    n_tensor = lax.axis_size("tensor")
    place = lax.axis_index("tensor")
    n_dp = lax.axis_size("dp")
    dp_place = lax.axis_index("dp")
    tokens, width = layer_input.shape
    share = tokens // n_tensor
    local_heads = qv_bias.shape[0]
    heads = local_heads * n_tensor
    head_dim = qv_bias.shape[1] // 2
    score_scale = float(head_dim) ** (-0.5)
    shares_per_row = SEQ // share
    row_start = (place // shares_per_row) * SEQ
    own_start = place * share
    in_row = (place % shares_per_row) * share

    units = w_up.shape[1]
    local_width = local_heads * head_dim
    local_a = w_qkv.reshape(width, local_heads, 3, head_dim).transpose(2, 1, 3, 0).reshape(-1, width)
    local_b = jnp.concatenate([w_out, w_up], axis=0)
    local_c = w_down
    local_small = jnp.zeros((8, width), HIGH)
    local_small = local_small.at[0, :local_width].set(qv_bias[:, :head_dim].reshape(-1).astype(HIGH))
    local_small = local_small.at[1, :local_width].set(qv_bias[:, head_dim:].reshape(-1).astype(HIGH))
    local_small = local_small.at[2, :units].set(up_bias.astype(HIGH))

    row_input = lax.dynamic_slice_in_dim(layer_input, row_start, SEQ, 0)
    own_input = lax.dynamic_slice_in_dim(layer_input, own_start, share, 0)
    row_segments = lax.dynamic_slice_in_dim(segment_ids, row_start, SEQ, 0)
    own_segments = lax.dynamic_slice_in_dim(segment_ids, own_start, share, 0)

    own_column, row_line = own_segments[:, None], row_segments[None, :]
    vmem = pl.BlockSpec(memory_space=pltpu.VMEM)
    anywhere = pl.BlockSpec(memory_space=pl.ANY)
    shape_a = (n_tensor,) + local_a.shape
    shape_b = (n_tensor,) + local_b.shape
    shape_c = (n_tensor,) + local_c.shape
    per_head = (n_tensor, local_heads)
    whole_a, whole_b, whole_c, small, attended, queries, keys, values, log_totals = pl.pallas_call(
        functools.partial(gather_attend, n_tensor, local_heads, score_scale),
        out_shape=(
            jax.ShapeDtypeStruct(shape_a, LOW),
            jax.ShapeDtypeStruct(shape_b, LOW),
            jax.ShapeDtypeStruct(shape_c, LOW),
            jax.ShapeDtypeStruct((n_tensor,) + local_small.shape, HIGH),
            jax.ShapeDtypeStruct((n_tensor, share, local_width), LOW),
            jax.ShapeDtypeStruct(per_head + (share, head_dim), LOW),
            jax.ShapeDtypeStruct(per_head + (SEQ, head_dim), LOW),
            jax.ShapeDtypeStruct(per_head + (SEQ, head_dim), LOW),
            jax.ShapeDtypeStruct(per_head + (share, 1), HIGH),
        ),
        in_specs=[vmem, vmem, vmem, anywhere, anywhere, anywhere, vmem],
        out_specs=(anywhere, anywhere, anywhere, vmem, vmem, vmem, vmem, vmem, vmem),
        scratch_shapes=[
            pltpu.VMEM(shape_a, LOW),
            pltpu.VMEM((n_tensor,) + local_small.shape, HIGH),
            pltpu.VMEM((share, SEQ), HIGH),
            pltpu.VMEM((local_heads, share, head_dim), LOW),
            pltpu.SemaphoreType.DMA((3, n_tensor, 8)),
            pltpu.SemaphoreType.DMA((3, n_tensor, 8)),
            pltpu.SemaphoreType.DMA((n_tensor,)),
            pltpu.SemaphoreType.DMA((n_tensor,)),
            pltpu.SemaphoreType.DMA((8,)),
        ],
        compiler_params=pltpu.CompilerParams(
            collective_id=0, has_side_effects=True, vmem_limit_bytes=VMEM_LIMIT
        ),
        name="gather_attend",
    )(row_input, own_column, row_line, local_a, local_b, local_c, local_small)
    out_rows = whole_b[:, :local_width]
    up_cols = whole_b[:, local_width:]
    down_rows = whole_c
    up_bias_full = small[:, 2, :units]

    first_sum = own_input.astype(HIGH) + out_bias.astype(HIGH)
    for z in range(n_tensor):
        first_sum = first_sum + dot_nn(attended[z], out_rows[z])
    gain_first = norm1_gain.astype(HIGH)
    gain_second = norm2_gain.astype(HIGH)
    xhat_first, inverse_first = norm_forward(first_sum)
    hidden = xhat_first * gain_first + norm1_bias.astype(HIGH)
    hidden_low = hidden.astype(LOW)
    second_sum = hidden + down_bias.astype(HIGH)
    slopes, activations = [], []
    for z in range(n_tensor):
        gelu_value, gelu_slope = gelu_parts(dot_nn(hidden_low, up_cols[z]) + up_bias_full[z])
        activations.append(gelu_value.astype(LOW))
        slopes.append(gelu_slope)
        second_sum = second_sum + dot_nn(activations[z], down_rows[z])
    xhat_second, inverse_second = norm_forward(second_sum)
    output = (xhat_second * gain_second + norm2_bias.astype(HIGH)).astype(LOW)

    live = (own_segments >= 0).astype(HIGH)
    cotangent = out_cotangent.astype(HIGH) * live[:, None]
    grad_second = norm_backward(xhat_second, inverse_second, cotangent * gain_second)
    second_low = grad_second.astype(LOW)
    grad_hidden = grad_second
    grads_up, grads_down, grad_ups = [], [], []
    for z in range(n_tensor):
        grads_down.append(dot_tn(activations[z], second_low).astype(LOW))
        grad_up_pre = (dot_nt(second_low, down_rows[z]) * slopes[z]).astype(LOW)
        grads_up.append(dot_tn(hidden_low, grad_up_pre).astype(LOW))
        grad_hidden = grad_hidden + dot_nt(grad_up_pre, up_cols[z])
        grad_ups.append(jnp.sum(grad_up_pre.astype(HIGH), axis=0))
    grad_first = norm_backward(xhat_first, inverse_first, grad_hidden * gain_first)
    first_low = grad_first.astype(LOW)
    grads_out = [dot_tn(attended[z], first_low).astype(LOW) for z in range(n_tensor)]

    grad_a, bias_sums, own_term, row_term = pl.pallas_call(
        functools.partial(attend_back, n_tensor, local_heads, score_scale),
        out_shape=(
            jax.ShapeDtypeStruct(shape_a, LOW),
            jax.ShapeDtypeStruct((n_tensor, 16, width), HIGH),
            jax.ShapeDtypeStruct((share, width), HIGH),
            jax.ShapeDtypeStruct((SEQ, width), HIGH),
        ),
        in_specs=[vmem] * 10,
        out_specs=(vmem,) * 4,
        scratch_shapes=[
            pltpu.VMEM((share, SEQ), HIGH),
            pltpu.VMEM((local_heads, share, head_dim), LOW),
            pltpu.VMEM((local_heads, share, head_dim), LOW),
            pltpu.VMEM((local_heads, head_dim, SEQ), LOW),
            pltpu.VMEM((local_heads, head_dim, SEQ), LOW),
        ],
        compiler_params=pltpu.CompilerParams(vmem_limit_bytes=VMEM_LIMIT),
        name="attend_back",
    )(
        row_input, own_column, row_line, first_low, whole_a, out_rows, queries, keys, values, log_totals
    )

    row_term = row_term.reshape(shares_per_row, share, width)
    my_half = place % shares_per_row
    input_grad = grad_first + own_term + row_term[my_half]
    for step in range(1, shares_per_row):
        pairs = [
            (p, (p // shares_per_row) * shares_per_row + (p + step) % shares_per_row)
            for p in range(n_tensor)
        ]
        sent = row_term[(my_half + step) % shares_per_row].astype(LOW)
        input_grad = input_grad + lax.ppermute(sent, "tensor", pairs).astype(HIGH)

    gradients = jnp.stack(
        [
            jnp.concatenate([grad_a[z], grads_out[z], grads_up[z], grads_down[z]], axis=0)
            for z in range(n_tensor)
        ]
    )
    rows_all = gradients.shape[1]
    slab = rows_all // n_dp
    gradients = gradients.reshape(n_tensor, n_dp, slab, width).transpose(1, 0, 2, 3)
    part = lax.psum_scatter(gradients.reshape(-1, width), "dp", scatter_dimension=0, tiled=True)
    part = lax.psum_scatter(part, "tensor", scatter_dimension=0, tiled=True)
    summed = lax.all_gather(part, "dp", axis=0, tiled=True).astype(HIGH)
    at = 3 * local_width
    grad_qkv = (
        summed[:at].reshape(3, local_heads, head_dim, width).transpose(3, 1, 0, 2)
    ).reshape(width, local_heads, 3 * head_dim)
    grad_out = summed[at : at + local_width]
    at += local_width
    grad_up = summed[at : at + width]
    at += width
    grad_down = summed[at : at + units]

    vectors = lax.psum(
        (
            bias_sums[:, 0, :local_width].reshape(heads, head_dim),
            bias_sums[:, 8, :local_width].reshape(heads, head_dim),
            jnp.concatenate(grad_ups),
            jnp.sum(grad_first, axis=0),
            jnp.sum(grad_hidden * xhat_first, axis=0),
            jnp.sum(grad_hidden, axis=0),
            jnp.sum(grad_second, axis=0),
            jnp.sum(cotangent * xhat_second, axis=0),
            jnp.sum(cotangent, axis=0),
        ),
        ("dp", "tensor"),
    )
    grad_qv = jnp.concatenate([vectors[0], vectors[1]], axis=1)
    grad_qv_bias = lax.dynamic_slice_in_dim(grad_qv, place * local_heads, local_heads, 0)
    grad_up_bias = lax.dynamic_slice_in_dim(vectors[2], place * units, units, 0)
    return (
        output,
        input_grad,
        grad_qkv,
        grad_qv_bias,
        grad_out,
        vectors[3],
        vectors[4],
        vectors[5],
        grad_up,
        grad_up_bias,
        grad_down,
        vectors[6],
        vectors[7],
        vectors[8],
    )


def solution(mesh):
    return jax.shard_map(
        on_device,
        mesh=mesh,
        in_specs=(
            P("dp", None),
            P("dp"),
            P(None, "tensor", None),
            P("tensor", None),
            P("tensor", None),
            P(),
            P(),
            P(),
            P(None, "tensor"),
            P("tensor"),
            P("tensor", None),
            P(),
            P(),
            P(),
            P(("dp", "tensor"), None),
        ),
        out_specs=(
            P(("dp", "tensor"), None),
            P(("dp", "tensor"), None),
            P(None, "tensor", None),
            P("tensor", None),
            P("tensor", None),
            P(),
            P(),
            P(),
            P(None, "tensor"),
            P("tensor"),
            P("tensor", None),
            P(),
            P(),
            P(),
        ),
        check_vma=False,
    )
```

time: 559 us -> 430 us (0.77)
  matrix products: 187 us -> 38.2 us
  Pallas kernels: 0 us -> 137 us
  waiting for transfers between devices: 226 us -> 140 us
  blocking collectives: 56.9 us -> 41.8 us
  other arithmetic: 24.1 us -> 14.1 us
    dot_general x6 -> x0, matrix products: 140 us -> none  [the longest x1 46.5 us: on_device(): jnp.einsum('hqk,qhd->khd', grad_raw, queries, preferred_element_type=HIGH)]
    pallas_call x0 -> x2, Pallas kernels: none -> 137 us  [the longest x1 98.2 us: on_device(): pl.pallas_call(functools.partial(gather_attend, n_tensor, local_heads, sc...]
    all_gather x1 -> x0, waiting for transfers between devices: 86.1 us -> none  [on_device(): everything = lax.all_gather(mine, ('tensor', 'dp'), axis=0, tiled=True)]
    all_gather x1 -> x0, blocking collectives: 14.8 us -> none  [on_device(): small = lax.all_gather(small, 'tensor', axis=0, tiled=False)]
    reduce_sum x1 -> x0, other arithmetic: 12.1 us -> none  [on_device(): total = jnp.sum(jnp.exp(scores - top), axis=-1, keepdims=True)]
    dot_general x6 -> x8, matrix products: 17 us -> 8.49 us  [dot_nt(): lax.dot_general(left, right, (((1,), (1,)), ((), ())), preferred_element_...]
    slice x3, local copies, waits for them, and re-layouts: 12.2 us -> 4.08 us  [the longest x1 2.45 us: on_device(): out_rows = whole_b[:, :local_width]]
    reshape x1 -> x0, local copies, waits for them, and re-layouts: 5.59 us -> none  [on_device(): gradients.reshape(n_tensor, n_dp, slab, width).transpose(1, 0, 2, 3)]
  transfers between devices with their start and end apart: 5 -> 4, of which waited for: 3 -> 2; matrix products, arithmetic and copies ran while one was open for 3% -> 2% of each run, Pallas kernels for 0% -> 0%
where the time goes in v2:
time: 430 us; the launch traced here: 422 us
  waiting for transfers between devices  140 us (33%)
  Pallas kernels  137 us (32%)
  blocking collectives  41.8 us (10%)
  matrix products  38.2 us (9%)
  local copies, waits for them, and re-layouts  35.8 us (8%)
  between operations  14.8 us (3%)
  other arithmetic  14.1 us (3%)
    reduce_scatter x1, waiting for transfers between devices, on_device(): lax.psum_scatter(gradients.reshape(-1, width), 'dp', scatter_dimension=0,...  99.1 us
    pallas_call x1, Pallas kernels, on_device(): pl.pallas_call(functools.partial(gather_attend, n_tensor, local_heads, sc...  98.2 us
    psum x1, blocking collectives, on_device(): lax.psum((bias_sums[:, 0, :local_width].reshape(heads, head_dim), bias_su...  41.8 us
    reduce_scatter x1, waiting for transfers between devices, on_device(): part = lax.psum_scatter(part, 'tensor', scatter_dimension=0, tiled=True)  40.7 us
    pallas_call x1, Pallas kernels, on_device(): pl.pallas_call(functools.partial(attend_back, n_tensor, local_heads, scor...  38.7 us
    dot_general x12, matrix products, dot_tn(): lax.dot_general(left, right, (((0,), (0,)), ((), ())), preferred_element_...  16.3 us
    dot_general x12, matrix products, dot_nn(): lax.dot_general(left, right, (((1,), (0,)), ((), ())), preferred_element_...  13.4 us
  transfers between devices with their start and end apart: 4, of which 2 were waited for; matrix products, arithmetic and copies ran while one was open for 2% of the time, Pallas kernels for 0%

profile of v2, /device:TPU:0, one launch (start us, length us, event | category | flops | bytes accessed | tf_op | source)
XLA Modules:
  0.0 422.1 jit_solution(10681539491079156142)
XLA Ops:
  7.2 0.7 reshape.220
  7.9 0.8 slice_convert_fusion
  8.9 1.3 dynamic_slice.27
  10.2 0.8 compare_convert_fusion
  11.0 0.9 copy.33.own_segments
  11.8 2.1 copy.32
  14.0 2.8 constant_dynamic-slice_fusion.row_input
  16.9 1.2 pad_maximum_fusion.4.local_b
  18.8 98.2 %gather_attend.1 = (bf16[4,576,768]{2,1,0:T(8,128)(2,1)}, bf16[4,960,768]{2,1,0:T(8,128)(2,1)}, bf16[4,768,768]{2,1,0:T(8,128)(2,1)}, f32[4,8,768]{2,1,0:T(8,128...) custom-call(bf16[1024,768]{1,0:T(8,128)(2,1)} %constant_dynamic-slic, ...), custom_call_target="tpu_custom_call" | custom-call | tf_op jit(solution)/shard_map/gather_attend/pallas_call | solution.py:484
  117.0 2.5 slice.201.whole_out
  119.4 1.5 fusion.69
  120.9 1.6 fusion.71
  122.6 1.3 fusion.73
  124.1 0.8 slice_reduce_fusion.2
  124.9 1.8 fusion.99
  127.4 0.8 convolution_add_fusion
  128.2 0.9 multiply_convert_fusion.1
  129.1 0.9 multiply_convert_fusion.2
  130.0 0.8 fusion.34
  130.8 0.8 fusion.40
  131.6 0.9 multiply_convert_fusion.3
  132.5 0.8 fusion.46
  133.3 1.4 fusion.100
  135.0 0.8 copy-done.3
  135.8 0.9 multiply_reduce_fusion
  136.7 1.6 fusion.96
  138.4 1.1 convert_reduce_fusion
  139.5 1.9 convolution_convert_fusion
  141.4 2.0 convolution_convert_fusion.2
  143.4 0.8 convolution_convert_fusion.4
  144.2 1.8 convolution_convert_fusion.6
  146.0 1.1 convert_reduce_fusion.1
  147.2 1.9 convolution_convert_fusion.3
  149.0 0.8 fusion.36
  149.8 1.1 convert_reduce_fusion.2
  151.0 1.8 convolution_convert_fusion.5
  152.8 0.8 fusion.42
  153.6 1.1 convert_reduce_fusion.3
  154.7 1.8 convolution_convert_fusion.7
  156.6 0.8 fusion.48
  157.4 1.9 convolution_convert_fusion.1
  159.3 1.6 multiply_reduce_fusion.1
  162.2 0.6 convolution_convert_fusion.10
  162.9 1.1 convolution_convert_fusion.11
  163.9 38.7 %attend_back.1 = (bf16[4,576,768]{2,1,0:T(8,128)(2,1)}, f32[4,16,768]{2,1,0:T(8,128)}, f32[512,768]{1,0:T(8,128)}, f32[1024,768]{1,0:T(8,128)}) custom-call(bf16[1024,768]{1,0:T(8,128)(2,1)} %constant_dynamic-slice_fusion.row_input, s32[512,1]{1,0:T(8,128)} %copy.33.own_segments, s32[1,1024]{1,0:T(1,128)} %bitcast.174, bf16[512,768]{1,0:T(8,128)(2,1)} %copy-done, ...), custom_call_target="tpu_custom_call" | custom-call | tf_op jit(solution)/shard_map/attend_back/pallas_call | solution.py:554
  202.6 2.3 slice_bitcast_fusion.3
  205.7 0.9 copy-done.7
  207.3 0.9 copy-done.6
  208.9 0.9 copy-done.9
  210.2 1.9 maximum_bitcast_fusion
  212.1 5.6 %copy.35 = bf16[8,4,288,768]{3,2,1,0:T(8,128)(2,1)} copy(bf16[8,4,288,768]{3,2,0,1:T(8,128)(2,1)S(1)} %maximum_bitcast_fusion) | data formatting | bytes 28311552 | tf_op jit(solution)/shard_map/transpose | solution.py:596
  217.8 99.1 %reduce-scatter.3.cloned.1.call-done = bf16[1152,768]{1,0:T(8,128)(2,1)} async-done(((bf16[9216,768]{1,0:T(8,128)(2,1)}), bf16[1152,768]{1,0:T(8,128)(2,1)}) %reduce-scatter.3.cloned.1.call-update) | async-done | bytes 1769488 | tf_op jit(solution)/shard_map/reduce_scatter | solution.py:597
  316.9 40.7 %reduce-scatter.5.cloned.1.call-done = bf16[288,768]{1,0:T(8,128)(2,1)} async-done(((bf16[1152,768]{1,0:T(8,128)(2,1)}), bf16[288,768]{1,0:T(8,128)(2,1)}) %reduce-scatter.5.cloned.1.call-update) | async-done | bytes 442384 | tf_op jit(solution)/shard_map/reduce_scatter | solution.py:598
  357.6 2.4 fusion.67
  360.6 0.8 slice_reduce_fusion
  361.5 41.8 %all-reduce.1 = (f32[12,64]{1,0:T(8,128)S(1)}, f32[12,64]{1,0:T(8,128)S(1)}, f32[768]{0:T(1024)}, f32[768]{0:T(1024)}, f32[768]{0:T(1024)}, /*index=5*/f32[3072]...) all-reduce(f32[12,64]{1,0:T(8,128)S(1)} %reshape_squeeze.6, ...), channel_id=1, replica_groups=mesh['dp'=8,'tensor'=4] {'dp','tensor'}, use_global_device_ids=true, to_apply=%region_10.11 | all-reduce | flops 9216 | bytes 73728 | tf_op jit(solution)/shard_map/psum | solution.py:610
  403.3 0.7 dynamic_slice.31
  404.0 0.7 fusion.95
  404.7 3.2 fusion.24
  407.8 1.3 slice.212
  409.1 1.3 copy.36
  410.5 1.3 copy-done.1
  411.8 0.9 slice.213
  412.6 2.5 fusion.98
  (88 shorter events, 6.8 us)
Async XLA Ops:
  7.2 309.7 %reduce-scatter.3.cloned.1.call-start = ((), (), s32[]{:S(2)}) async-start(), calls=%async_computation.2 | async-start | bytes 15925248 | tf_op jit(solution)/shard_map/reduce_scatter | solution.py:597
  14.0 2.9 copy-start.14
  14.0 2.9 copy-start.15
  18.2 0.6 copy-start.16
  117.0 2.5 copy-start.2
  119.4 5.5 %copy-start.4 = (bf16[4,960,768]{2,1,0:T(8,128)(2,1)S(1)}, bf16[4,960,768]{2,1,0:T(8,128)(2,1)}, u32[]{:S(2)}) copy-start(bf16[4,960,768]{2,1,0:T(8,128)(2,1)} %get-tuple-element.64) | copy-start | bytes 17694724
  122.6 1.4 copy-start.17
  122.6 1.4 copy-start.18
  122.6 1.4 copy-start.19
  122.6 1.4 copy-start.20
  122.6 1.5 copy-start.21
  122.6 1.5 copy-start.22
  127.4 2.6 slice-start
  128.2 1.8 slice-start.1
  134.7 1.1 copy-start.3
  161.5 1.3 copy-start
  202.6 2.4 copy-start.10
  202.6 2.7 copy-start.12
  202.6 2.7 copy-start.13
  205.3 1.3 copy-start.7
  205.3 1.6 copy-start.11
  206.9 1.3 copy-start.6
  206.9 1.6 copy-start.8
  208.6 1.3 copy-start.9
  217.7 139.8 %reduce-scatter.5.cloned.1.call-start = ((), (), s32[]{:S(2)}) async-start(), calls=%async_computation.3 | async-start | bytes 2211840 | tf_op jit(solution)/shard_map/reduce_scatter | solution.py:598
  316.9 87.8 %copy-start.5 = (f32[512,768]{1,0:T(8,128)S(1)}, f32[512,768]{1,0:T(8,128)}, u32[]{:S(2)}) copy-start(f32[512,768]{1,0:T(8,128)} %get-tuple-element.72) | copy-start | bytes 4718596
  316.9 91.0 %all-gather.2.cloned.1.call-start = ((), (), s32[]{:S(2)}) async-start(), calls=%async_computation.4 | async-start | bytes 3981312 | tf_op jit(solution)/shard_map/all_gather | solution.py:599
  360.0 44.7 %collective-permute-start = (bf16[512,768]{1,0:T(8,128)(2,1)}, bf16[512,768]{1,0:T(8,128)(2,1)}, u32[]{:S(2)}, u32[]{:S(2)}) collective-permute-start(bf16[512,768]{1,0:T(8,128)(2,1)} %fusion.67), channel_id=1, source_target_pairs={{0,1},{1,0},{2,3},{3,2},{4,5},{5,4},{6,7},{7,6},{8,9},{9,8},{10,11... | collective-permute-start | bytes 2359304 | tf_op jit(solution)/shard_map/ppermute | solution.py:586
  409.1 2.6 copy-start.1
Sparse Core Ops, SparseCore 0:
  217.9 98.9 reduce-scatter.2
  319.2 38.3 reduce-scatter.4
  359.6 33.3 all-gather.1

commit v3 on v1

v3 whole, which is shorter than its diff:
```python
import functools

import jax
import jax.numpy as jnp
from jax import lax
from jax.experimental import pallas as pl
from jax.experimental.pallas import tpu as pltpu
from jax.sharding import PartitionSpec as P

SEQ = 1024


EPSILON = 1e-06
MASKED = -1e30
LOW = jnp.bfloat16
HIGH = jnp.float32
MESH = pl.DeviceIdType.MESH
VMEM_LIMIT = 60 * 1024 * 1024


def dot_nn(left, right):
    return lax.dot_general(left, right, (((1,), (0,)), ((), ())), preferred_element_type=HIGH)


def dot_nt(left, right):
    return lax.dot_general(left, right, (((1,), (1,)), ((), ())), preferred_element_type=HIGH)


def dot_tn(left, right):
    return lax.dot_general(left, right, (((0,), (0,)), ((), ())), preferred_element_type=HIGH)


def norm_forward(summed):
    mean = jnp.mean(summed, axis=-1, keepdims=True)
    centred = summed - mean
    spread = jnp.mean(centred * centred, axis=-1, keepdims=True)
    inverse = lax.rsqrt(spread + EPSILON)
    return centred * inverse, inverse


def norm_backward(xhat, inverse, scaled):
    return inverse * (
        scaled
        - jnp.mean(scaled, axis=-1, keepdims=True)
        - xhat * jnp.mean(scaled * xhat, axis=-1, keepdims=True)
    )


def gelu_parts(u):
    phi_cdf = 0.5 * (1.0 + lax.erf(u * (2.0**-0.5)))
    density = jnp.exp(-0.5 * u * u) * 0.3989422804014327
    return u * phi_cdf, phi_cdf + u * density


def column_sum(values):
    return jnp.sum(values, axis=0, keepdims=True)


def segment_bias(own_segments, row_segments):
    return jnp.where(own_segments == row_segments, 0.0, MASKED)


class Place:
    def __init__(self, n_tensor):
        self.n_tensor = n_tensor
        self.z = lax.axis_index("tensor")
        self.dp = lax.axis_index("dp")
        self.core = lax.rem(self.dp, 2)
        self.a = lax.rem(self.dp // 2, 2)
        self.b = lax.rem(self.dp // 4, 2)
        self.to_core = (self.dp + 1 - 2 * self.core, self.z)
        self.to_a = (self.dp + 2 - 4 * self.a, self.z)
        self.to_b = (self.dp + 4 - 8 * self.b, self.z)
        self.others = [lax.rem(self.z + step, n_tensor) for step in range(1, n_tensor)]
        if n_tensor == 4:
            near = self.z + 1 - 2 * lax.rem(self.z, 2)
            upper = self.z // 2
            self.others = [near, 2 - upper, 3 - 3 * upper]

    def pick(self, at, order):
        chosen = order[0]
        for index in range(1, len(order)):
            chosen = jnp.where(at == index, order[index], chosen)
        return chosen


def meet(partners):
    barrier = pltpu.get_barrier_semaphore()
    for partner in partners:
        pl.semaphore_signal(barrier, inc=1, device_id=partner, device_id_type=MESH)
    pl.semaphore_wait(barrier, len(partners))


def remote(src, dst, send, recv, target):
    return pltpu.make_async_remote_copy(
        src_ref=src,
        dst_ref=dst,
        send_sem=send,
        recv_sem=recv,
        device_id=target,
        device_id_type=MESH,
    )


class Spread:
    def __init__(self, place, whole, send, recv, group):
        self.place, self.whole, self.send, self.recv, self.group = place, whole, send, recv, group
        self.mine = None
        self.quarter = whole.shape[2] // 4
        self.half = whole.shape[3] // 2

    def odd(self, z):
        return lax.rem(z + self.group, 2)

    def piece(self, z, a, b, side):
        odd = self.odd(z)
        row = odd * (2 * b + a) + (1 - odd) * (2 * a + b)
        rows = pl.ds(pl.multiple_of(row * self.quarter, 16), self.quarter)
        return self.whole.at[self.group, z, rows, pl.ds(pl.multiple_of(side * self.half, 128), self.half)]

    def pass_on(self, z, slot, a, b, side, target):
        part = self.piece(z, a, b, side)
        send = self.send.at[self.group, z, slot]
        recv = self.recv.at[self.group, z, slot % 8]
        source = self.mine if self.mine is not None and slot in (1, 2, 4) else part
        return remote(source, part, send, recv, target)

    def turn(self, z):
        p = self.place
        odd = self.odd(z)
        a = p.a * odd + (1 - p.a) * (1 - odd)
        b = p.b * (1 - odd) + (1 - p.b) * odd
        target = odd * p.to_a[0] + (1 - odd) * p.to_b[0]
        return self.pass_on(z, 3, a, b, p.core, (target, p.z))

    def hand_out(self, z):
        p = self.place
        self.pass_on(z, 1, p.a, p.b, p.core, p.to_a).start()
        self.pass_on(z, 2, p.a, p.b, p.core, p.to_b).start()
        self.pass_on(z, 4, p.a, p.b, p.core, p.to_core).start()

    def second(self, z):
        p = self.place
        self.pass_on(z, 1, 1 - p.a, p.b, p.core, p.to_a).wait_recv()
        self.pass_on(z, 2, p.a, 1 - p.b, p.core, p.to_b).wait_recv()
        self.turn(z).start()
        self.pass_on(z, 5, 1 - p.a, p.b, p.core, p.to_core).start()
        self.pass_on(z, 6, p.a, 1 - p.b, p.core, p.to_core).start()

    def third(self, z):
        p = self.place
        self.pass_on(z, 3, 1 - p.a, 1 - p.b, p.core, p.to_a).wait_recv()
        self.pass_on(z, 7, 1 - p.a, 1 - p.b, p.core, p.to_core).start()

    def last(self, z):
        p = self.place
        side = 1 - p.core
        self.pass_on(z, 4, p.a, p.b, side, p.to_core).wait_recv()
        self.pass_on(z, 5, 1 - p.a, p.b, side, p.to_core).wait_recv()
        self.pass_on(z, 6, p.a, 1 - p.b, side, p.to_core).wait_recv()
        self.pass_on(z, 7, 1 - p.a, 1 - p.b, side, p.to_core).wait_recv()

    def sent(self, z):
        p = self.place
        self.pass_on(z, 1, p.a, p.b, p.core, p.to_a).wait_send()
        self.pass_on(z, 2, p.a, p.b, p.core, p.to_b).wait_send()
        self.turn(z).wait_send()
        self.pass_on(z, 4, p.a, p.b, p.core, p.to_core).wait_send()
        self.pass_on(z, 5, 1 - p.a, p.b, p.core, p.to_core).wait_send()
        self.pass_on(z, 6, p.a, 1 - p.b, p.core, p.to_core).wait_send()
        self.pass_on(z, 7, 1 - p.a, 1 - p.b, p.core, p.to_core).wait_send()


class Gather(Spread):
    def along(self, z):
        p = self.place
        part = self.piece(p.z, p.a, p.b, p.core)
        send, recv = self.send.at[self.group, z, 0], self.recv.at[self.group, p.z, 0]
        return remote(part, part, send, recv, (p.dp, z))

    def onward(self, z):
        p = self.place
        target = jnp.where(z < p.z, p.z + 1, p.z - 1)
        copy = self.pass_on(z, 8, p.a, p.b, p.core, (p.dp, target))
        return (target >= 0) & (target < p.n_tensor), copy

    def start(self):
        p = self.place
        for z in (p.z - 1, p.z + 1):
            pl.when((z >= 0) & (z < p.n_tensor))(self.along(z).start)

    def first(self, z):
        p = self.place
        self.pass_on(z, 0, p.a, p.b, p.core, p.to_core).wait_recv()
        there, copy = self.onward(z)
        pl.when(there)(copy.start)
        self.hand_out(z)

    def finish(self):
        p = self.place
        for z in (p.z - 1, p.z + 1):
            pl.when((z >= 0) & (z < p.n_tensor))(self.along(z).wait_send)
        for z in p.others:
            there, copy = self.onward(z)
            pl.when(there)(copy.wait_send)
            self.sent(z)


def forward_kernel(
    n_tensor,
    heads,
    scale,
    layer_input,
    own_segments,
    row_segments,
    local_a,
    w_up,
    w_down,
    local_small,
    vectors,
    out_w,
    out_q,
    out_k,
    out_v,
    out_totals,
    out_attended,
    out_activation,
    out_slope,
    small,
    hidden_low,
    xhat,
    inverse,
    second_sum,
    weights,
    row_input,
    bias,
    q_all,
    k_all,
    v_all,
    totals,
    attended,
    activation,
    slope,
    queries,
    keys,
    values,
    mixed,
    send,
    recv,
    small_send,
    small_recv,
    copy_sem,
    save_sem,
):
    place = Place(n_tensor)
    share = own_segments.shape[0]
    length = row_input.shape[0]
    shares_per_row = length // share
    width = row_input.shape[1]
    group_rows = q_all.shape[2]
    size = group_rows // heads
    in_row = pl.ds(pl.multiple_of(lax.rem(place.z, shares_per_row) * share, share), share)
    row_start = pl.multiple_of(place.z // shares_per_row * length, length)
    near, middle, far = place.others

    own = [
        pltpu.make_async_copy(source, weights.at[group, place.z], copy_sem.at[group])
        for group, source in enumerate((local_a, w_up, w_down))
    ]
    load_input = pltpu.make_async_copy(
        layer_input.at[pl.ds(row_start, length)], row_input, copy_sem.at[3]
    )
    for copy in own:
        copy.start()
    load_input.start()
    meet([place.to_core, place.to_a, place.to_b] + [(place.dp, z) for z in place.others])
    gathers = [Gather(place, weights, send, recv, group) for group in range(3)]
    gather_a, gather_b, gather_c = gathers

    def small_copy(z):
        sems = small_send.at[z], small_recv.at[place.z]
        return remote(local_small, small.at[place.z], *sems, (place.dp, z))

    def small_arrival(z):
        return remote(local_small, small.at[z], small_send.at[z], small_recv.at[z], (place.dp, z))

    own[0].wait()
    gather_a.start()
    for z in place.others:
        small_copy(z).start()
    own[1].wait()
    gather_b.start()
    own[2].wait()
    gather_c.start()
    small[place.z] = local_small[...]
    bias[...] = segment_bias(own_segments[...], row_segments[...])
    load_input.wait()

    saves = []

    def save(source, target):
        copy = pltpu.make_async_copy(source, target, save_sem.at[len(saves)])
        copy.start()
        saves.append(copy)

    def attend(z, between):
        weight = weights.at[0, z]
        q_bias = small[z, 0:1, :group_rows]
        v_bias = small[z, 1:2, :group_rows]
        x_row = row_input[...]
        q = dot_nt(row_input[in_row], weight[:group_rows]) + q_bias
        q = q.astype(LOW) * scale
        k = dot_nt(x_row, weight[group_rows : 2 * group_rows]).astype(LOW)
        v = (dot_nt(x_row, weight[2 * group_rows : 3 * group_rows]) + v_bias).astype(LOW)
        q_all[z], k_all[z], v_all[z] = q, k, v
        for head in range(heads):
            part = slice(head * size, (head + 1) * size)
            queries[head], keys[head], values[head] = q[:, part], k[:, part], v[:, part]

        def one_head(head, carry):
            chunk = min(256, share)
            for at in range(0, share, chunk):
                rows = pl.ds(at, chunk)
                scores = dot_nt(queries[head, rows], keys[head]) + bias[rows]
                top = jnp.max(scores, axis=-1, keepdims=True)
                raised = jnp.exp(scores - top)
                total = jnp.sum(raised, axis=-1, keepdims=True)
                summed = dot_nn(raised.astype(LOW), values[head])
                mixed[head, rows] = (summed / total).astype(LOW)
                totals[z, head, rows] = top + jnp.log(total)
            for at, service in enumerate(between):
                pl.when(head == at)(service)
            return carry

        lax.fori_loop(0, heads, one_head, 0)
        attended[z] = jnp.concatenate([mixed[head] for head in range(heads)], axis=-1)
        save(weights.at[0, z], out_w.at[0, z])
        save(q_all.at[z], out_q.at[z])
        save(k_all.at[z], out_k.at[z])
        save(v_all.at[z], out_v.at[z])
        save(totals.at[z], out_totals.at[z])
        save(attended.at[z], out_attended.at[z])

    def services(*steps):
        def run():
            for step, z in steps:
                step(z)

        return run

    attend(place.z, [])
    save(weights.at[1, place.z], out_w.at[1, place.z])
    save(weights.at[2, place.z], out_w.at[2, place.z])
    services(
        (gather_a.first, near),
        (gather_a.first, middle),
        (gather_a.second, near),
        (gather_a.first, far),
        (gather_a.second, middle),
        (gather_a.third, near),
        (gather_b.first, near),
        (gather_a.second, far),
        (gather_a.third, middle),
        (gather_c.first, near),
        (gather_a.third, far),
        (gather_b.second, near),
        (gather_b.first, middle),
        (gather_a.last, near),
    )()
    for z in place.others:
        small_arrival(z).wait_recv()
    attend(
        near,
        [
            services((gather_c.second, near), (gather_c.first, middle)),
            services((gather_b.third, near), (gather_b.second, middle)),
            services((gather_c.third, near), (gather_b.first, far)),
        ],
    )
    gather_a.last(middle)
    attend(
        middle,
        [
            services((gather_c.second, middle), (gather_c.first, far)),
            services((gather_b.third, middle)),
            services((gather_b.second, far)),
        ],
    )
    gather_a.last(far)
    attend(
        far,
        [
            services((gather_c.third, middle)),
            services((gather_c.second, far)),
            services((gather_b.third, far)),
        ],
    )

    out_bias, gain, shift, down_bias = (vectors[at : at + 1] for at in range(4))
    first_sum = row_input[in_row].astype(HIGH) + out_bias
    for z in range(n_tensor):
        first_sum = first_sum + dot_nn(attended[z], weights[0, z, 3 * group_rows :])
    normed, spread = norm_forward(first_sum)
    xhat[...] = normed
    inverse[...] = spread
    hidden = normed * gain + shift
    hidden_low[...] = hidden.astype(LOW)
    second_sum[...] = hidden + down_bias

    order = [place.z] + place.others

    def one_shard(at, carry):
        z = place.pick(at, order)

        @pl.when(at > 0)
        def _():
            pl.when(at == 1)(services((gather_c.third, far)))
            gather_b.last(z)
            gather_c.last(z)

        raw = dot_nn(hidden_low[...], weights[1, z]) + small[z, 2:3]
        value, rise = gelu_parts(raw)
        activation[z] = value.astype(LOW)
        slope[z] = rise.astype(LOW)
        second_sum[...] += dot_nn(activation[z], weights[2, z])
        return carry

    lax.fori_loop(0, n_tensor, one_shard, 0)
    for z in place.others:
        save(weights.at[1, z], out_w.at[1, z])
        save(weights.at[2, z], out_w.at[2, z])
    save(activation, out_activation)
    save(slope, out_slope)
    for z in place.others:
        small_copy(z).wait_send()
    for gather in gathers:
        gather.finish()
    for copy in saves:
        copy.wait()


class Reduce:
    def __init__(self, place, grads, lands, pieces, send, recv, wide, group):
        self.place, self.grads, self.pieces = place, grads, pieces
        self.wide_flips, self.wide_out, self.wide_land, self.wide_send, self.wide_recv = wide
        self.core_land, self.first_land, self.second_land, self.far_land = lands
        self.send, self.recv, self.group = send, recv, group
        self.half = grads.shape[2] // 2
        self.quarter = grads.shape[2] // 4
        self.side = grads.shape[3] // 2

    def columns(self, side):
        return pl.ds(pl.multiple_of(side * self.side, 128), self.side)

    def axes(self, z):
        p = self.place
        odd = lax.rem(z + self.group, 2)
        ahead, behind = odd * p.b + (1 - odd) * p.a, odd * p.a + (1 - odd) * p.b
        to_first = odd * p.to_b[0] + (1 - odd) * p.to_a[0]
        to_second = odd * p.to_a[0] + (1 - odd) * p.to_b[0]
        return ahead, behind, (to_first, p.z), (to_second, p.z)

    def rows(self, start, size):
        return pl.ds(pl.multiple_of(start, 16), size)

    def copy(self, z, slot, source, target_ref, target):
        send, recv = self.send.at[self.group, z, slot], self.recv.at[self.group, z, slot]
        return remote(source, target_ref, send, recv, target)

    def core_copy(self, z):
        p, group = self.place, self.group
        source = self.grads.at[group, z, :, self.columns(1 - p.core)]
        return self.copy(z, 0, source, self.core_land.at[group, z], p.to_core)

    def first_copy(self, z):
        ahead, _, target, _ = self.axes(z)
        source = self.core_land.at[self.group, z, self.rows((1 - ahead) * self.half, self.half)]
        return self.copy(z, 1, source, self.first_land.at[self.group, z], target)

    def second_copy(self, z):
        ahead, behind, _, target = self.axes(z)
        start = ahead * self.half + (1 - behind) * self.quarter
        source = self.core_land.at[self.group, z, self.rows(start, self.quarter)]
        return self.copy(z, 2, source, self.second_land.at[self.group, z], target)

    def kept(self, z):
        ahead, behind, _, _ = self.axes(z)
        return self.rows(ahead * self.half + behind * self.quarter, self.quarter)

    def far_copy(self, z):
        p, group = self.place, self.group
        source = self.core_land.at[group, z, self.kept(z)]
        send, recv = self.send.at[group, z, 3], self.recv.at[group, p.z, 3]
        return remote(source, self.far_land.at[group, p.z], send, recv, (p.dp, z))

    def far_arrival(self, z):
        p, group = self.place, self.group
        land = self.far_land.at[group, z]
        return remote(land, land, self.send.at[group, z, 3], self.recv.at[group, z, 3], (p.dp, z))

    def wide_copy(self, at):
        group = self.group
        sems = self.wide_send.at[group, at], self.wide_recv.at[group, at]
        target = (self.wide_flips[at], self.place.z)
        return remote(self.wide_out.at[group, at], self.wide_land.at[group, at], *sems, target)

    def start(self, z):
        self.core_copy(z).start()

    def add(self, target, rows, other):
        target[rows] = (target[rows].astype(HIGH) + other.astype(HIGH)).astype(LOW)

    def first(self, z):
        p = self.place
        self.core_copy(z).wait_recv()
        mine = self.grads[self.group, z, :, self.columns(p.core)]
        land = self.core_land.at[self.group, z]
        self.add(land, slice(None), mine)
        self.first_copy(z).start()

    def second(self, z):
        ahead, _, _, _ = self.axes(z)
        self.first_copy(z).wait_recv()
        land = self.core_land.at[self.group, z]
        self.add(land, self.rows(ahead * self.half, self.half), self.first_land[self.group, z])
        self.second_copy(z).start()

    def third(self, z):
        self.second_copy(z).wait_recv()
        land = self.core_land.at[self.group, z]
        self.add(land, self.kept(z), self.second_land[self.group, z])
        pl.when(z != self.place.z)(self.far_copy(z).start)

    def fourth(self):
        p = self.place
        total = self.core_land[self.group, p.z, self.kept(p.z)].astype(HIGH)
        for z in p.others:
            self.far_arrival(z).wait_recv()
            total = total + self.far_land[self.group, z].astype(HIGH)
        for at in range(len(self.wide_flips)):
            self.wide_out[self.group, at] = total.astype(LOW)
            copy = self.wide_copy(at)
            copy.start()
            copy.wait_recv()
            total = self.wide_out[self.group, at].astype(HIGH) + self.wide_land[self.group, at].astype(HIGH)
        self.pieces[self.group] = total.astype(LOW)

    def finish(self):
        p = self.place
        for z in [p.z] + p.others:
            self.core_copy(z).wait_send()
            self.first_copy(z).wait_send()
            self.second_copy(z).wait_send()
        for z in p.others:
            self.far_copy(z).wait_send()
        for at in range(len(self.wide_flips)):
            self.wide_copy(at).wait_send()


class Return(Spread):
    def __init__(self, place, whole, pieces, send, recv, keep_sem, group):
        super().__init__(place, whole, send, recv, group)
        self.mine = pieces.at[group]
        p = place
        self.keep = pltpu.make_async_copy(self.mine, self.piece(0, p.a, p.b, p.core), keep_sem.at[group])

    def hand_out(self, z):
        super().hand_out(z)
        self.keep.start()

    def sent(self, z):
        super().sent(z)
        self.keep.wait()

    def odd(self, z):
        return lax.rem(self.place.z + self.group, 2)


def backward_kernel(
    n_tensor,
    heads,
    scale,
    layer_input,
    own_segments,
    row_segments,
    vectors,
    in_cotangent,
    in_w,
    in_q,
    in_k,
    in_v,
    in_totals,
    in_attended,
    in_activation,
    in_slope,
    in_hidden,
    in_xhat,
    in_inverse,
    in_second,
    out_layer,
    out_partial,
    out_landed,
    out_summed,
    out_sums,
    weights,
    core_land,
    first_land,
    second_land,
    far_land,
    pieces,
    activation,
    slope,
    row_input,
    bias,
    q_all,
    k_all,
    v_all,
    totals,
    attended,
    queries,
    keys,
    values,
    grad_mixed,
    grad_k,
    grad_v,
    inverse,
    terms,
    hidden_low,
    grad_low,
    spare,
    landed,
    sums,
    sums_land,
    sums_far,
    send,
    recv,
    final_send,
    final_recv,
    wide_out,
    wide_land,
    wide_send,
    wide_recv,
    load_sem,
    weight_sem,
    stream_sem,
    term_send,
    term_recv,
    sums_send,
    sums_recv,
    save_sem,
    keep_sem,
):
    place = Place(n_tensor)
    share = own_segments.shape[0]
    length = row_input.shape[0]
    shares_per_row = length // share
    group_rows = q_all.shape[2]
    size = group_rows // heads
    my_share = lax.rem(place.z, shares_per_row)
    in_row = pl.ds(pl.multiple_of(my_share * share, share), share)
    row_start = pl.multiple_of(place.z // shares_per_row * length, length)
    order = list(reversed(place.others)) + [place.z]
    bits = sums_land.shape[0]
    flips = [place.dp + (1 << bit) - (2 << bit) * lax.rem(place.dp // (1 << bit), 2) for bit in range(bits)]

    accum, xhat = terms.at[0], terms.at[1]

    def load(source, target, at):
        copy = pltpu.make_async_copy(source, target, load_sem.at[at])
        copy.start()
        return copy

    def weight_load(group, z):
        return pltpu.make_async_copy(in_w.at[group, z], weights.at[group, z], weight_sem.at[group, z])

    def stream(at, sources, first_sem):
        z, slot = place.pick(at, order), lax.rem(at, 2)
        return [
            pltpu.make_async_copy(source.at[z], target.at[slot], stream_sem.at[first_sem + index, slot])
            for index, (source, target) in enumerate(sources)
        ]

    ffn_streams = [(in_activation, activation), (in_slope, slope)]
    head_streams = [
        (in_q, q_all),
        (in_k, k_all),
        (in_v, v_all),
        (in_totals, totals),
        (in_attended, attended),
    ]

    early = [
        load(source, target, at)
        for at, (source, target) in enumerate(
            [(in_second, accum), (in_cotangent, spare.at[0]), (in_xhat, xhat), (in_inverse, inverse), (in_hidden, hidden_low)]
        )
    ]
    for copy in stream(0, ffn_streams, 0):
        copy.start()
    for z in order:
        weight_load(2, z).start()
        weight_load(1, z).start()
    late = load(layer_input.at[pl.ds(row_start, length)], row_input, 5)
    for z in order:
        weight_load(0, z).start()
    for copy in stream(0, head_streams, 2):
        copy.start()
    meet([(flip, place.z) for flip in flips] + [(place.dp, z) for z in place.others])
    lands = (core_land, first_land, second_land, far_land)
    wide = (flips[3:], wide_out, wide_land, wide_send, wide_recv)
    reduces = [Reduce(place, weights, lands, pieces, send, recv, wide, group) for group in range(3)]
    returns = [
        Return(place, out_summed, pieces, final_send, final_recv, keep_sem, group) for group in range(3)
    ]
    reduce_a, reduce_b, reduce_c = reduces
    sums[0] = jnp.zeros(sums.shape[1:], HIGH)
    bias[...] = segment_bias(own_segments[...], row_segments[...])
    gain_first, gain_second, shift_second = vectors[1:2], vectors[4:5], vectors[5:6]

    for copy in early:
        copy.wait()
    band = min(128, share)

    def second_norm(at, carry):
        rows = pl.ds(pl.multiple_of(at * band, band), band)
        normed, spread = norm_forward(accum[rows])
        live = (own_segments[rows] >= 0).astype(HIGH)
        cotangent = spare[0, rows].astype(HIGH) * live
        spare[0, rows] = (normed * gain_second + shift_second).astype(LOW)
        grad_second = norm_backward(normed, spread, cotangent * gain_second)
        sums[0, n_tensor, 4:5] += column_sum(cotangent * normed)
        sums[0, n_tensor, 5:6] += column_sum(cotangent)
        sums[0, n_tensor, 3:4] += column_sum(grad_second)
        grad_low[rows] = grad_second.astype(LOW)
        accum[rows] = grad_second
        return carry

    lax.fori_loop(0, share // band, second_norm, 0)
    save_layer = pltpu.make_async_copy(spare.at[0], out_layer, save_sem.at[0])
    save_layer.start()

    def feed_forward(at, carry):
        z, slot = place.pick(at, order), lax.rem(at, 2)
        before = place.pick(at - 1, order)

        @pl.when(at + 1 < n_tensor)
        def _():
            for copy in stream(at + 1, ffn_streams, 0):
                copy.start()

        for copy in stream(at, ffn_streams, 0):
            copy.wait()
        weight_load(2, z).wait()
        low = grad_low[...]
        grad_up = (dot_nt(low, weights[2, z]) * slope[slot].astype(HIGH)).astype(LOW)
        weights[2, z] = dot_tn(activation[slot], low).astype(LOW)
        reduce_c.start(z)
        pl.when(at >= 1)(functools.partial(reduce_b.first, before))
        pl.when(at >= 3)(functools.partial(reduce_b.second, order[0]))
        weight_load(1, z).wait()
        accum[...] += dot_nt(grad_up, weights[1, z])
        weights[1, z] = dot_tn(hidden_low[...], grad_up).astype(LOW)
        reduce_b.start(z)
        sums[0, z, 2:3] = column_sum(grad_up.astype(HIGH))
        reduce_c.first(z)
        pl.when(at == 2)(functools.partial(reduce_c.second, order[0]))
        return carry

    lax.fori_loop(0, n_tensor, feed_forward, 0)

    def first_norm(at, carry):
        rows = pl.ds(pl.multiple_of(at * band, band), band)
        grad_hidden, normed = accum[rows], xhat[rows]
        grad_first = norm_backward(normed, inverse[rows], grad_hidden * gain_first)
        sums[0, n_tensor, 0:1] += column_sum(grad_first)
        sums[0, n_tensor, 1:2] += column_sum(grad_hidden * normed)
        sums[0, n_tensor, 2:3] += column_sum(grad_hidden)
        accum[rows] = grad_first
        grad_low[rows] = grad_first.astype(LOW)
        return carry

    lax.fori_loop(0, share // band, first_norm, 0)
    for index in range(shares_per_row):
        terms[1 + index] = jnp.zeros(accum.shape, HIGH)
    reduce_b.first(order[-1])
    late.wait()

    def attend(at, carry):
        z, slot = place.pick(at, order), lax.rem(at, 2)
        after = place.pick(at + 1, order)
        before, earlier = place.pick(at - 1, order), place.pick(at - 2, order)

        @pl.when(at + 1 < n_tensor)
        def _():
            for copy in stream(at + 1, head_streams, 2):
                copy.start()

        for copy in stream(at, head_streams, 2):
            copy.wait()
        weight_load(0, z).wait()
        incoming = dot_nt(grad_low[...], weights[0, z, 3 * group_rows :]).astype(LOW)
        weights[0, z, 3 * group_rows :] = dot_tn(attended[slot], grad_low[...]).astype(LOW)
        for head in range(heads):
            part = slice(head * size, (head + 1) * size)
            queries[head], keys[head] = q_all[slot, :, part], k_all[slot, :, part]
            values[head], grad_mixed[head] = v_all[slot, :, part], incoming[:, part]
        pl.when(at >= 1)(functools.partial(reduce_a.first, before))

        def one_head(head, inner):
            k, v = keys[head], values[head]
            grad_kt = jnp.zeros((size, length), HIGH)
            grad_vt = jnp.zeros((size, length), HIGH)
            chunk = min(256, share)
            for start in range(0, share, chunk):
                rows = pl.ds(start, chunk)
                q, up = queries[head, rows], grad_mixed[head, rows]
                chance = jnp.exp(dot_nt(q, k) + bias[rows] - totals[slot, head, rows])
                change = chance * dot_nt(up, v)
                change = change - chance * jnp.sum(change, axis=-1, keepdims=True)
                change = change.astype(LOW)
                grad_kt = grad_kt + dot_nn(q.T, change)
                grad_vt = grad_vt + dot_nn(up.T, chance.astype(LOW))
                grad_mixed[head, rows] = (dot_nn(change, k) * scale).astype(LOW)
            grad_k[head] = grad_kt.astype(LOW)
            grad_v[head] = grad_vt.astype(LOW)

            @pl.when(head == 0)
            def _():
                reduce_c.third(z)
                pl.when(at + 1 < n_tensor)(functools.partial(reduce_c.second, after))

            pl.when(head == 1)(functools.partial(reduce_b.third, z))

            @pl.when(head == 2)
            def _():
                pl.when(at + 1 < n_tensor)(functools.partial(reduce_b.second, after))
                pl.when(at >= 3)(functools.partial(reduce_a.third, order[0]))
                pl.when(at >= 2)(functools.partial(reduce_a.second, earlier))

            return inner

        lax.fori_loop(0, heads, one_head, 0)
        dq = jnp.concatenate([grad_mixed[head] for head in range(heads)], axis=-1)
        dk = grad_k[...].reshape(group_rows, length)
        dv = grad_v[...].reshape(group_rows, length)
        x_row = row_input[...]
        accum[...] += dot_nn(dq, weights[0, z, :group_rows])
        row_term = dot_tn(jnp.concatenate([dk, dv], axis=0), weights[0, z, group_rows : 3 * group_rows])
        for index in range(shares_per_row):
            terms[1 + index] += row_term[index * share : (index + 1) * share]
        weights[0, z, :group_rows] = dot_tn(dq, row_input[in_row]).astype(LOW)
        weights[0, z, group_rows : 2 * group_rows] = dot_nn(dk, x_row).astype(LOW)
        weights[0, z, 2 * group_rows : 3 * group_rows] = dot_nn(dv, x_row).astype(LOW)
        reduce_a.start(z)
        ones = jnp.ones((8, length), LOW)
        sums[0, z, 0:1, :group_rows] = dot_nn(ones[:, :share], dq)[0:1]
        sums[0, z, 1:2, :group_rows] = dot_nt(ones, dv)[0:1]
        return carry

    lax.fori_loop(0, n_tensor, attend, 0)

    save_layer.wait()
    term_copies = []
    for step in range(1, shares_per_row):
        other = lax.rem(my_share + step, shares_per_row)
        spare[step - 1] = terms[1 + other].astype(LOW)
        partner = place.z - my_share + other
        copy = remote(
            spare.at[step - 1], landed.at[step - 1], term_send.at[step - 1], term_recv.at[step - 1], (place.dp, partner)
        )
        copy.start()
        term_copies.append(copy)
    accum[...] += terms[1 + my_share]
    save_partial = pltpu.make_async_copy(accum, out_partial, save_sem.at[1])
    save_partial.start()

    def sum_copy(bit):
        return remote(
            sums.at[bit], sums_land.at[bit], sums_send.at[bit], sums_recv.at[bit], (flips[bit], place.z)
        )

    def fold(bit):
        sum_copy(bit).wait_recv()
        sums[bit + 1] = sums[bit] + sums_land[bit]

    def far_sum(z):
        sems = sums_send.at[bits + z], sums_recv.at[bits + place.z]
        return remote(sums.at[bits], sums_far.at[place.z], *sems, (place.dp, z))

    def far_sum_arrival(z):
        sems = sums_send.at[bits + z], sums_recv.at[bits + z]
        return remote(sums.at[bits], sums_far.at[z], *sems, (place.dp, z))

    return_a, return_b, return_c = returns
    sum_copy(0).start()
    reduce_c.fourth()
    return_c.hand_out(0)
    reduce_b.fourth()
    return_b.hand_out(0)
    reduce_a.first(order[3])
    reduce_a.second(order[2])
    reduce_a.third(order[1])
    fold(0)
    sum_copy(1).start()
    return_c.second(0)
    return_b.second(0)
    reduce_a.second(order[3])
    reduce_a.third(order[2])
    fold(1)
    sum_copy(2).start()
    return_c.third(0)
    return_b.third(0)
    reduce_a.third(order[3])
    reduce_a.fourth()
    return_a.hand_out(0)
    for bit in range(2, bits):
        fold(bit)
        if bit + 1 < bits:
            sum_copy(bit + 1).start()
    for z in place.others:
        far_sum(z).start()
    sums_far[place.z] = sums[bits]
    return_c.last(0)
    return_b.last(0)
    return_a.second(0)
    for copy in term_copies:
        copy.wait_recv()
    save_landed = pltpu.make_async_copy(landed, out_landed, save_sem.at[5])
    save_landed.start()
    return_a.third(0)
    for z in place.others:
        far_sum_arrival(z).wait_recv()
    total = sums_far[0]
    for z in range(1, n_tensor):
        total = total + sums_far[z]
    out_sums[...] = total
    return_a.last(0)
    save_partial.wait()
    save_landed.wait()
    for copy in term_copies:
        copy.wait_send()
    for bit in range(bits):
        sum_copy(bit).wait_send()
    for z in place.others:
        far_sum(z).wait_send()
    for reduce in reduces:
        reduce.finish()
    for part in returns:
        part.sent(0)


def on_device(
    layer_input,
    segment_ids,
    w_qkv,
    qv_bias,
    w_out,
    out_bias,
    norm1_gain,
    norm1_bias,
    w_up,
    up_bias,
    w_down,
    down_bias,
    norm2_gain,
    norm2_bias,
    out_cotangent,
):
    n_tensor = lax.axis_size("tensor")
    place = lax.axis_index("tensor")
    n_dp = lax.axis_size("dp")
    bits = n_dp.bit_length() - 1
    tokens, width = layer_input.shape
    share = tokens // n_tensor
    heads = qv_bias.shape[0]
    head_dim = qv_bias.shape[1] // 2
    score_scale = float(head_dim) ** (-0.5)
    shares_per_row = SEQ // share
    group_rows = heads * head_dim

    local_a = w_qkv.reshape(width, heads, 3, head_dim).transpose(2, 1, 3, 0).reshape(-1, width)
    local_a = jnp.concatenate([local_a, w_out], axis=0)
    local_small = jnp.concatenate(
        [
            jnp.pad(qv_bias[:, :head_dim].reshape(1, -1), ((0, 0), (0, width - group_rows))),
            jnp.pad(qv_bias[:, head_dim:].reshape(1, -1), ((0, 0), (0, width - group_rows))),
            up_bias.reshape(1, -1),
            jnp.zeros((5, width), LOW),
        ]
    ).astype(HIGH)
    vectors = jnp.stack(
        [out_bias, norm1_gain, norm1_bias, down_bias, norm2_gain, norm2_bias, out_bias, out_bias]
    ).astype(HIGH)
    row_start = (place // shares_per_row) * SEQ
    own_segments = lax.dynamic_slice_in_dim(segment_ids, place * share, share, 0)[:, None]
    row_segments = lax.dynamic_slice_in_dim(segment_ids, row_start, SEQ, 0)[None, :]

    vmem = pl.BlockSpec(memory_space=pltpu.VMEM)
    anywhere = pl.BlockSpec(memory_space=pl.ANY)

    def low(*shape):
        return jax.ShapeDtypeStruct(shape, LOW)

    def high(*shape):
        return jax.ShapeDtypeStruct(shape, HIGH)

    def low_scratch(*shape):
        return pltpu.VMEM(shape, LOW)

    def high_scratch(*shape):
        return pltpu.VMEM(shape, HIGH)

    dma = pltpu.SemaphoreType.DMA
    whole = (3, n_tensor, width, width)
    (w, q, k, v, totals, attended, activation, slope, small, hidden, xhat, inverse, second_sum) = pl.pallas_call(
        functools.partial(forward_kernel, n_tensor, heads, score_scale),
        out_shape=(
            low(*whole),
            low(n_tensor, share, group_rows),
            low(n_tensor, SEQ, group_rows),
            low(n_tensor, SEQ, group_rows),
            high(n_tensor, heads, share, 1),
            low(n_tensor, share, group_rows),
            low(n_tensor, share, width),
            low(n_tensor, share, width),
            high(n_tensor, 8, width),
            low(share, width),
            high(share, width),
            high(share, 1),
            high(share, width),
        ),
        in_specs=[anywhere, vmem, vmem, anywhere, anywhere, anywhere, vmem, vmem],
        out_specs=(anywhere,) * 8 + (vmem,) * 5,
        scratch_shapes=[
            low_scratch(*whole),
            low_scratch(SEQ, width),
            high_scratch(share, SEQ),
            low_scratch(n_tensor, share, group_rows),
            low_scratch(n_tensor, SEQ, group_rows),
            low_scratch(n_tensor, SEQ, group_rows),
            high_scratch(n_tensor, heads, share, 1),
            low_scratch(n_tensor, share, group_rows),
            low_scratch(n_tensor, share, width),
            low_scratch(n_tensor, share, width),
            low_scratch(heads, share, head_dim),
            low_scratch(heads, SEQ, head_dim),
            low_scratch(heads, SEQ, head_dim),
            low_scratch(heads, share, head_dim),
            dma((3, n_tensor, 9)),
            dma((3, n_tensor, 8)),
            dma((n_tensor,)),
            dma((n_tensor,)),
            dma((4,)),
            dma((40,)),
        ],
        compiler_params=pltpu.CompilerParams(
            collective_id=0, has_side_effects=True, vmem_limit_bytes=VMEM_LIMIT
        ),
        name="forward",
    )(layer_input, own_segments, row_segments, local_a, w_up, w_down, local_small, vectors)

    half, side = width // 2, width // 2
    quarter = width // 4
    wide = max(bits - 3, 1)
    layer_output, partial, landed, summed, sums = pl.pallas_call(
        functools.partial(backward_kernel, n_tensor, heads, score_scale),
        out_shape=(
            low(share, width),
            high(share, width),
            low(shares_per_row - 1, share, width),
            low(3, 1, width, width),
            high(n_tensor + 1, 8, width),
        ),
        in_specs=[anywhere, vmem, vmem, vmem] + [anywhere] * 13,
        out_specs=(anywhere,) * 4 + (vmem,),
        scratch_shapes=[
            low_scratch(*whole),
            low_scratch(3, n_tensor, width, side),
            low_scratch(3, n_tensor, half, side),
            low_scratch(3, n_tensor, quarter, side),
            low_scratch(3, n_tensor, quarter, side),
            low_scratch(3, quarter, side),
            low_scratch(2, share, width),
            low_scratch(2, share, width),
            low_scratch(SEQ, width),
            high_scratch(share, SEQ),
            low_scratch(2, share, group_rows),
            low_scratch(2, SEQ, group_rows),
            low_scratch(2, SEQ, group_rows),
            high_scratch(2, heads, share, 1),
            low_scratch(2, share, group_rows),
            low_scratch(heads, share, head_dim),
            low_scratch(heads, SEQ, head_dim),
            low_scratch(heads, SEQ, head_dim),
            low_scratch(heads, share, head_dim),
            low_scratch(heads, head_dim, SEQ),
            low_scratch(heads, head_dim, SEQ),
            high_scratch(share, 1),
            high_scratch(1 + shares_per_row, share, width),
            low_scratch(share, width),
            low_scratch(share, width),
            low_scratch(shares_per_row - 1, share, width),
            low_scratch(shares_per_row - 1, share, width),
            high_scratch(bits + 1, n_tensor + 1, 8, width),
            high_scratch(bits, n_tensor + 1, 8, width),
            high_scratch(n_tensor, n_tensor + 1, 8, width),
            dma((3, n_tensor, 4)),
            dma((3, n_tensor, 4)),
            dma((3, 1, 9)),
            dma((3, 1, 8)),
            low_scratch(3, wide, quarter, side),
            low_scratch(3, wide, quarter, side),
            dma((3, wide)),
            dma((3, wide)),
            dma((8,)),
            dma((3, n_tensor)),
            dma((7, 2)),
            dma((shares_per_row - 1,)),
            dma((shares_per_row - 1,)),
            dma((bits + n_tensor,)),
            dma((bits + n_tensor,)),
            dma((6,)),
            dma((3,)),
        ],
        compiler_params=pltpu.CompilerParams(
            collective_id=1, has_side_effects=True, vmem_limit_bytes=VMEM_LIMIT
        ),
        name="backward",
    )(
        layer_input,
        own_segments,
        row_segments,
        vectors,
        out_cotangent,
        w,
        q,
        k,
        v,
        totals,
        attended,
        activation,
        slope,
        hidden,
        xhat,
        inverse,
        second_sum,
    )

    input_grad = partial
    for step in range(shares_per_row - 1):
        input_grad = input_grad + landed[step].astype(HIGH)
    summed = summed[:, 0].astype(HIGH)
    grad_qkv = summed[0, : 3 * group_rows].reshape(3, heads, head_dim, width).transpose(3, 1, 0, 2)
    mine = lax.dynamic_slice_in_dim(sums, place, 1, 0)[0]
    every = sums[n_tensor]
    grad_qv_bias = jnp.concatenate(
        [mine[at, :group_rows].reshape(heads, head_dim) for at in range(2)], axis=1
    )
    return (
        layer_output,
        input_grad,
        grad_qkv.reshape(width, heads, 3 * head_dim),
        grad_qv_bias,
        summed[0, 3 * group_rows :],
        every[0],
        every[1],
        every[2],
        summed[1],
        mine[2],
        summed[2],
        every[3],
        every[4],
        every[5],
    )


def solution(mesh):
    return jax.shard_map(
        on_device,
        mesh=mesh,
        in_specs=(
            P("dp", None),
            P("dp"),
            P(None, "tensor", None),
            P("tensor", None),
            P("tensor", None),
            P(),
            P(),
            P(),
            P(None, "tensor"),
            P("tensor"),
            P("tensor", None),
            P(),
            P(),
            P(),
            P(("dp", "tensor"), None),
        ),
        out_specs=(
            P(("dp", "tensor"), None),
            P(("dp", "tensor"), None),
            P(None, "tensor", None),
            P("tensor", None),
            P("tensor", None),
            P(),
            P(),
            P(),
            P(None, "tensor"),
            P("tensor"),
            P("tensor", None),
            P(),
            P(),
            P(),
        ),
        check_vma=False,
    )
```

time: 559 us -> 221 us (0.40); the launches traced: 549 us -> 221 us
  waiting for transfers between devices: 226 us -> 0 us
  Pallas kernels: 0 us -> 194 us
  matrix products: 187 us -> 0 us
  blocking collectives: 56.9 us -> 0 us
  local copies, waits for them, and re-layouts: 39.4 us -> 18.5 us
  other arithmetic: 24.1 us -> 7.16 us
  between operations: 14.9 us -> 0.75 us
    pallas_call x0 -> x2, Pallas kernels: none -> 194 us  [the longest x1 114 us: on_device(): pl.pallas_call(functools.partial(backward_kernel, n_tensor, heads, score_...]
    dot_general x24 -> x0, matrix products: 187 us -> none  [the longest x1 46.5 us: on_device(): jnp.einsum('hqk,qhd->khd', grad_raw, queries, preferred_element_type=HIGH)]
    reduce_scatter x2 -> x0, waiting for transfers between devices: 139 us -> none  [the longest x1 99 us: on_device(): lax.psum_scatter(gradients.reshape(-1, width), 'dp', scatter_dimension=0,...]
    all_gather x2 -> x0, waiting for transfers between devices: 86.1 us -> none  [the longest x1 86.1 us: on_device(): everything = lax.all_gather(mine, ('tensor', 'dp'), axis=0, tiled=True)]
    psum x1 -> x0, blocking collectives: 42 us -> none  [on_device(): lax.psum((jnp.sum(grad_queries.astype(HIGH), axis=0).reshape(heads, head_...]
    reduce_sum x6 -> x0, other arithmetic: 15.7 us -> none  [the longest x1 12.1 us: on_device(): total = jnp.sum(jnp.exp(scores - top), axis=-1, keepdims=True)]
    all_gather x1 -> x0, blocking collectives: 14.8 us -> none  [on_device(): small = lax.all_gather(small, 'tensor', axis=0, tiled=False)]
    slice x6 -> x4, local copies, waits for them, and re-layouts: 16.1 us -> 2.64 us  [the longest x1 1.68 us: on_device(): every[5]]
  transfers between devices with their start and end apart: 5 -> 0, of which waited for: 3 -> 0; matrix products, arithmetic and copies ran while one was open for 3% -> 0% of each run, Pallas kernels for 0% -> 0%
where the time goes in v3:
time: 221 us
  Pallas kernels  194 us (88%)
  local copies, waits for them, and re-layouts  18.5 us (8%)
  other arithmetic  7.16 us (3%)
    pallas_call x1, Pallas kernels, on_device(): pl.pallas_call(functools.partial(backward_kernel, n_tensor, heads, score_...  114 us
    pallas_call x1, Pallas kernels, on_device(): pl.pallas_call(functools.partial(forward_kernel, n_tensor, heads, score_s...  80.6 us

profile of v3, /device:TPU:0, one launch (start us, length us, event | category | flops | bytes accessed | tf_op | source)
XLA Modules:
  0.0 220.9 jit_solution(1579989474990414049)
XLA Ops:
  0.6 0.0 copy-start.2
  0.7 0.1 pad.14.clone
  0.8 0.8 dynamic_slice.9
  1.5 0.8 fusion.8
  2.3 0.1 reshape.69
  2.4 0.1 reshape.70
  2.5 0.7 stack.23
  3.2 0.7 stack.24
  3.9 0.7 stack.25
  4.6 0.7 reshape.71
  5.3 0.7 stack.26
  5.9 0.7 stack.27
  6.6 0.7 stack.28
  7.4 1.3 dynamic_slice.10
  8.6 0.6 convert_element_type.21.vectors
  9.3 0.7 fusion.6.local_small
  9.9 0.9 copy.33.own_segments
  10.8 1.2 copy.31
  12.0 0.0 copy-done.2
  12.0 1.1 pad_maximum_fusion.local_a
  13.1 80.6 %forward.1 = (bf16[3,4,768,768]{3,2,1,0:T(8,128)(2,1)}, bf16[4,512,192]{2,1,0:T(8,128)(2,1)}, bf16[4,1024,192]{2,1,0:T(8,128)(2,1)}, bf16[4,1024,192]{2,1,0:T(8,...) custom-call(bf16[2048,768]{1,0:T(8,128)(2,1)} %layer_input.3, ...), custom_call_target="tpu_custom_call" | custom-call | tf_op jit(solution)/shard_map/forward/pallas_call | solution.py:1015
  93.7 113.9 %backward.1 = (bf16[512,768]{1,0:T(8,128)(2,1)}, f32[512,768]{1,0:T(8,128)}, bf16[1,512,768]{2,1,0:T(8,128)(2,1)}, bf16[3,1,768,768]{3,2,1,0:T(8,128)(2,1)}, f32[5,8,768]{2,1,0:T(8,128)}) custom-call(bf16[2048,768]{1,0:T(8,128)(2,1)} %layer_input.3, s32[512,1]{1,0:T(8,128)} %copy.33.own_segments, s32[1,1024]{1,0:T(1,128)} %bitcast.28, ...), custom_call_target="tpu_custom_call" | custom-call | tf_op jit(solution)/shard_map/backward/pallas_call | solution.py:1065
  207.6 0.0 copy-start
  207.6 0.9 dynamic-slice_bitcast_fusion
  208.5 1.7 slice_reduce_fusion
  210.2 0.1 reshape_squeeze.10
  210.3 0.1 reshape_squeeze.11
  210.4 0.7 pad_maximum_fusion.1
  211.0 2.9 %convert_add_fusion = f32[512,768]{1,0:T(8,128)} fusion(f32[512,768]{1,0:T(8,128)} %get-tuple-element.44, bf16[1,512,768]{2,1,0:T(8,128)(2,1)} %get-tuple-element.45), kind=kLoop, calls=%fused_computation.3 | loop fusion | flops 786432 | bytes 3932160 | tf_op jit(solution)/shard_map/add | solution.py:1151
  213.9 0.0 copy-done
  213.9 1.2 fusion.7
  215.2 2.5 %slice_bitcast_fusion = (f32[768,768]{1,0:T(8,128)}, f32[768,768]{1,0:T(8,128)}) fusion(f32[3,1,768,768]{3,2,1,0:T(8,128)S(1)} %get-tuple-element.59), kind=kLoop, calls=%fused_computation | loop fusion | bytes 9437184 | tf_op jit(solution)/shard_map/squeeze | solution.py:1170
  217.7 0.9 slice_bitcast_fusion.2
  218.5 0.1 slice.76
  218.6 0.0 copy-start.1
  218.6 1.3 copy.34
  220.0 0.0 copy-done.1
  220.0 0.9 copy.36
  (3 shorter events, 0.1 us)
Async XLA Ops:
  0.6 11.4 %copy-start.2 = (bf16[192,768]{1,0:T(8,128)(2,1)S(1)}, bf16[192,768]{1,0:T(8,128)(2,1)}, u32[]{:S(2)}) copy-start(bf16[192,768]{1,0:T(8,128)(2,1)} %param.19) | copy-start | bytes 884740
  207.6 6.3 %copy-start = (bf16[3,1,768,768]{3,2,1,0:T(8,128)(2,1)S(1)}, bf16[3,1,768,768]{3,2,1,0:T(8,128)(2,1)}, u32[]{:S(2)}) copy-start(bf16[3,1,768,768]{3,2,1,0:T(8,128)(2,1)} %get-tuple-element.46) | copy-start | bytes 10616836
  218.6 1.4 copy-start.1

commit v4 on v3

--- a/solution.py
+++ b/solution.py
@@ -15,7 +15,7 @@
 LOW = jnp.bfloat16
 HIGH = jnp.float32
 MESH = pl.DeviceIdType.MESH
-VMEM_LIMIT = 60 * 1024 * 1024
+VMEM_LIMIT = 62 * 1024 * 1024
 
 
 def dot_nn(left, right):
@@ -54,6 +54,19 @@
 
 def column_sum(values):
     return jnp.sum(values, axis=0, keepdims=True)
+
+
+def as_row(vector):
+    return vector[...].astype(HIGH).reshape(1, -1)
+
+
+def as_column(row):
+    return jnp.broadcast_to(row, (8, row.shape[1])).T[:, :1]
+
+
+def segment_rows(segment_ids, own_start, share, row_start, length):
+    own = segment_ids[pl.ds(own_start, share)].astype(HIGH).reshape(1, share)
+    return as_column(own), segment_ids[pl.ds(row_start, length)].astype(HIGH).reshape(1, length)
 
 
 def segment_bias(own_segments, row_segments):
@@ -103,10 +116,11 @@
 
 
 class Spread:
-    def __init__(self, place, whole, send, recv, group):
+    def __init__(self, place, whole, send, recv, group, block):
         self.place, self.whole, self.send, self.recv, self.group = place, whole, send, recv, group
+        self.matrix, self.base, size = block
         self.mine = None
-        self.quarter = whole.shape[2] // 4
+        self.quarter = size // 4
         self.half = whole.shape[3] // 2
 
     def odd(self, z):
@@ -115,8 +129,8 @@
     def piece(self, z, a, b, side):
         odd = self.odd(z)
         row = odd * (2 * b + a) + (1 - odd) * (2 * a + b)
-        rows = pl.ds(pl.multiple_of(row * self.quarter, 16), self.quarter)
-        return self.whole.at[self.group, z, rows, pl.ds(pl.multiple_of(side * self.half, 128), self.half)]
+        rows = pl.ds(pl.multiple_of(self.base + row * self.quarter, 16), self.quarter)
+        return self.whole.at[self.matrix, z, rows, pl.ds(pl.multiple_of(side * self.half, 128), self.half)]
 
     def pass_on(self, z, slot, a, b, side, target):
         part = self.piece(z, a, b, side)
@@ -206,18 +220,63 @@
             self.sent(z)
 
 
+FORWARD_PLAN = (
+    {
+        "0.4": ("Fan",),
+        "need.1": ("San", "Fam", "Fbn", "Tan", "Faf", "Lan",),
+        "1.0": ("Sam",),
+        "1.1": ("Fbm",),
+        "1.4": ("Sbn",),
+        "need.2": ("Fbf", "Saf", "Tam", "Lam",),
+        "2.0": ("Sbm",),
+        "2.1": ("Fcn",),
+        "2.3": ("Tbn",),
+        "need.3": ("Lbn", "Taf", "Fcm", "Sbf", "Laf",),
+        "3.0": ("Tbm",),
+        "3.1": ("Fcf",),
+        "3.3": ("Lbm",),
+        "3.4": ("Scn",),
+        "ffn.0": ("Scm", "Tbf",),
+        "ffn.1": ("Lbf", "Scf", "Tcn", "Tcm", "Lcn",),
+        "ffn.2": ("Tcf", "Lcm",),
+        "ffn.3": ("Lcf",),
+    },
+    {
+        "0.4": ("Fan", "Fam",),
+        "need.1": ("Faf", "San", "Fbn", "Fbm", "Sam", "Fbf", "Saf", "Tan", "Lan",),
+        "1.0": ("Sbn",),
+        "1.2": ("Fcn",),
+        "1.3": ("Sbm",),
+        "need.2": ("Taf", "Tam", "Fcm", "Laf", "Lam",),
+        "2.0": ("Fcf", "Sbf", "Tbn",),
+        "2.3": ("Scn",),
+        "2.4": ("Lbn",),
+        "3.0": ("Tbm",),
+        "3.3": ("Lbm",),
+        "3.5": ("Scm",),
+        "ffn.0": ("Scf", "Tbf",),
+        "ffn.1": ("Tcn", "Lbf", "Lcn",),
+        "ffn.2": ("Tcm", "Tcf", "Lcm",),
+        "ffn.3": ("Lcf",),
+    },
+)
+
+
 def forward_kernel(
     n_tensor,
     heads,
     scale,
     layer_input,
-    own_segments,
-    row_segments,
-    local_a,
+    segment_ids,
+    local_qkv,
+    w_out,
     w_up,
     w_down,
     local_small,
-    vectors,
+    out_bias,
+    norm1_gain,
+    norm1_bias,
+    down_bias,
     out_w,
     out_q,
     out_k,
@@ -251,30 +310,36 @@
     small_recv,
     copy_sem,
     save_sem,
+    shard_sem,
 ):
     place = Place(n_tensor)
-    share = own_segments.shape[0]
-    length = row_input.shape[0]
+    share = hidden_low.shape[0]
+    length, width = row_input.shape
     shares_per_row = length // share
-    width = row_input.shape[1]
     group_rows = q_all.shape[2]
     size = group_rows // heads
     in_row = pl.ds(pl.multiple_of(lax.rem(place.z, shares_per_row) * share, share), share)
     row_start = pl.multiple_of(place.z // shares_per_row * length, length)
     near, middle, far = place.others
 
+    mine = weights.at[0, place.z]
+    pairs = [
+        (local_qkv, mine.at[pl.ds(0, 3 * group_rows)]),
+        (w_out, mine.at[pl.ds(3 * group_rows, group_rows)]),
+        (w_up, weights.at[1, place.z]),
+        (w_down, weights.at[2, place.z]),
+    ]
     own = [
-        pltpu.make_async_copy(source, weights.at[group, place.z], copy_sem.at[group])
-        for group, source in enumerate((local_a, w_up, w_down))
+        pltpu.make_async_copy(source, target, copy_sem.at[at]) for at, (source, target) in enumerate(pairs)
     ]
     load_input = pltpu.make_async_copy(
-        layer_input.at[pl.ds(row_start, length)], row_input, copy_sem.at[3]
+        layer_input.at[pl.ds(row_start, length)], row_input, copy_sem.at[4]
     )
     for copy in own:
         copy.start()
     load_input.start()
     meet([place.to_core, place.to_a, place.to_b] + [(place.dp, z) for z in place.others])
-    gathers = [Gather(place, weights, send, recv, group) for group in range(3)]
+    gathers = [Gather(place, weights, send, recv, group, (group, 0, width)) for group in range(3)]
     gather_a, gather_b, gather_c = gathers
 
     def small_copy(z):
@@ -285,15 +350,13 @@
         return remote(local_small, small.at[z], small_send.at[z], small_recv.at[z], (place.dp, z))
 
     own[0].wait()
+    own[1].wait()
     gather_a.start()
     for z in place.others:
         small_copy(z).start()
-    own[1].wait()
-    gather_b.start()
-    own[2].wait()
-    gather_c.start()
     small[place.z] = local_small[...]
-    bias[...] = segment_bias(own_segments[...], row_segments[...])
+    own_start = pl.multiple_of(place.z * share, share)
+    bias[...] = segment_bias(*segment_rows(segment_ids, own_start, share, row_start, length))
     load_input.wait()
 
     saves = []
@@ -303,24 +366,62 @@
         copy.start()
         saves.append(copy)
 
-    def attend(z, between):
-        weight = weights.at[0, z]
-        q_bias = small[z, 0:1, :group_rows]
-        v_bias = small[z, 1:2, :group_rows]
+    def shard_saves(at, z):
+        pairs = [
+            (weights.at[1, z], out_w.at[1, z]),
+            (weights.at[2, z], out_w.at[2, z]),
+            (activation.at[z], out_activation.at[z]),
+            (slope.at[z], out_slope.at[z]),
+        ]
+        return [
+            pltpu.make_async_copy(source, target, shard_sem.at[index, at])
+            for index, (source, target) in enumerate(pairs)
+        ]
+
+    shards = dict(zip("nmf", place.others))
+    stages = {"F": "first", "S": "second", "T": "third", "L": "last"}
+    matrices = dict(zip("abc", gathers))
+    at_end = (place.z == 0) | (place.z == n_tensor - 1)
+
+    def serve(slot, there=True):
+        for inside, plan in enumerate(FORWARD_PLAN):
+            steps = plan.get(slot, ())
+            if not steps:
+                continue
+
+            def run(steps=steps):
+                for stage, matrix, shard in steps:
+                    getattr(matrices[matrix], stages[stage])(shards[shard])
+
+            pl.when(jnp.logical_and(at_end != bool(inside), there))(run)
+
+    def start_b():
+        own[2].wait()
+        gather_b.start()
+
+    def start_c():
+        own[3].wait()
+        gather_c.start()
+
+    def attend(turn, z):
+        q_rows, k_rows, v_rows = (
+            jnp.concatenate([weights[0, z, pl.ds((3 * head + kind) * size, size)] for head in range(heads)], axis=0)
+            for kind in range(3)
+        )
+        q_bias, v_bias = small[z, 0:1, :group_rows], small[z, 1:2, :group_rows]
         x_row = row_input[...]
-        q = dot_nt(row_input[in_row], weight[:group_rows]) + q_bias
-        q = q.astype(LOW) * scale
-        k = dot_nt(x_row, weight[group_rows : 2 * group_rows]).astype(LOW)
-        v = (dot_nt(x_row, weight[2 * group_rows : 3 * group_rows]) + v_bias).astype(LOW)
+        q = (dot_nt(row_input[in_row], q_rows) + q_bias).astype(LOW) * scale
+        k = dot_nt(x_row, k_rows).astype(LOW)
+        v = (dot_nt(x_row, v_rows) + v_bias).astype(LOW)
         q_all[z], k_all[z], v_all[z] = q, k, v
         for head in range(heads):
             part = slice(head * size, (head + 1) * size)
             queries[head], keys[head], values[head] = q[:, part], k[:, part], v[:, part]
 
         def one_head(head, carry):
-            chunk = min(256, share)
-            for at in range(0, share, chunk):
-                rows = pl.ds(at, chunk)
+            chunk = share // 2
+            for part in range(2):
+                rows = pl.ds(part * chunk, chunk)
                 scores = dot_nt(queries[head, rows], keys[head]) + bias[rows]
                 top = jnp.max(scores, axis=-1, keepdims=True)
                 raised = jnp.exp(scores - top)
@@ -328,8 +429,10 @@
                 summed = dot_nn(raised.astype(LOW), values[head])
                 mixed[head, rows] = (summed / total).astype(LOW)
                 totals[z, head, rows] = top + jnp.log(total)
-            for at, service in enumerate(between):
-                pl.when(head == at)(service)
+                for index in range(heads):
+                    serve(f"{turn}.{2 * index + part}", head == index)
+                    if (turn, index, part) == (1, 0, 1):
+                        pl.when(head == index)(start_c)
             return carry
 
         lax.fori_loop(0, heads, one_head, 0)
@@ -341,113 +444,74 @@
         save(totals.at[z], out_totals.at[z])
         save(attended.at[z], out_attended.at[z])
 
-    def services(*steps):
-        def run():
-            for step, z in steps:
-                step(z)
-
-        return run
-
-    attend(place.z, [])
-    save(weights.at[1, place.z], out_w.at[1, place.z])
-    save(weights.at[2, place.z], out_w.at[2, place.z])
-    services(
-        (gather_a.first, near),
-        (gather_a.first, middle),
-        (gather_a.second, near),
-        (gather_a.first, far),
-        (gather_a.second, middle),
-        (gather_a.third, near),
-        (gather_b.first, near),
-        (gather_a.second, far),
-        (gather_a.third, middle),
-        (gather_c.first, near),
-        (gather_a.third, far),
-        (gather_b.second, near),
-        (gather_b.first, middle),
-        (gather_a.last, near),
-    )()
+    attend(0, place.z)
+    start_b()
+    serve("need.1")
     for z in place.others:
         small_arrival(z).wait_recv()
-    attend(
-        near,
-        [
-            services((gather_c.second, near), (gather_c.first, middle)),
-            services((gather_b.third, near), (gather_b.second, middle)),
-            services((gather_c.third, near), (gather_b.first, far)),
-        ],
-    )
-    gather_a.last(middle)
-    attend(
-        middle,
-        [
-            services((gather_c.second, middle), (gather_c.first, far)),
-            services((gather_b.third, middle)),
-            services((gather_b.second, far)),
-        ],
-    )
-    gather_a.last(far)
-    attend(
-        far,
-        [
-            services((gather_c.third, middle)),
-            services((gather_c.second, far)),
-            services((gather_b.third, far)),
-        ],
-    )
-
-    out_bias, gain, shift, down_bias = (vectors[at : at + 1] for at in range(4))
-    first_sum = row_input[in_row].astype(HIGH) + out_bias
+    attend(1, near)
+    serve("need.2")
+    attend(2, middle)
+    serve("need.3")
+    attend(3, far)
+
+    first_sum = row_input[in_row].astype(HIGH) + as_row(out_bias)
     for z in range(n_tensor):
         first_sum = first_sum + dot_nn(attended[z], weights[0, z, 3 * group_rows :])
     normed, spread = norm_forward(first_sum)
     xhat[...] = normed
     inverse[...] = spread
-    hidden = normed * gain + shift
+    hidden = normed * as_row(norm1_gain) + as_row(norm1_bias)
     hidden_low[...] = hidden.astype(LOW)
-    second_sum[...] = hidden + down_bias
+    second_sum[...] = hidden + as_row(down_bias)
 
     order = [place.z] + place.others
 
     def one_shard(at, carry):
         z = place.pick(at, order)
 
-        @pl.when(at > 0)
-        def _():
-            pl.when(at == 1)(services((gather_c.third, far)))
-            gather_b.last(z)
-            gather_c.last(z)
-
+        for index in range(n_tensor):
+            serve(f"ffn.{index}", at == index)
         raw = dot_nn(hidden_low[...], weights[1, z]) + small[z, 2:3]
         value, rise = gelu_parts(raw)
         activation[z] = value.astype(LOW)
         slope[z] = rise.astype(LOW)
         second_sum[...] += dot_nn(activation[z], weights[2, z])
+        for copy in shard_saves(at, z):
+            copy.start()
         return carry
 
     lax.fori_loop(0, n_tensor, one_shard, 0)
-    for z in place.others:
-        save(weights.at[1, z], out_w.at[1, z])
-        save(weights.at[2, z], out_w.at[2, z])
-    save(activation, out_activation)
-    save(slope, out_slope)
     for z in place.others:
         small_copy(z).wait_send()
     for gather in gathers:
         gather.finish()
     for copy in saves:
         copy.wait()
+    for at in range(n_tensor):
+        for copy in shard_saves(at, order[at]):
+            copy.wait()
 
 
 class Reduce:
-    def __init__(self, place, grads, lands, pieces, send, recv, wide, group):
-        self.place, self.grads, self.pieces = place, grads, pieces
-        self.wide_flips, self.wide_out, self.wide_land, self.wide_send, self.wide_recv = wide
-        self.core_land, self.first_land, self.second_land, self.far_land = lands
-        self.send, self.recv, self.group = send, recv, group
-        self.half = grads.shape[2] // 2
-        self.quarter = grads.shape[2] // 4
-        self.side = grads.shape[3] // 2
+    def __init__(self, place, grads, lands, pieces, send, recv, wide, group, block):
+        matrix, base, size = block
+        self.place, self.send, self.recv, self.group = place, send, recv, group
+        self.half, self.quarter, self.side = size // 2, size // 4, grads.shape[3] // 2
+
+        def rows(ref, parts):
+            return ref.at[matrix, :, pl.ds(base // parts, size // parts)]
+
+        core_land, first_land, second_land, far_land = lands
+        self.grads, self.core_land = rows(grads, 1), rows(core_land, 1)
+        self.first_land, self.second_land, self.far_land = (
+            rows(first_land, 2),
+            rows(second_land, 4),
+            rows(far_land, 4),
+        )
+        self.piece = pieces.at[matrix, pl.ds(base // 4, size // 4)]
+        self.wide_flips, wide_out, wide_land, self.wide_send, self.wide_recv = wide
+        self.wide_out, self.wide_land = rows(wide_out, 4), rows(wide_land, 4)
 
     def columns(self, side):
         return pl.ds(pl.multiple_of(side * self.side, 128), self.side)
@@ -468,20 +532,20 @@
         return remote(source, target_ref, send, recv, target)
 
     def core_copy(self, z):
-        p, group = self.place, self.group
-        source = self.grads.at[group, z, :, self.columns(1 - p.core)]
-        return self.copy(z, 0, source, self.core_land.at[group, z], p.to_core)
+        p = self.place
+        source = self.grads.at[z, :, self.columns(1 - p.core)]
+        return self.copy(z, 0, source, self.core_land.at[z], p.to_core)
 
     def first_copy(self, z):
         ahead, _, target, _ = self.axes(z)
-        source = self.core_land.at[self.group, z, self.rows((1 - ahead) * self.half, self.half)]
-        return self.copy(z, 1, source, self.first_land.at[self.group, z], target)
+        source = self.core_land.at[z, self.rows((1 - ahead) * self.half, self.half)]
+        return self.copy(z, 1, source, self.first_land.at[z], target)
 
     def second_copy(self, z):
         ahead, behind, _, target = self.axes(z)
         start = ahead * self.half + (1 - behind) * self.quarter
-        source = self.core_land.at[self.group, z, self.rows(start, self.quarter)]
-        return self.copy(z, 2, source, self.second_land.at[self.group, z], target)
+        source = self.core_land.at[z, self.rows(start, self.quarter)]
+        return self.copy(z, 2, source, self.second_land.at[z], target)
 
     def kept(self, z):
         ahead, behind, _, _ = self.axes(z)
@@ -489,20 +553,20 @@
 
     def far_copy(self, z):
         p, group = self.place, self.group
-        source = self.core_land.at[group, z, self.kept(z)]
+        source = self.core_land.at[z, self.kept(z)]
         send, recv = self.send.at[group, z, 3], self.recv.at[group, p.z, 3]
-        return remote(source, self.far_land.at[group, p.z], send, recv, (p.dp, z))
+        return remote(source, self.far_land.at[p.z], send, recv, (p.dp, z))
 
     def far_arrival(self, z):
         p, group = self.place, self.group
-        land = self.far_land.at[group, z]
+        land = self.far_land.at[z]
         return remote(land, land, self.send.at[group, z, 3], self.recv.at[group, z, 3], (p.dp, z))
 
     def wide_copy(self, at):
         group = self.group
         sems = self.wide_send.at[group, at], self.wide_recv.at[group, at]
         target = (self.wide_flips[at], self.place.z)
-        return remote(self.wide_out.at[group, at], self.wide_land.at[group, at], *sems, target)
+        return remote(self.wide_out.at[at], self.wide_land.at[at], *sems, target)
 
     def start(self, z):
         self.core_copy(z).start()
@@ -513,37 +577,37 @@
     def first(self, z):
         p = self.place
         self.core_copy(z).wait_recv()
-        mine = self.grads[self.group, z, :, self.columns(p.core)]
-        land = self.core_land.at[self.group, z]
+        mine = self.grads[z, :, self.columns(p.core)]
+        land = self.core_land.at[z]
         self.add(land, slice(None), mine)
         self.first_copy(z).start()
 
     def second(self, z):
         ahead, _, _, _ = self.axes(z)
         self.first_copy(z).wait_recv()
-        land = self.core_land.at[self.group, z]
-        self.add(land, self.rows(ahead * self.half, self.half), self.first_land[self.group, z])
+        land = self.core_land.at[z]
+        self.add(land, self.rows(ahead * self.half, self.half), self.first_land[z])
         self.second_copy(z).start()
 
     def third(self, z):
         self.second_copy(z).wait_recv()
-        land = self.core_land.at[self.group, z]
-        self.add(land, self.kept(z), self.second_land[self.group, z])
+        land = self.core_land.at[z]
+        self.add(land, self.kept(z), self.second_land[z])
         pl.when(z != self.place.z)(self.far_copy(z).start)
 
     def fourth(self):
         p = self.place
-        total = self.core_land[self.group, p.z, self.kept(p.z)].astype(HIGH)
+        total = self.core_land[p.z, self.kept(p.z)].astype(HIGH)
         for z in p.others:
             self.far_arrival(z).wait_recv()
-            total = total + self.far_land[self.group, z].astype(HIGH)
+            total = total + self.far_land[z].astype(HIGH)
         for at in range(len(self.wide_flips)):
-            self.wide_out[self.group, at] = total.astype(LOW)
+            self.wide_out[at] = total.astype(LOW)
             copy = self.wide_copy(at)
             copy.start()
             copy.wait_recv()
-            total = self.wide_out[self.group, at].astype(HIGH) + self.wide_land[self.group, at].astype(HIGH)
-        self.pieces[self.group] = total.astype(LOW)
+            total = self.wide_out[at].astype(HIGH) + self.wide_land[at].astype(HIGH)
+        self.piece[...] = total.astype(LOW)
 
     def finish(self):
         p = self.place
@@ -558,9 +622,9 @@
 
 
 class Return(Spread):
-    def __init__(self, place, whole, pieces, send, recv, keep_sem, group):
-        super().__init__(place, whole, send, recv, group)
-        self.mine = pieces.at[group]
+    def __init__(self, place, whole, pieces, send, recv, keep_sem, group, block):
+        super().__init__(place, whole, send, recv, group, block)
+        self.mine = pieces.at[self.matrix, pl.ds(self.base // 4, self.quarter)]
         p = place
         self.keep = pltpu.make_async_copy(self.mine, self.piece(0, p.a, p.b, p.core), keep_sem.at[group])
 
@@ -574,6 +638,18 @@
 
     def odd(self, z):
         return lax.rem(self.place.z + self.group, 2)
+
+
+class Several:
+    def __init__(self, parts):
+        self.parts = parts
+
+    def __getattr__(self, name):
+        def call(*arguments):
+            for part in self.parts:
+                getattr(part, name)(*arguments)
+
+        return call
 
 
 def backward_kernel(
@@ -581,9 +657,10 @@
     heads,
     scale,
     layer_input,
-    own_segments,
-    row_segments,
-    vectors,
+    segment_ids,
+    norm1_gain,
+    norm2_gain,
+    norm2_bias,
     in_cotangent,
     in_w,
     in_q,
@@ -624,6 +701,7 @@
     grad_k,
     grad_v,
     inverse,
+    live_rows,
     terms,
     hidden_low,
     grad_low,
@@ -651,8 +729,7 @@
     keep_sem,
 ):
     place = Place(n_tensor)
-    share = own_segments.shape[0]
-    length = row_input.shape[0]
+    share, length = hidden_low.shape[0], row_input.shape[0]
     shares_per_row = length // share
     group_rows = q_all.shape[2]
     size = group_rows // heads
@@ -708,14 +785,24 @@
     meet([(flip, place.z) for flip in flips] + [(place.dp, z) for z in place.others])
     lands = (core_land, first_land, second_land, far_land)
     wide = (flips[3:], wide_out, wide_land, wide_send, wide_recv)
-    reduces = [Reduce(place, weights, lands, pieces, send, recv, wide, group) for group in range(3)]
+    width = row_input.shape[1]
+    blocks = [(0, 0, width // 2), (0, width // 2, width // 2), (1, 0, width), (2, 0, width)]
+    reduces = [
+        Reduce(place, weights, lands, pieces, send, recv, wide, group, block)
+        for group, block in enumerate(blocks)
+    ]
     returns = [
-        Return(place, out_summed, pieces, final_send, final_recv, keep_sem, group) for group in range(3)
+        Return(place, out_summed, pieces, final_send, final_recv, keep_sem, group, block)
+        for group, block in enumerate(blocks)
     ]
-    reduce_a, reduce_b, reduce_c = reduces
+    reduce_a, reduce_b, reduce_c = Several(reduces[:2]), reduces[2], reduces[3]
+    return_a, return_b, return_c = Several(returns[:2]), returns[2], returns[3]
     sums[0] = jnp.zeros(sums.shape[1:], HIGH)
-    bias[...] = segment_bias(own_segments[...], row_segments[...])
-    gain_first, gain_second, shift_second = vectors[1:2], vectors[4:5], vectors[5:6]
+    own_start = pl.multiple_of(place.z * share, share)
+    own_segments, row_segments = segment_rows(segment_ids, own_start, share, row_start, length)
+    bias[...] = segment_bias(own_segments, row_segments)
+    live_rows[...] = (own_segments >= 0).astype(HIGH)
+    gain_first, gain_second, shift_second = as_row(norm1_gain), as_row(norm2_gain), as_row(norm2_bias)
 
     for copy in early:
         copy.wait()
@@ -724,13 +811,12 @@
     def second_norm(at, carry):
         rows = pl.ds(pl.multiple_of(at * band, band), band)
         normed, spread = norm_forward(accum[rows])
-        live = (own_segments[rows] >= 0).astype(HIGH)
-        cotangent = spare[0, rows].astype(HIGH) * live
+        cotangent = spare[0, rows].astype(HIGH) * live_rows[rows]
         spare[0, rows] = (normed * gain_second + shift_second).astype(LOW)
         grad_second = norm_backward(normed, spread, cotangent * gain_second)
-        sums[0, n_tensor, 4:5] += column_sum(cotangent * normed)
-        sums[0, n_tensor, 5:6] += column_sum(cotangent)
-        sums[0, n_tensor, 3:4] += column_sum(grad_second)
+        sums[0, 0, 6:7] += column_sum(cotangent * normed)
+        sums[0, 0, 7:8] += column_sum(cotangent)
+        sums[0, 0, 5:6] += column_sum(grad_second)
         grad_low[rows] = grad_second.astype(LOW)
         accum[rows] = grad_second
         return carry
@@ -761,7 +847,7 @@
         accum[...] += dot_nt(grad_up, weights[1, z])
         weights[1, z] = dot_tn(hidden_low[...], grad_up).astype(LOW)
         reduce_b.start(z)
-        sums[0, z, 2:3] = column_sum(grad_up.astype(HIGH))
+        sums[0, z, 1:2] = column_sum(grad_up.astype(HIGH))
         reduce_c.first(z)
         pl.when(at == 2)(functools.partial(reduce_c.second, order[0]))
         return carry
@@ -772,9 +858,9 @@
         rows = pl.ds(pl.multiple_of(at * band, band), band)
         grad_hidden, normed = accum[rows], xhat[rows]
         grad_first = norm_backward(normed, inverse[rows], grad_hidden * gain_first)
-        sums[0, n_tensor, 0:1] += column_sum(grad_first)
-        sums[0, n_tensor, 1:2] += column_sum(grad_hidden * normed)
-        sums[0, n_tensor, 2:3] += column_sum(grad_hidden)
+        sums[0, 0, 2:3] += column_sum(grad_first)
+        sums[0, 0, 3:4] += column_sum(grad_hidden * normed)
+        sums[0, 0, 4:5] += column_sum(grad_hidden)
         accum[rows] = grad_first
         grad_low[rows] = grad_first.astype(LOW)
         return carry
@@ -785,10 +871,30 @@
     reduce_b.first(order[-1])
     late.wait()
 
+    def finish_c():
+        reduce_c.fourth()
+        return_c.hand_out(0)
+
+    def finish_b():
+        reduce_b.fourth()
+        return_b.hand_out(0)
+
+    term_copies = []
+    for step in range(1, shares_per_row):
+        partner = place.z - my_share + lax.rem(my_share + step, shares_per_row)
+        sems = term_send.at[step - 1], term_recv.at[step - 1]
+        term_copies.append(remote(spare.at[step - 1], landed.at[step - 1], *sems, (place.dp, partner)))
+
+    def send_terms():
+        save_layer.wait()
+        for step in range(1, shares_per_row):
+            spare[step - 1] = terms[1 + lax.rem(my_share + step, shares_per_row)].astype(LOW)
+            term_copies[step - 1].start()
+
     def attend(at, carry):
         z, slot = place.pick(at, order), lax.rem(at, 2)
         after = place.pick(at + 1, order)
-        before, earlier = place.pick(at - 1, order), place.pick(at - 2, order)
+        before = place.pick(at - 1, order)
 
         @pl.when(at + 1 < n_tensor)
         def _():
@@ -829,13 +935,17 @@
                 reduce_c.third(z)
                 pl.when(at + 1 < n_tensor)(functools.partial(reduce_c.second, after))
 
-            pl.when(head == 1)(functools.partial(reduce_b.third, z))
+            @pl.when(head == 1)
+            def _():
+                reduce_b.third(z)
+                pl.when(at == n_tensor - 1)(finish_c)
+                pl.when(at >= 2)(functools.partial(reduce_a.third, place.pick(at - 2, order)))
 
             @pl.when(head == 2)
             def _():
                 pl.when(at + 1 < n_tensor)(functools.partial(reduce_b.second, after))
-                pl.when(at >= 3)(functools.partial(reduce_a.third, order[0]))
-                pl.when(at >= 2)(functools.partial(reduce_a.second, earlier))
+                pl.when(at == n_tensor - 1)(finish_b)
+                pl.when(at >= 1)(functools.partial(reduce_a.second, before))
 
             return inner
 
@@ -844,32 +954,30 @@
         dk = grad_k[...].reshape(group_rows, length)
         dv = grad_v[...].reshape(group_rows, length)
         x_row = row_input[...]
-        accum[...] += dot_nn(dq, weights[0, z, :group_rows])
-        row_term = dot_tn(jnp.concatenate([dk, dv], axis=0), weights[0, z, group_rows : 3 * group_rows])
+        q_rows, k_rows, v_rows = (
+            jnp.concatenate([weights[0, z, pl.ds((3 * head + kind) * size, size)] for head in range(heads)], axis=0)
+            for kind in range(3)
+        )
         for index in range(shares_per_row):
-            terms[1 + index] += row_term[index * share : (index + 1) * share]
-        weights[0, z, :group_rows] = dot_tn(dq, row_input[in_row]).astype(LOW)
-        weights[0, z, group_rows : 2 * group_rows] = dot_nn(dk, x_row).astype(LOW)
-        weights[0, z, 2 * group_rows : 3 * group_rows] = dot_nn(dv, x_row).astype(LOW)
+            tokens = slice(index * share, (index + 1) * share)
+            terms[1 + index] += dot_tn(dk[:, tokens], k_rows) + dot_tn(dv[:, tokens], v_rows)
+        pl.when(at == n_tensor - 1)(send_terms)
+        accum[...] += dot_nn(dq, q_rows)
+        for kind, (left, right) in enumerate(((dq.T, row_input[in_row]), (dk, x_row), (dv, x_row))):
+            grad = dot_nn(left, right).astype(LOW)
+            for head in range(heads):
+                weights[0, z, pl.ds((3 * head + kind) * size, size)] = grad[head * size : (head + 1) * size]
         reduce_a.start(z)
         ones = jnp.ones((8, length), LOW)
-        sums[0, z, 0:1, :group_rows] = dot_nn(ones[:, :share], dq)[0:1]
-        sums[0, z, 1:2, :group_rows] = dot_nt(ones, dv)[0:1]
+        q_sums, v_sums = dot_nn(ones[:, :share], dq)[0:1], dot_nt(ones, dv)[0:1]
+        for head in range(heads):
+            part = slice(head * size, (head + 1) * size)
+            pair = jnp.concatenate([q_sums[:, part], v_sums[:, part]], axis=1)
+            sums[0, z, 0:1, 2 * head * size : 2 * (head + 1) * size] = pair
         return carry
 
     lax.fori_loop(0, n_tensor, attend, 0)
 
-    save_layer.wait()
-    term_copies = []
-    for step in range(1, shares_per_row):
-        other = lax.rem(my_share + step, shares_per_row)
-        spare[step - 1] = terms[1 + other].astype(LOW)
-        partner = place.z - my_share + other
-        copy = remote(
-            spare.at[step - 1], landed.at[step - 1], term_send.at[step - 1], term_recv.at[step - 1], (place.dp, partner)
-        )
-        copy.start()
-        term_copies.append(copy)
     accum[...] += terms[1 + my_share]
     save_partial = pltpu.make_async_copy(accum, out_partial, save_sem.at[1])
     save_partial.start()
@@ -885,27 +993,22 @@
 
     def far_sum(z):
         sems = sums_send.at[bits + z], sums_recv.at[bits + place.z]
-        return remote(sums.at[bits], sums_far.at[place.z], *sems, (place.dp, z))
+        return remote(sums.at[bits, z], sums_far.at[place.z], *sems, (place.dp, z))
 
     def far_sum_arrival(z):
         sems = sums_send.at[bits + z], sums_recv.at[bits + z]
-        return remote(sums.at[bits], sums_far.at[z], *sems, (place.dp, z))
-
-    return_a, return_b, return_c = returns
+        return remote(sums.at[bits, z], sums_far.at[z], *sems, (place.dp, z))
+
+    for z in range(1, n_tensor):
+        sums[0, z, 2:8] = sums[0, 0, 2:8]
     sum_copy(0).start()
-    reduce_c.fourth()
-    return_c.hand_out(0)
-    reduce_b.fourth()
-    return_b.hand_out(0)
     reduce_a.first(order[3])
-    reduce_a.second(order[2])
-    reduce_a.third(order[1])
+    reduce_a.third(order[2])
     fold(0)
     sum_copy(1).start()
     return_c.second(0)
     return_b.second(0)
     reduce_a.second(order[3])
-    reduce_a.third(order[2])
     fold(1)
     sum_copy(2).start()
     return_c.third(0)
@@ -919,7 +1022,7 @@
             sum_copy(bit + 1).start()
     for z in place.others:
         far_sum(z).start()
-    sums_far[place.z] = sums[bits]
+    sums_far[place.z] = sums[bits, place.z]
     return_c.last(0)
     return_b.last(0)
     return_a.second(0)
@@ -947,6 +1050,80 @@
         reduce.finish()
     for part in returns:
         part.sent(0)
+
+
+def finish_kernel(
+    heads,
+    in_layer,
+    in_partial,
+    in_landed,
+    in_summed,
+    sums,
+    out_layer,
+    out_input,
+    out_qkv,
+    qv_bias,
+    out_out,
+    out_bias,
+    gain_first,
+    shift_first,
+    out_up,
+    up_bias,
+    out_down,
+    down_bias,
+    gain_second,
+    shift_second,
+    layer,
+    partial,
+    landed,
+    summed,
+    qkv,
+    rest,
+    matrices,
+    load_sem,
+    save_sem,
+):
+    size = qkv.shape[1]
+    pairs = [(in_summed.at[2, 0], summed.at[2]), (in_summed.at[1, 0], summed.at[1]), (in_partial, partial)]
+    pairs += [(in_landed, landed), (in_summed.at[0, 0], summed.at[0]), (in_layer, layer)]
+    loads = [
+        pltpu.make_async_copy(source, target, load_sem.at[at]) for at, (source, target) in enumerate(pairs)
+    ]
+    for copy in loads:
+        copy.start()
+    for at, vector in enumerate(
+        [up_bias, out_bias, gain_first, shift_first, down_bias, gain_second, shift_second]
+    ):
+        vector[...] = sums[1 + at : 2 + at].reshape(vector.shape)
+    for head in range(heads):
+        width = qv_bias.shape[1]
+        qv_bias[head : head + 1] = sums[0:1, head * width : (head + 1) * width]
+    saves = []
+
+    def save(source, target):
+        copy = pltpu.make_async_copy(source, target, save_sem.at[len(saves)])
+        copy.start()
+        saves.append(copy)
+
+    for at, target in ((2, out_down), (1, out_up)):
+        loads[2 - at].wait()
+        matrices[at - 1] = summed[at].astype(HIGH)
+        save(matrices.at[at - 1], target)
+    loads[2].wait()
+    loads[3].wait()
+    for step in range(landed.shape[0]):
+        partial[...] += landed[step].astype(HIGH)
+    save(partial, out_input)
+    loads[4].wait()
+    rest[...] = summed[0, heads * size :].astype(HIGH)
+    save(rest, out_out)
+    for head in range(heads):
+        qkv[head] = summed[0, head * size : (head + 1) * size].astype(HIGH)
+    save(qkv, out_qkv)
+    loads[5].wait()
+    save(layer, out_layer)
+    for copy in saves:
+        copy.wait()
 
 
 def on_device(
@@ -978,8 +1155,7 @@
     shares_per_row = SEQ // share
     group_rows = heads * head_dim
 
-    local_a = w_qkv.reshape(width, heads, 3, head_dim).transpose(2, 1, 3, 0).reshape(-1, width)
-    local_a = jnp.concatenate([local_a, w_out], axis=0)
+    local_qkv = w_qkv.transpose(1, 2, 0).reshape(3 * group_rows, width)
     local_small = jnp.concatenate(
         [
             jnp.pad(qv_bias[:, :head_dim].reshape(1, -1), ((0, 0), (0, width - group_rows))),
@@ -988,12 +1164,6 @@
             jnp.zeros((5, width), LOW),
         ]
     ).astype(HIGH)
-    vectors = jnp.stack(
-        [out_bias, norm1_gain, norm1_bias, down_bias, norm2_gain, norm2_bias, out_bias, out_bias]
-    ).astype(HIGH)
-    row_start = (place // shares_per_row) * SEQ
-    own_segments = lax.dynamic_slice_in_dim(segment_ids, place * share, share, 0)[:, None]
-    row_segments = lax.dynamic_slice_in_dim(segment_ids, row_start, SEQ, 0)[None, :]
 
     vmem = pl.BlockSpec(memory_space=pltpu.VMEM)
     anywhere = pl.BlockSpec(memory_space=pl.ANY)
@@ -1029,7 +1199,7 @@
             high(share, 1),
             high(share, width),
         ),
-        in_specs=[anywhere, vmem, vmem, anywhere, anywhere, anywhere, vmem, vmem],
+        in_specs=[anywhere, vmem] + [anywhere] * 4 + [vmem] * 5,
         out_specs=(anywhere,) * 8 + (vmem,) * 5,
         scratch_shapes=[
             low_scratch(*whole),
@@ -1050,14 +1220,27 @@
             dma((3, n_tensor, 8)),
             dma((n_tensor,)),
             dma((n_tensor,)),
-            dma((4,)),
-            dma((40,)),
+            dma((5,)),
+            dma((24,)),
+            dma((4, n_tensor)),
         ],
         compiler_params=pltpu.CompilerParams(
             collective_id=0, has_side_effects=True, vmem_limit_bytes=VMEM_LIMIT
         ),
         name="forward",
-    )(layer_input, own_segments, row_segments, local_a, w_up, w_down, local_small, vectors)
+    )(
+        layer_input,
+        segment_ids,
+        local_qkv,
+        w_out,
+        w_up,
+        w_down,
+        local_small,
+        out_bias,
+        norm1_gain,
+        norm1_bias,
+        down_bias,
+    )
 
     half, side = width // 2, width // 2
     quarter = width // 4
@@ -1069,9 +1252,9 @@
             high(share, width),
             low(shares_per_row - 1, share, width),
             low(3, 1, width, width),
-            high(n_tensor + 1, 8, width),
+            high(8, width),
         ),
-        in_specs=[anywhere, vmem, vmem, vmem] + [anywhere] * 13,
+        in_specs=[anywhere] + [vmem] * 4 + [anywhere] * 13,
         out_specs=(anywhere,) * 4 + (vmem,),
         scratch_shapes=[
             low_scratch(*whole),
@@ -1096,22 +1279,23 @@
             low_scratch(heads, head_dim, SEQ),
             low_scratch(heads, head_dim, SEQ),
             high_scratch(share, 1),
+            high_scratch(share, 1),
             high_scratch(1 + shares_per_row, share, width),
             low_scratch(share, width),
             low_scratch(share, width),
             low_scratch(shares_per_row - 1, share, width),
             low_scratch(shares_per_row - 1, share, width),
-            high_scratch(bits + 1, n_tensor + 1, 8, width),
-            high_scratch(bits, n_tensor + 1, 8, width),
-            high_scratch(n_tensor, n_tensor + 1, 8, width),
-            dma((3, n_tensor, 4)),
-            dma((3, n_tensor, 4)),
-            dma((3, 1, 9)),
-            dma((3, 1, 8)),
+            high_scratch(bits + 1, n_tensor, 8, width),
+            high_scratch(bits, n_tensor, 8, width),
+            high_scratch(n_tensor, 8, width),
+            dma((4, n_tensor, 4)),
+            dma((4, n_tensor, 4)),
+            dma((4, 1, 9)),
+            dma((4, 1, 8)),
             low_scratch(3, wide, quarter, side),
             low_scratch(3, wide, quarter, side),
-            dma((3, wide)),
-            dma((3, wide)),
+            dma((4, wide)),
+            dma((4, wide)),
             dma((8,)),
             dma((3, n_tensor)),
             dma((7, 2)),
@@ -1120,7 +1304,7 @@
             dma((bits + n_tensor,)),
             dma((bits + n_tensor,)),
             dma((6,)),
-            dma((3,)),
+            dma((4,)),
         ],
         compiler_params=pltpu.CompilerParams(
             collective_id=1, has_side_effects=True, vmem_limit_bytes=VMEM_LIMIT
@@ -1128,9 +1312,10 @@
         name="backward",
     )(
         layer_input,
-        own_segments,
-        row_segments,
-        vectors,
+        segment_ids,
+        norm1_gain,
+        norm2_gain,
+        norm2_bias,
         out_cotangent,
         w,
         q,
@@ -1146,32 +1331,43 @@
         second_sum,
     )
 
-    input_grad = partial
-    for step in range(shares_per_row - 1):
-        input_grad = input_grad + landed[step].astype(HIGH)
-    summed = summed[:, 0].astype(HIGH)
-    grad_qkv = summed[0, : 3 * group_rows].reshape(3, heads, head_dim, width).transpose(3, 1, 0, 2)
-    mine = lax.dynamic_slice_in_dim(sums, place, 1, 0)[0]
-    every = sums[n_tensor]
-    grad_qv_bias = jnp.concatenate(
-        [mine[at, :group_rows].reshape(heads, head_dim) for at in range(2)], axis=1
-    )
-    return (
-        layer_output,
-        input_grad,
-        grad_qkv.reshape(width, heads, 3 * head_dim),
-        grad_qv_bias,
-        summed[0, 3 * group_rows :],
-        every[0],
-        every[1],
-        every[2],
-        summed[1],
-        mine[2],
-        summed[2],
-        every[3],
-        every[4],
-        every[5],
-    )
+    vector = high(width)
+    matrix = high(width, width)
+    layer_output, input_grad, grad_qkv, *rest = pl.pallas_call(
+        functools.partial(finish_kernel, heads),
+        out_shape=(
+            low(share, width),
+            high(share, width),
+            high(heads, 3 * head_dim, width),
+            high(heads, 2 * head_dim),
+            high(group_rows, width),
+            vector,
+            vector,
+            vector,
+            matrix,
+            vector,
+            matrix,
+            vector,
+            vector,
+            vector,
+        ),
+        in_specs=[anywhere] * 4 + [vmem],
+        out_specs=(anywhere,) * 3 + (vmem, anywhere, vmem, vmem, vmem, anywhere, vmem, anywhere, vmem, vmem, vmem),
+        scratch_shapes=[
+            low_scratch(share, width),
+            high_scratch(share, width),
+            low_scratch(shares_per_row - 1, share, width),
+            low_scratch(3, width, width),
+            high_scratch(heads, 3 * head_dim, width),
+            high_scratch(group_rows, width),
+            high_scratch(2, width, width),
+            dma((6,)),
+            dma((6,)),
+        ],
+        compiler_params=pltpu.CompilerParams(vmem_limit_bytes=VMEM_LIMIT),
+        name="finish",
+    )(layer_output, partial, landed, summed, sums)
+    return (layer_output, input_grad, grad_qkv.transpose(2, 0, 1), *rest)
 
 
 def solution(mesh):

time: 221 us -> 189 us (0.86)
  local copies, waits for them, and re-layouts: 18.5 us -> 1.76 us
  Pallas kernels: 194 us -> 185 us
  other arithmetic: 7.16 us -> 0.68 us
    pallas_call x1, Pallas kernels: 80.6 us -> 68.1 us  [on_device(): pl.pallas_call(functools.partial(forward_kernel, n_tensor, heads, score_s...]
    pallas_call x0 -> x1, Pallas kernels: none -> 6.6 us  [on_device(): pl.pallas_call(functools.partial(finish_kernel, heads), out_shape=(low(sh...]
    another operation x9 -> x0, local copies, waits for them, and re-layouts: 4.32 us -> none  [the longest x7 4.16 us: on_device(): jnp.stack([out_bias, norm1_gain, norm1_bias, down_bias, norm2_gain, norm2...]
    squeeze x3 -> x0, local copies, waits for them, and re-layouts: 4.23 us -> none  [the longest x1 2.49 us: on_device(): summed[2]]
    pallas_call x1, Pallas kernels: 114 us -> 110 us  [on_device(): pl.pallas_call(functools.partial(backward_kernel, n_tensor, heads, score_...]
    add x1 -> x0, other arithmetic: 2.89 us -> none  [on_device(): input_grad = input_grad + landed[step].astype(HIGH)]
where the time goes in v4:
time: 189 us; the launch traced here: 188 us
  Pallas kernels  185 us (98%)
    pallas_call x1, Pallas kernels, on_device(): pl.pallas_call(functools.partial(backward_kernel, n_tensor, heads, score_...  110 us
    pallas_call x1, Pallas kernels, on_device(): pl.pallas_call(functools.partial(forward_kernel, n_tensor, heads, score_s...  68.1 us
    pallas_call x1, Pallas kernels, on_device(): pl.pallas_call(functools.partial(finish_kernel, heads), out_shape=(low(sh...  6.6 us

profile of v4, /device:TPU:0, one launch (start us, length us, event | category | flops | bytes accessed | tf_op | source)
XLA Modules:
  0.0 188.2 jit_solution(11895756334962928390)
XLA Ops:
  0.7 0.1 pad.12.clone
  0.7 0.8 fusion.7
  1.6 0.1 reshape.41
  1.6 0.1 reshape.42
  1.7 0.7 reshape.43
  2.4 0.7 fusion.6.local_small
  3.1 68.1 %forward.1 = (bf16[3,4,768,768]{3,2,1,0:T(8,128)(2,1)}, bf16[4,512,192]{2,1,0:T(8,128)(2,1)}, bf16[4,1024,192]{2,1,0:T(8,128)(2,1)}, bf16[4,1024,192]{2,1,0:T(8,...) custom-call(bf16[2048,768]{1,0:T(8,128)(2,1)} %layer_input.3, ...), custom_call_target="tpu_custom_call" | custom-call | tf_op jit(solution)/shard_map/forward/pallas_call | solution.py:1185
  71.2 110.2 %backward.1 = (bf16[512,768]{1,0:T(8,128)(2,1)}, f32[512,768]{1,0:T(8,128)}, bf16[1,512,768]{2,1,0:T(8,128)(2,1)}, bf16[3,1,768,768]{3,2,1,0:T(8,128)(2,1)}, f32[8,768]{1,0:T(8,128)}) custom-call(bf16[2048,768]{1,0:T(8,128)(2,1)} %layer_input.3, s32[2048]{0:T(1024)} %segment_ids.3, bf16[768]{0:T(1024)(128)(2,1)} %norm1_gain.3, bf16[768]{0:T(1024)(128)(2,1)} %norm2_gain.1, ...), custom_call_target="tpu_custom_call" | custom-call | tf_op jit(solution)/shard_map/backward/pallas_call | solution.py:1248
  181.4 6.6 %finish.1 = (bf16[512,768]{1,0:T(8,128)(2,1)}, f32[512,768]{1,0:T(8,128)}, f32[3,192,768]{2,1,0:T(8,128)}, f32[3,128]{1,0:T(4,128)}, f32[192,768]{1,0:T(8,128)},...) custom-call(bf16[512,768]{1,0:T(8,128)(2,1)} %get-tuple-element.57.i, ...), custom_call_target="tpu_custom_call" | custom-call | tf_op jit(solution)/shard_map/finish/pallas_call | solution.py:1336
  (1 shorter events, 0.0 us)

commit v5 on v4

v5 whole, which is shorter than its diff:
```python
import functools

import jax
import jax.numpy as jnp
from jax import lax
from jax.experimental import pallas as pl
from jax.experimental.pallas import tpu as pltpu
from jax.sharding import PartitionSpec as P

SEQ = 1024


EPSILON = 1e-06
MASKED = -1e30
LOW = jnp.bfloat16
HIGH = jnp.float32
MESH = pl.DeviceIdType.MESH
VMEM_LIMIT = 127 * 512 * 1024


def dot_nn(left, right):
    return lax.dot_general(left, right, (((1,), (0,)), ((), ())), preferred_element_type=HIGH)


def dot_nt(left, right):
    return lax.dot_general(left, right, (((1,), (1,)), ((), ())), preferred_element_type=HIGH)


def dot_tn(left, right):
    return lax.dot_general(left, right, (((0,), (0,)), ((), ())), preferred_element_type=HIGH)


def norm_forward(summed):
    mean = jnp.mean(summed, axis=-1, keepdims=True)
    centred = summed - mean
    spread = jnp.mean(centred * centred, axis=-1, keepdims=True)
    inverse = lax.rsqrt(spread + EPSILON)
    return centred * inverse, inverse


def norm_backward(xhat, inverse, scaled):
    return inverse * (
        scaled
        - jnp.mean(scaled, axis=-1, keepdims=True)
        - xhat * jnp.mean(scaled * xhat, axis=-1, keepdims=True)
    )


def gelu_parts(u):
    phi_cdf = 0.5 * (1.0 + lax.erf(u * (2.0**-0.5)))
    density = jnp.exp(-0.5 * u * u) * 0.3989422804014327
    return u * phi_cdf, phi_cdf + u * density


def column_sum(values):
    return jnp.sum(values, axis=0, keepdims=True)


def as_row(vector):
    return vector[...].astype(HIGH).reshape(1, -1)


def as_column(row):
    return jnp.broadcast_to(row, (8, row.shape[1])).T[:, :1]


def segment_rows(segment_ids, own_start, share, row_start, length):
    own = segment_ids[pl.ds(own_start, share)].astype(HIGH).reshape(1, share)
    return as_column(own), segment_ids[pl.ds(row_start, length)].astype(HIGH).reshape(1, length)


def segment_bias(own_segments, row_segments):
    return jnp.where(own_segments == row_segments, 0.0, MASKED)


class Place:
    def __init__(self, n_tensor):
        self.n_tensor = n_tensor
        self.z = lax.axis_index("tensor")
        self.dp = lax.axis_index("dp")
        self.core = lax.rem(self.dp, 2)
        self.a = lax.rem(self.dp // 2, 2)
        self.b = lax.rem(self.dp // 4, 2)
        self.to_core = (self.dp + 1 - 2 * self.core, self.z)
        self.to_a = (self.dp + 2 - 4 * self.a, self.z)
        self.to_b = (self.dp + 4 - 8 * self.b, self.z)
        self.others = [lax.rem(self.z + step, n_tensor) for step in range(1, n_tensor)]
        if n_tensor == 4:
            near = self.z + 1 - 2 * lax.rem(self.z, 2)
            upper = self.z // 2
            self.others = [near, 2 - upper, 3 - 3 * upper]

    def pick(self, at, order):
        chosen = order[0]
        for index in range(1, len(order)):
            chosen = jnp.where(at == index, order[index], chosen)
        return chosen


def greet(partners):
    barrier = pltpu.get_barrier_semaphore()
    for partner in partners:
        pl.semaphore_signal(barrier, inc=1, device_id=partner, device_id_type=MESH)


def meet(partners):
    pl.semaphore_wait(pltpu.get_barrier_semaphore(), len(partners))


def remote(src, dst, send, recv, target):
    return pltpu.make_async_remote_copy(
        src_ref=src,
        dst_ref=dst,
        send_sem=send,
        recv_sem=recv,
        device_id=target,
        device_id_type=MESH,
    )


class Spread:
    def __init__(self, place, whole, send, recv, group, block):
        self.place, self.whole, self.send, self.recv, self.group = place, whole, send, recv, group
        self.matrix, self.base, size = block
        self.mine = None
        self.quarter = size // 4
        self.half = whole.shape[3] // 2

    def odd(self, z):
        return lax.rem(z + self.group, 2)

    def piece(self, z, a, b, side):
        odd = self.odd(z)
        row = odd * (2 * b + a) + (1 - odd) * (2 * a + b)
        rows = pl.ds(pl.multiple_of(self.base + row * self.quarter, 16), self.quarter)
        return self.whole.at[self.matrix, z, rows, pl.ds(pl.multiple_of(side * self.half, 128), self.half)]

    def pass_on(self, z, slot, a, b, side, target):
        part = self.piece(z, a, b, side)
        send = self.send.at[self.group, z, slot]
        recv = self.recv.at[self.group, z, slot % 8]
        source = self.mine if self.mine is not None and slot in (1, 2, 4) else part
        return remote(source, part, send, recv, target)

    def turn(self, z):
        p = self.place
        odd = self.odd(z)
        a = p.a * odd + (1 - p.a) * (1 - odd)
        b = p.b * (1 - odd) + (1 - p.b) * odd
        target = odd * p.to_a[0] + (1 - odd) * p.to_b[0]
        return self.pass_on(z, 3, a, b, p.core, (target, p.z))

    def hand_out(self, z):
        p = self.place
        self.pass_on(z, 1, p.a, p.b, p.core, p.to_a).start()
        self.pass_on(z, 2, p.a, p.b, p.core, p.to_b).start()
        self.pass_on(z, 4, p.a, p.b, p.core, p.to_core).start()

    def second(self, z):
        p = self.place
        self.pass_on(z, 1, 1 - p.a, p.b, p.core, p.to_a).wait_recv()
        self.pass_on(z, 2, p.a, 1 - p.b, p.core, p.to_b).wait_recv()
        self.turn(z).start()
        self.pass_on(z, 5, 1 - p.a, p.b, p.core, p.to_core).start()
        self.pass_on(z, 6, p.a, 1 - p.b, p.core, p.to_core).start()

    def third(self, z):
        p = self.place
        self.pass_on(z, 3, 1 - p.a, 1 - p.b, p.core, p.to_a).wait_recv()
        self.pass_on(z, 7, 1 - p.a, 1 - p.b, p.core, p.to_core).start()

    def last(self, z):
        p = self.place
        side = 1 - p.core
        self.pass_on(z, 4, p.a, p.b, side, p.to_core).wait_recv()
        self.pass_on(z, 5, 1 - p.a, p.b, side, p.to_core).wait_recv()
        self.pass_on(z, 6, p.a, 1 - p.b, side, p.to_core).wait_recv()
        self.pass_on(z, 7, 1 - p.a, 1 - p.b, side, p.to_core).wait_recv()

    def sent(self, z):
        p = self.place
        self.pass_on(z, 1, p.a, p.b, p.core, p.to_a).wait_send()
        self.pass_on(z, 2, p.a, p.b, p.core, p.to_b).wait_send()
        self.turn(z).wait_send()
        self.pass_on(z, 4, p.a, p.b, p.core, p.to_core).wait_send()
        self.pass_on(z, 5, 1 - p.a, p.b, p.core, p.to_core).wait_send()
        self.pass_on(z, 6, p.a, 1 - p.b, p.core, p.to_core).wait_send()
        self.pass_on(z, 7, 1 - p.a, 1 - p.b, p.core, p.to_core).wait_send()


class Gather(Spread):
    def along(self, z):
        p = self.place
        part = self.piece(p.z, p.a, p.b, p.core)
        send, recv = self.send.at[self.group, z, 0], self.recv.at[self.group, p.z, 0]
        return remote(part, part, send, recv, (p.dp, z))

    def onward(self, z):
        p = self.place
        target = jnp.where(z < p.z, p.z + 1, p.z - 1)
        copy = self.pass_on(z, 8, p.a, p.b, p.core, (p.dp, target))
        return (target >= 0) & (target < p.n_tensor), copy

    def start(self):
        p = self.place
        for z in (p.z - 1, p.z + 1):
            pl.when((z >= 0) & (z < p.n_tensor))(self.along(z).start)

    def first(self, z):
        p = self.place
        self.pass_on(z, 0, p.a, p.b, p.core, p.to_core).wait_recv()
        there, copy = self.onward(z)
        pl.when(there)(copy.start)
        self.hand_out(z)

    def finish(self):
        p = self.place
        for z in (p.z - 1, p.z + 1):
            pl.when((z >= 0) & (z < p.n_tensor))(self.along(z).wait_send)
        for z in p.others:
            there, copy = self.onward(z)
            pl.when(there)(copy.wait_send)
            self.sent(z)


FORWARD_PLAN = (
    {
        4: (0,),
        19: (100, 1, 10, 200, 2, 300,),
        10: (101,),
        11: (11,),
        14: (110,),
        29: (12, 102, 201, 301,),
        20: (111,),
        21: (20,),
        23: (210,),
        39: (310, 202, 21, 112, 302,),
        30: (211,),
        31: (22,),
        33: (311,),
        34: (120,),
        40: (121, 212,),
        41: (312, 122, 220, 221, 320,),
        42: (222, 321,),
        43: (322,),
    },
    {
        4: (0, 1,),
        19: (2, 100, 10, 11, 101, 12, 102, 200, 300,),
        10: (110,),
        12: (20,),
        13: (111,),
        29: (202, 201, 21, 302, 301,),
        20: (22, 112, 210,),
        23: (120,),
        24: (310,),
        30: (211,),
        33: (311,),
        35: (121,),
        40: (122, 212,),
        41: (220, 312, 320,),
        42: (221, 222, 321,),
        43: (322,),
    },
)


def in_bands(start, count, work):
    band = 96

    def one(at, carry):
        offset = pl.multiple_of(at * band, 16)
        work(pl.ds(pl.multiple_of(start + offset, 16), band), pl.ds(offset, band))
        return carry

    lax.fori_loop(0, count // band, one, 0)


class Reduce:
    def __init__(self, place, grads, lands, pieces, send, recv, wide, group, block, near_land=None):
        matrix, base, size = block
        self.near_land = near_land
        self.near = place.others[0]
        self.far = place.others if near_land is None else place.others[1:]
        self.place, self.send, self.recv, self.group = place, send, recv, group
        self.half, self.quarter, self.side = size // 2, size // 4, grads.shape[3] // 2

        def rows(ref, parts):
            return ref.at[matrix, :, pl.ds(base // parts, size // parts)]

        core_land, first_land, second_land, far_land = lands
        self.grads = rows(grads, 1)
        self.core_land = core_land.at[max(matrix - 1, 0)]
        self.first_land, self.second_land, self.far_land = (
            rows(first_land, 2),
            rows(second_land, 4),
            rows(far_land, 4),
        )
        self.piece = pieces.at[matrix, pl.ds(base // 4, size // 4)]
        self.wide_flips, wide_out, wide_land, self.wide_send, self.wide_recv = wide
        if self.wide_flips:
            self.wide_out, self.wide_land = rows(wide_out, 4), rows(wide_land, 4)

    def columns(self, side):
        return pl.ds(pl.multiple_of(side * self.side, 128), self.side)

    def axes(self, z):
        p = self.place
        odd = lax.rem(z + self.group, 2)
        ahead, behind = odd * p.b + (1 - odd) * p.a, odd * p.a + (1 - odd) * p.b
        to_first = odd * p.to_b[0] + (1 - odd) * p.to_a[0]
        to_second = odd * p.to_a[0] + (1 - odd) * p.to_b[0]
        return ahead, behind, (to_first, p.z), (to_second, p.z)

    def rows(self, start, size):
        return pl.ds(pl.multiple_of(start, 16), size)

    def copy(self, z, slot, source, target_ref, target):
        send, recv = self.send.at[self.group, z, slot], self.recv.at[self.group, z, slot]
        return remote(source, target_ref, send, recv, target)

    def core_copy(self, z):
        p = self.place
        source = self.grads.at[z, :, self.columns(1 - p.core)]
        return self.copy(z, 0, source, self.core_land.at[z], p.to_core)

    def first_copy(self, z):
        ahead, _, target, _ = self.axes(z)
        source = self.core_land.at[z, self.rows((1 - ahead) * self.half, self.half)]
        return self.copy(z, 1, source, self.first_land.at[z], target)

    def second_copy(self, z):
        ahead, behind, _, target = self.axes(z)
        start = ahead * self.half + (1 - behind) * self.quarter
        source = self.core_land.at[z, self.rows(start, self.quarter)]
        return self.copy(z, 2, source, self.second_land.at[z], target)

    def kept_start(self, z):
        ahead, behind, _, _ = self.axes(z)
        return ahead * self.half + behind * self.quarter

    def kept(self, z):
        return self.rows(self.kept_start(z), self.quarter)

    def far_slot(self, source, target):
        return lax.rem(source - target + self.place.n_tensor, self.place.n_tensor) - 1

    def far_copy(self, z):
        p, group = self.place, self.group
        source = self.core_land.at[z, self.kept(z)]
        send, recv = self.send.at[group, z, 3], self.recv.at[group, p.z, 3]
        return remote(source, self.far_land.at[self.far_slot(p.z, z)], send, recv, (p.dp, z))

    def far_arrival(self, z):
        p, group = self.place, self.group
        land = self.far_land.at[self.far_slot(z, p.z)]
        return remote(land, land, self.send.at[group, z, 3], self.recv.at[group, z, 3], (p.dp, z))

    def wide_copy(self, at):
        group = self.group
        sems = self.wide_send.at[group, at], self.wide_recv.at[group, at]
        target = (self.wide_flips[at], self.place.z)
        return remote(self.wide_out.at[at], self.wide_land.at[at], *sems, target)

    def start(self, z):
        self.core_copy(z).start()

    def add(self, target, start, count, other):
        def work(rows, part):
            target[rows] = target[rows] + other[part]

        in_bands(start, count, work)

    def near_copy(self):
        p, group = self.place, self.group
        sems = self.send.at[group, self.near, 3], self.recv.at[group, p.z, 3]
        return remote(self.core_land.at[self.near], self.near_land, *sems, (p.dp, self.near))

    def near_arrival(self):
        p, group = self.place, self.group
        sems = self.send.at[group, self.near, 3], self.recv.at[group, self.near, 3]
        return remote(self.near_land, self.near_land, *sems, (p.dp, self.near))

    def first(self, z):
        p = self.place
        self.core_copy(z).wait_recv()
        mine = self.grads.at[z, :, self.columns(p.core)]
        land = self.core_land.at[z]
        self.add(land, 0, 2 * self.half, mine)
        if self.near_land is not None and z is self.near:
            self.near_copy().start()
            return
        if self.near_land is not None and z is p.z:
            self.near_arrival().wait_recv()
            self.add(land, 0, 2 * self.half, self.near_land)
        self.first_copy(z).start()

    def second(self, z):
        ahead, _, _, _ = self.axes(z)
        self.first_copy(z).wait_recv()
        land = self.core_land.at[z]
        self.add(land, ahead * self.half, self.half, self.first_land.at[z])
        self.second_copy(z).start()

    def third(self, z):
        self.second_copy(z).wait_recv()
        land = self.core_land.at[z]
        self.add(land, self.kept_start(z), self.quarter, self.second_land.at[z])
        if z is not self.place.z:
            self.far_copy(z).start()

    def fourth(self):
        p = self.place
        for z in self.far:
            self.far_arrival(z).wait_recv()

        def gather_up(rows, part):
            total = self.core_land[p.z, rows].astype(HIGH)
            for z in self.far:
                total = total + self.far_land[self.far_slot(z, p.z), part].astype(HIGH)
            self.piece[part] = total.astype(LOW)

        in_bands(self.kept_start(p.z), self.quarter, gather_up)
        for at in range(len(self.wide_flips)):
            copy = self.wide_copy(at)

            def set_out(rows, part, at=at):
                self.wide_out[at, part] = self.piece[part]

            def take_in(rows, part, at=at):
                self.piece[part] = self.wide_out[at, part] + self.wide_land[at, part]

            in_bands(0, self.quarter, set_out)
            copy.start()
            copy.wait_recv()
            in_bands(0, self.quarter, take_in)

    def finish(self):
        p = self.place
        for z in [p.z] + p.others:
            self.core_copy(z).wait_send()
        for z in [p.z] + self.far:
            self.first_copy(z).wait_send()
            self.second_copy(z).wait_send()
        for z in self.far:
            self.far_copy(z).wait_send()
        if self.near_land is not None:
            self.near_copy().wait_send()
        for at in range(len(self.wide_flips)):
            self.wide_copy(at).wait_send()


class Return(Spread):
    def __init__(self, place, whole, pieces, send, recv, keep_sem, group, block):
        super().__init__(place, whole, send, recv, group, block)
        self.mine = pieces.at[self.matrix, pl.ds(self.base // 4, self.quarter)]
        p = place
        self.keep = pltpu.make_async_copy(self.mine, self.piece(0, p.a, p.b, p.core), keep_sem.at[group])

    def hand_out(self, z):
        super().hand_out(z)
        self.keep.start()

    def sent(self, z):
        super().sent(z)
        self.keep.wait()

    def odd(self, z):
        return lax.rem(self.place.z + self.group, 2)


class Fold:
    def __init__(self, place, flips, stages, lands, far, send, recv):
        self.place, self.flips, self.bits = place, flips, len(flips)
        self.stages, self.lands, self.far, self.send, self.recv = stages, lands, far, send, recv

    def copy(self, bit):
        sems = self.send.at[bit], self.recv.at[bit]
        return remote(self.stages.at[bit], self.lands.at[bit], *sems, (self.flips[bit], self.place.z))

    def start(self):
        self.copy(0).start()

    def fold(self, bit):
        self.copy(bit).wait_recv()
        self.stages[bit + 1] = self.stages[bit] + self.lands[bit]
        if bit + 1 < self.bits:
            self.copy(bit + 1).start()
        else:
            for z in self.place.others:
                self.far_copy(z).start()
            self.far[self.place.z] = self.tile(self.place.z)[...]

    def tile(self, z):
        return self.stages.at[self.bits, z if self.stages.shape[1] > 1 else 0]

    def far_copy(self, z):
        p = self.place
        sems = self.send.at[self.bits + z], self.recv.at[self.bits + p.z]
        return remote(self.tile(z), self.far.at[p.z], *sems, (p.dp, z))

    def total(self):
        p = self.place
        for z in p.others:
            sems = self.send.at[self.bits + z], self.recv.at[self.bits + z]
            remote(self.tile(z), self.far.at[z], *sems, (p.dp, z)).wait_recv()
        total = self.far[0]
        for z in range(1, self.far.shape[0]):
            total = total + self.far[z]
        return total

    def finish(self):
        for bit in range(self.bits):
            self.copy(bit).wait_send()
        for z in self.place.others:
            self.far_copy(z).wait_send()


BACKWARD_PLAN = (
    {
        11: (30,),
        20: (20, 32,),
        21: (22,),
        30: (31,),
        31: (21,),
        50: (33,),
        106: (130,),
        103: (122,),
        107: (23, 132,),
        116: (131,),
        110: (0,),
        111: (10,),
        112: (121,),
        115: (133, 222,),
        126: (230,),
        121: (2, 12,),
        122: (123, 232,),
        125: (100, 231,),
        136: (110, 221,),
        131: (1, 11,),
        132: (102, 233,),
        134: (333, 223, 112, 323,),
        137: (210, 200,),
        200: (111, 101, 3, 202, 701, 13,),
        201: (212, 433, 423, 201, 211, 702,),
        202: (113, 103, 523, 533, 203, 213,),
        203: (303, 313, 623, 703, 633, 403, 413,),
        204: (503, 513, 603, 613,),
    },
    {
        11: (30,),
        20: (20, 32,),
        21: (22,),
        30: (31,),
        31: (21,),
        50: (33,),
        106: (130,),
        101: (132,),
        107: (23, 122, 121,),
        110: (0,),
        111: (10,),
        112: (131,),
        114: (133,),
        115: (232,),
        117: (230,),
        121: (2, 12, 222,),
        122: (123,),
        123: (100,),
        125: (221,),
        127: (231,),
        136: (110,),
        130: (112,),
        131: (1, 11, 233,),
        133: (223,),
        135: (102, 210,),
        137: (101, 200, 212,),
        200: (202, 333, 3, 13, 701, 111,),
        201: (201, 323, 433, 113, 103, 702,),
        202: (211, 423, 203, 303, 533, 213,),
        203: (633, 523, 313, 703, 403, 623, 413,),
        204: (503, 513, 603, 613,),
    },
)


def layer_kernel(
    n_tensor,
    heads,
    scale,
    layer_input,
    segment_ids,
    local_qkv,
    w_out,
    w_up,
    w_down,
    in_cotangent,
    local_small,
    out_bias,
    norm1_gain,
    norm1_bias,
    down_bias,
    norm2_gain,
    norm2_bias,
    out_layer,
    out_partial,
    out_landed,
    out_summed,
    out_sums,
    small,
    weights,
    core_land,
    first_land,
    second_land,
    far_land,
    near_land,
    pieces,
    activation,
    slope,
    row_input,
    bias,
    q_and_mixed,
    k_and_v,
    totals,
    head_totals,
    queries,
    keys,
    values,
    grad_mixed,
    grad_k,
    grad_v,
    inverse,
    live_rows,
    terms,
    hidden_low,
    grad_low,
    spare,
    sums,
    sums_land,
    sums_far,
    late_sums,
    late_land,
    late_far,
    wide_out,
    wide_land,
    gather_send,
    gather_recv,
    small_send,
    small_recv,
    copy_sem,
    send,
    recv,
    final_send,
    final_recv,
    wide_send,
    wide_recv,
    term_send,
    term_recv,
    sums_send,
    sums_recv,
    late_send,
    late_recv,
    save_sem,
    keep_sem,
):
    place = Place(n_tensor)
    share = hidden_low.shape[0]
    length, width = row_input.shape
    shares_per_row = length // share
    group_rows = k_and_v.shape[2] // 2
    size = group_rows // heads
    my_share = lax.rem(place.z, shares_per_row)
    in_row = pl.ds(pl.multiple_of(my_share * share, share), share)
    row_start = pl.multiple_of(place.z // shares_per_row * length, length)
    near, middle, far = place.others
    bits = sums_land.shape[0]
    flips = [place.dp + (1 << bit) - (2 << bit) * lax.rem(place.dp // (1 << bit), 2) for bit in range(bits)]

    accum, xhat = terms.at[0], terms.at[1]

    mine = weights.at[0, place.z]
    pairs = [
        (local_qkv, mine.at[pl.ds(0, 3 * group_rows)]),
        (w_out, mine.at[pl.ds(3 * group_rows, group_rows)]),
        (w_up, weights.at[1, place.z]),
        (w_down, weights.at[2, place.z]),
    ]
    own = [
        pltpu.make_async_copy(source, target, copy_sem.at[at]) for at, (source, target) in enumerate(pairs)
    ]
    load_input = pltpu.make_async_copy(
        layer_input.at[pl.ds(row_start, length)], row_input, copy_sem.at[4]
    )
    for copy in own:
        copy.start()
    load_input.start()
    load_cotangent = pltpu.make_async_copy(in_cotangent, spare.at[0], copy_sem.at[5])
    load_cotangent.start()
    partners = [(flip, place.z) for flip in flips] + [(place.dp, z) for z in place.others]
    greet(partners)
    meet(partners)
    gathers = [Gather(place, weights, gather_send, gather_recv, group, (group, 0, width)) for group in range(3)]
    gather_a, gather_b, gather_c = gathers

    def small_copy(z):
        sems = small_send.at[z], small_recv.at[place.z]
        return remote(local_small, small.at[place.z], *sems, (place.dp, z))

    def small_arrival(z):
        return remote(local_small, small.at[z], small_send.at[z], small_recv.at[z], (place.dp, z))

    own[0].wait()
    own[1].wait()
    gather_a.start()
    for z in place.others:
        small_copy(z).start()
    small[place.z] = local_small[...]
    own_start = pl.multiple_of(place.z * share, share)
    own_segments, row_segments = segment_rows(segment_ids, own_start, share, row_start, length)
    bias[...] = segment_bias(own_segments, row_segments)
    live_rows[...] = (own_segments >= 0).astype(HIGH)
    load_input.wait()

    at_end = (place.z == 0) | (place.z == n_tensor - 1)

    def pass_pieces(slot, there=True):
        for inside, plan in enumerate(FORWARD_PLAN):
            steps = plan.get(slot, ())
            if not steps:
                continue

            def run(steps=steps):
                for step in steps:
                    part = gathers[step // 10 % 10]
                    stage = (part.first, part.second, part.third, part.last)[step // 100]
                    stage(place.others[step % 10])

            pl.when(jnp.logical_and(at_end != bool(inside), there))(run)

    def start_b():
        own[2].wait()
        gather_b.start()

    def start_c():
        own[3].wait()
        gather_c.start()

    def attend_forward(turn, z):
        q_rows, k_rows, v_rows = (
            jnp.concatenate([weights[0, z, pl.ds((3 * head + kind) * size, size)] for head in range(heads)], axis=0)
            for kind in range(3)
        )
        q_bias, v_bias = small[z, 0:1, :group_rows], small[z, 1:2, :group_rows]
        x_row = row_input[...]
        q = (dot_nt(row_input[in_row], q_rows) + q_bias).astype(LOW) * scale
        k = dot_nt(x_row, k_rows).astype(LOW)
        v = (dot_nt(x_row, v_rows) + v_bias).astype(LOW)
        k_and_v[z] = jnp.concatenate([k, v], axis=1)
        for head in range(heads):
            part = slice(head * size, (head + 1) * size)
            queries[head], keys[head], values[head] = q[:, part], k[:, part], v[:, part]

        def one_head(head, carry):
            chunk = share // 2
            for part in range(2):
                rows = pl.ds(part * chunk, chunk)
                scores = dot_nt(queries[head, rows], keys[head]) + bias[rows]
                top = jnp.max(scores, axis=-1, keepdims=True)
                raised = jnp.exp(scores - top)
                total = jnp.sum(raised, axis=-1, keepdims=True)
                summed = dot_nn(raised.astype(LOW), values[head])
                grad_mixed[head, rows] = (summed / total).astype(LOW)
                head_totals[head, rows] = top + jnp.log(total)
                for index in range(heads):
                    pass_pieces(10 * turn + 2 * index + part, head == index)
                    if (turn, index, part) == (1, 0, 1):
                        pl.when(head == index)(start_c)
            return carry

        lax.fori_loop(0, heads, one_head, 0)
        columns = [queries[head] for head in range(heads)] + [grad_mixed[head] for head in range(heads)]
        q_and_mixed[z] = jnp.concatenate(columns, axis=-1)
        totals[z] = jnp.concatenate([head_totals[head] for head in range(heads)], axis=-1)

    attend_forward(0, place.z)
    start_b()
    pass_pieces(19)
    for z in place.others:
        small_arrival(z).wait_recv()
    attend_forward(1, near)
    pass_pieces(29)
    attend_forward(2, middle)
    pass_pieces(39)
    attend_forward(3, far)

    band = min(128, share)
    own_first = my_share * share
    out_shift, gain_first, shift_first = as_row(out_bias), as_row(norm1_gain), as_row(norm1_bias)
    down_shift = as_row(down_bias)

    def project_out(at, carry):
        rows = pl.ds(pl.multiple_of(at * band, band), band)
        own_rows = pl.ds(pl.multiple_of(own_first + at * band, band), band)
        first_sum = row_input[own_rows].astype(HIGH) + out_shift
        for z in range(n_tensor):
            first_sum = first_sum + dot_nn(q_and_mixed[z, rows, group_rows:], weights[0, z, 3 * group_rows :])
        normed, spread = norm_forward(first_sum)
        xhat[rows] = normed
        inverse[rows] = spread
        hidden = normed * gain_first + shift_first
        hidden_low[rows] = hidden.astype(LOW)
        accum[rows] = hidden + down_shift
        return carry

    lax.fori_loop(0, share // band, project_out, 0)

    def feed_forward(at, carry):
        z = place.pick(at, [place.z] + place.others)

        for index in range(n_tensor):
            pass_pieces(40 + index, at == index)
        pl.when(at == 1)(gather_a.finish)
        pl.when(at == 2)(gather_b.finish)
        raw = dot_nn(hidden_low[...], weights[1, z]) + small[z, 2:3]
        value, rise = gelu_parts(raw)
        activation[z] = value.astype(LOW)
        slope[z] = rise.astype(LOW)
        accum[...] += dot_nn(activation[z], weights[2, z])
        return carry

    lax.fori_loop(0, n_tensor, feed_forward, 0)
    gather_c.finish()

    order = [near, far, middle, place.z]
    lands = (core_land, first_land, second_land, far_land)
    wide = (flips[3:], wide_out, wide_land, wide_send, wide_recv)
    blocks = [(0, 0, width // 2), (0, width // 2, width // 2), (1, 0, width), (2, 0, width)]
    reduces = [
        Reduce(place, weights, lands, pieces, send, recv, wide, group, block, near_land if group == 2 else None)
        for group, block in enumerate(blocks)
    ]
    for half in range(2):
        side = pl.ds(half * width // 2, width // 2)
        reduces[half].core_land = activation.at[:, pl.ds(0, width // 2), side]
    returns = [
        Return(place, out_summed, pieces, final_send, final_recv, keep_sem, group, block)
        for group, block in enumerate(blocks)
    ]
    first_half, second_half, reduce_b, reduce_c = reduces
    fold = Fold(place, flips, sums, sums_land, sums_far, sums_send, sums_recv)
    late_fold = Fold(place, flips, late_sums, late_land, late_far, late_send, late_recv)
    sums[0] = jnp.zeros(sums.shape[1:], HIGH)
    late_sums[0] = jnp.zeros(late_sums.shape[1:], HIGH)

    shards = (near, middle, far, place.z)

    def finish_sum(reduce, spread):
        reduce.fourth()
        spread.hand_out(0)

    def take(step):
        stage, block, shard = step // 100, step // 10 % 10, step % 10
        if stage == 7:
            return next_term(shard)
        reduce, spread = reduces[block], returns[block]
        if stage < 3:
            return (reduce.first, reduce.second, reduce.third)[stage](shards[shard])
        if stage == 3:
            return finish_sum(reduce, spread)
        return (spread.second, spread.third, spread.last)[stage - 4](0)

    def serve(slot, there=True):
        for inside, plan in enumerate(BACKWARD_PLAN):
            steps = plan.get(slot, ())
            if not steps:
                continue

            def run(steps=steps):
                for step in steps:
                    take(step)

            pl.when(jnp.logical_and(at_end != bool(inside), there))(run)

    def serve_loop(at, slot):
        for index in range(n_tensor):
            serve(10 * index + slot, at == index)

    gain_second, shift_second = as_row(norm2_gain), as_row(norm2_bias)

    load_cotangent.wait()
    def second_norm(at, carry):
        rows = pl.ds(pl.multiple_of(at * band, band), band)
        normed, spread = norm_forward(accum[rows])
        cotangent = spare[0, rows].astype(HIGH) * live_rows[rows]
        spare[0, rows] = (normed * gain_second + shift_second).astype(LOW)
        grad_second = norm_backward(normed, spread, cotangent * gain_second)
        sums[0, 0, 6:7] += column_sum(cotangent * normed)
        sums[0, 0, 7:8] += column_sum(cotangent)
        sums[0, 0, 5:6] += column_sum(grad_second)
        grad_low[rows] = grad_second.astype(LOW)
        accum[rows] = grad_second
        return carry

    lax.fori_loop(0, share // band, second_norm, 0)
    save_layer = pltpu.make_async_copy(spare.at[0], out_layer, save_sem.at[0])
    save_layer.start()

    def feed_backward(at, carry):
        z = place.pick(at, order)
        low = grad_low[...]
        grad_up = (dot_nt(low, weights[2, z]) * slope[z].astype(HIGH)).astype(LOW)
        weights[2, z] = dot_tn(activation[z], low).astype(LOW)
        reduce_c.start(z)
        serve_loop(at, 0)
        accum[...] += dot_nt(grad_up, weights[1, z])
        weights[1, z] = dot_tn(hidden_low[...], grad_up).astype(LOW)
        reduce_b.start(z)
        sums[0, z, 1:2] = column_sum(grad_up.astype(HIGH))
        serve_loop(at, 1)
        return carry

    lax.fori_loop(0, n_tensor, feed_backward, 0)

    def first_norm(at, carry):
        rows = pl.ds(pl.multiple_of(at * band, band), band)
        grad_hidden, normed = accum[rows], xhat[rows]
        grad_first = norm_backward(normed, inverse[rows], grad_hidden * gain_first)
        sums[0, 0, 2:3] += column_sum(grad_first)
        sums[0, 0, 3:4] += column_sum(grad_hidden * normed)
        sums[0, 0, 4:5] += column_sum(grad_hidden)
        accum[rows] = grad_first
        grad_low[rows] = grad_first.astype(LOW)
        return carry

    lax.fori_loop(0, share // band, first_norm, 0)
    for step in range(1, shares_per_row):
        terms[step] = jnp.zeros(accum.shape, HIGH)
    for z in range(1, n_tensor):
        sums[0, z, 2:8] = sums[0, 0, 2:8]
    fold.start()
    serve(50)

    parts = 4
    part_rows = share // parts

    def term_copy(step, part):
        rows = pl.ds(part * part_rows, part_rows)
        partner = place.z - my_share + lax.rem(my_share + step, shares_per_row)
        sems = term_send.at[step - 1, part], term_recv.at[step - 1, part]
        return remote(spare.at[step - 1, rows], out_landed.at[step - 1, rows], *sems, (place.dp, partner))

    def fold_some(turn):
        for bit in range(bits):
            if min(bit, 2) == turn:
                fold.fold(bit)

    def send_terms():
        save_layer.wait()
        for step in range(1, shares_per_row):
            spare[step - 1] = terms[step].astype(LOW)
            term_copy(step, 0).start()

    def next_term(part):
        for step in range(1, shares_per_row):
            term_copy(step, part).start()

    def attend_backward(at, carry):
        z = place.pick(at, order)
        incoming = dot_nt(grad_low[...], weights[0, z, 3 * group_rows :]).astype(LOW)
        weights[0, z, 3 * group_rows :] = dot_tn(q_and_mixed[z, :, group_rows:], grad_low[...]).astype(LOW)
        for head in range(heads):
            part = slice(head * size, (head + 1) * size)
            queries[head], grad_mixed[head] = q_and_mixed[z, :, part], incoming[:, part]
            keys[head], values[head] = k_and_v[z, :, part], k_and_v[z, :, group_rows:][:, part]
            head_totals[head] = totals[z, :, head : head + 1]
        serve_loop(at, 106)

        def one_head(head, inner):
            k, v = keys[head], values[head]
            grad_kt = jnp.zeros((size, length), HIGH)
            grad_vt = jnp.zeros((size, length), HIGH)
            chunk = share // 2
            for part in range(2):
                rows = pl.ds(part * chunk, chunk)
                q, up = queries[head, rows], grad_mixed[head, rows]
                chance = jnp.exp(dot_nt(q, k) + bias[rows] - head_totals[head, rows])
                change = chance * dot_nt(up, v)
                change = change - chance * jnp.sum(change, axis=-1, keepdims=True)
                change = change.astype(LOW)
                grad_kt = grad_kt + dot_nn(q.T, change)
                grad_vt = grad_vt + dot_nn(up.T, chance.astype(LOW))
                grad_mixed[head, rows] = (dot_nn(change, k) * scale).astype(LOW)
                for index in range(heads):
                    for turn in range(n_tensor):
                        serve(100 + 10 * turn + 2 * index + part, (head == index) & (at == turn))
            grad_k[head] = grad_kt.astype(LOW)
            grad_v[head] = grad_vt.astype(LOW)
            for turn, bit in ((0, 0), (1, 1), (2, 2)):
                pl.when((head == heads - 1) & (at == turn))(functools.partial(fold_some, bit))
            return inner

        lax.fori_loop(0, heads, one_head, 0)
        dq = jnp.concatenate([grad_mixed[head] for head in range(heads)], axis=-1)
        dk = grad_k[...].reshape(group_rows, length)
        dv = grad_v[...].reshape(group_rows, length)
        x_row = row_input[...]
        q_rows, k_rows, v_rows = (
            jnp.concatenate([weights[0, z, pl.ds((3 * head + kind) * size, size)] for head in range(heads)], axis=0)
            for kind in range(3)
        )

        def share_term(step):
            first_token = lax.rem(my_share + step, shares_per_row) * share
            tokens = pl.ds(pl.multiple_of(first_token, share), share)
            grad_keys = grad_k[:, :, tokens].reshape(group_rows, share)
            grad_values = grad_v[:, :, tokens].reshape(group_rows, share)
            return dot_tn(grad_keys, k_rows) + dot_tn(grad_values, v_rows)

        for step in range(1, shares_per_row):
            terms[step] += share_term(step)
        pl.when(at == n_tensor - 1)(send_terms)
        accum[...] += share_term(0) + dot_nn(dq, q_rows)
        for kind, (left, right) in enumerate(((dq.T, row_input[in_row]), (dk, x_row), (dv, x_row))):
            grad = dot_nn(left, right).astype(LOW)
            for head in range(heads):
                weights[0, z, pl.ds((3 * head + kind) * size, size)] = grad[head * size : (head + 1) * size]
        first_half.start(z)
        second_half.start(z)
        ones = jnp.ones((8, length), LOW)
        q_sums, v_sums = dot_nn(ones[:, :share], dq)[0:1], dot_nt(ones, dv)[0:1]
        for head in range(heads):
            part = slice(head * size, (head + 1) * size)
            pair = jnp.concatenate([q_sums[:, part], v_sums[:, part]], axis=1)
            at_row = lax.broadcasted_iota(jnp.int32, (8, 2 * size), 0) == z
            late_sums[0, 0, :, 2 * head * size : 2 * (head + 1) * size] += jnp.where(at_row, pair, 0.0)
        serve_loop(at, 107)
        return carry

    lax.fori_loop(0, n_tensor, attend_backward, 0)

    def keep_row(values, z):
        out_sums[0:1] = values[z : z + 1]

    late_fold.start()
    save_partial = pltpu.make_async_copy(accum, out_partial, save_sem.at[1])
    save_partial.start()
    for bit in range(bits):
        if bit < 3:
            serve(200 + bit)
        late_fold.fold(bit)
    serve(203)
    for step in range(1, shares_per_row):
        for part in range(parts):
            term_copy(step, part).wait_send()
            term_copy(step, part).wait_recv()
    out_sums[...] = fold.total()
    late_total = late_fold.total()
    for z in range(n_tensor):
        pl.when(place.z == z)(functools.partial(keep_row, late_total, z))
    fold.finish()
    late_fold.finish()
    for reduce in reduces:
        reduce.finish()
    serve(204)
    for part in returns:
        part.sent(0)
    for z in place.others:
        small_copy(z).wait_send()
    save_partial.wait()


def finish_kernel(
    heads,
    in_layer,
    in_partial,
    in_landed,
    in_summed,
    sums,
    out_layer,
    out_input,
    out_qkv,
    qv_bias,
    out_out,
    out_bias,
    gain_first,
    shift_first,
    out_up,
    up_bias,
    out_down,
    down_bias,
    gain_second,
    shift_second,
    layer,
    partial,
    landed,
    summed,
    qkv,
    rest,
    matrices,
    load_sem,
    save_sem,
):
    size = qkv.shape[1]
    pairs = [(in_summed.at[2, 0], summed.at[2]), (in_summed.at[1, 0], summed.at[1]), (in_partial, partial)]
    pairs += [(in_landed, landed), (in_summed.at[0, 0], summed.at[0]), (in_layer, layer)]
    loads = [
        pltpu.make_async_copy(source, target, load_sem.at[at]) for at, (source, target) in enumerate(pairs)
    ]
    for copy in loads:
        copy.start()
    for at, vector in enumerate(
        [up_bias, out_bias, gain_first, shift_first, down_bias, gain_second, shift_second]
    ):
        vector[...] = sums[1 + at : 2 + at].reshape(vector.shape)
    for head in range(heads):
        width = qv_bias.shape[1]
        qv_bias[head : head + 1] = sums[0:1, head * width : (head + 1) * width]
    saves = []

    def save(source, target):
        copy = pltpu.make_async_copy(source, target, save_sem.at[len(saves)])
        copy.start()
        saves.append(copy)

    for at, target in ((2, out_down), (1, out_up)):
        loads[2 - at].wait()
        matrices[at - 1] = summed[at].astype(HIGH)
        save(matrices.at[at - 1], target)
    loads[2].wait()
    loads[3].wait()
    for step in range(landed.shape[0]):
        partial[...] += landed[step].astype(HIGH)
    save(partial, out_input)
    loads[4].wait()
    rest[...] = summed[0, heads * size :].astype(HIGH)
    save(rest, out_out)
    for head in range(heads):
        qkv[head] = summed[0, head * size : (head + 1) * size].astype(HIGH)
    save(qkv, out_qkv)
    loads[5].wait()
    save(layer, out_layer)
    for copy in saves:
        copy.wait()


def on_device(
    layer_input,
    segment_ids,
    w_qkv,
    qv_bias,
    w_out,
    out_bias,
    norm1_gain,
    norm1_bias,
    w_up,
    up_bias,
    w_down,
    down_bias,
    norm2_gain,
    norm2_bias,
    out_cotangent,
):
    n_tensor = lax.axis_size("tensor")
    place = lax.axis_index("tensor")
    n_dp = lax.axis_size("dp")
    bits = n_dp.bit_length() - 1
    tokens, width = layer_input.shape
    share = tokens // n_tensor
    heads = qv_bias.shape[0]
    head_dim = qv_bias.shape[1] // 2
    score_scale = float(head_dim) ** (-0.5)
    shares_per_row = SEQ // share
    group_rows = heads * head_dim

    local_qkv = w_qkv.transpose(1, 2, 0).reshape(3 * group_rows, width)
    local_small = jnp.concatenate(
        [
            jnp.pad(qv_bias[:, :head_dim].reshape(1, -1), ((0, 0), (0, width - group_rows))),
            jnp.pad(qv_bias[:, head_dim:].reshape(1, -1), ((0, 0), (0, width - group_rows))),
            up_bias.reshape(1, -1),
            jnp.zeros((5, width), LOW),
        ]
    ).astype(HIGH)

    vmem = pl.BlockSpec(memory_space=pltpu.VMEM)
    anywhere = pl.BlockSpec(memory_space=pl.ANY)

    def low(*shape):
        return jax.ShapeDtypeStruct(shape, LOW)

    def high(*shape):
        return jax.ShapeDtypeStruct(shape, HIGH)

    def low_scratch(*shape):
        return pltpu.VMEM(shape, LOW)

    def high_scratch(*shape):
        return pltpu.VMEM(shape, HIGH)

    dma = pltpu.SemaphoreType.DMA
    side, quarter = width // 2, width // 4
    wide = bits - 3
    wide_shape = (3, wide, quarter, side) if wide else (3, 1, 64, 128)
    layer_output, partial, landed, summed, sums = pl.pallas_call(
        functools.partial(layer_kernel, n_tensor, heads, score_scale),
        out_shape=(
            low(share, width),
            high(share, width),
            low(shares_per_row - 1, share, width),
            low(3, 1, width, width),
            high(8, width),
        ),
        in_specs=[anywhere, vmem] + [anywhere] * 5 + [vmem] * 7,
        out_specs=(anywhere,) * 4 + (vmem,),
        scratch_shapes=[
            high_scratch(n_tensor, 8, width),
            low_scratch(3, n_tensor, width, width),
            low_scratch(2, n_tensor, width, side),
            low_scratch(3, n_tensor, 2 * quarter, side),
            low_scratch(3, n_tensor, quarter, side),
            low_scratch(3, n_tensor - 1, quarter, side),
            low_scratch(width, side),
            low_scratch(3, quarter, side),
            low_scratch(n_tensor, share, width),
            low_scratch(n_tensor, share, width),
            low_scratch(SEQ, width),
            high_scratch(share, SEQ),
            low_scratch(n_tensor, share, 2 * group_rows),
            low_scratch(n_tensor, SEQ, 2 * group_rows),
            high_scratch(n_tensor, share, heads),
            high_scratch(heads, share, 1),
            low_scratch(heads, share, head_dim),
            low_scratch(heads, SEQ, head_dim),
            low_scratch(heads, SEQ, head_dim),
            low_scratch(heads, share, head_dim),
            low_scratch(heads, head_dim, SEQ),
            low_scratch(heads, head_dim, SEQ),
            high_scratch(share, 1),
            high_scratch(share, 1),
            high_scratch(shares_per_row, share, width),
            low_scratch(share, width),
            low_scratch(share, width),
            low_scratch(shares_per_row - 1, share, width),
            high_scratch(bits + 1, n_tensor, 8, width),
            high_scratch(bits, n_tensor, 8, width),
            high_scratch(n_tensor, 8, width),
            high_scratch(bits + 1, 1, 8, width),
            high_scratch(bits, 1, 8, width),
            high_scratch(n_tensor, 8, width),
            low_scratch(*wide_shape),
            low_scratch(*wide_shape),
            dma((3, n_tensor, 9)),
            dma((3, n_tensor, 8)),
            dma((n_tensor,)),
            dma((n_tensor,)),
            dma((6,)),
            dma((4, n_tensor, 4)),
            dma((4, n_tensor, 4)),
            dma((4, 1, 9)),
            dma((4, 1, 8)),
            dma((4, max(wide, 1))),
            dma((4, max(wide, 1))),
            dma((shares_per_row - 1, 4)),
            dma((shares_per_row - 1, 4)),
            dma((bits + n_tensor,)),
            dma((bits + n_tensor,)),
            dma((bits + n_tensor,)),
            dma((bits + n_tensor,)),
            dma((3,)),
            dma((4,)),
        ],
        compiler_params=pltpu.CompilerParams(
            collective_id=0, has_side_effects=True, vmem_limit_bytes=VMEM_LIMIT
        ),
        name="layer",
    )(
        layer_input,
        segment_ids,
        local_qkv,
        w_out,
        w_up,
        w_down,
        out_cotangent,
        local_small,
        out_bias,
        norm1_gain,
        norm1_bias,
        down_bias,
        norm2_gain,
        norm2_bias,
    )

    vector = high(width)
    matrix = high(width, width)
    layer_output, input_grad, grad_qkv, *rest = pl.pallas_call(
        functools.partial(finish_kernel, heads),
        out_shape=(
            low(share, width),
            high(share, width),
            high(heads, 3 * head_dim, width),
            high(heads, 2 * head_dim),
            high(group_rows, width),
            vector,
            vector,
            vector,
            matrix,
            vector,
            matrix,
            vector,
            vector,
            vector,
        ),
        in_specs=[anywhere] * 4 + [vmem],
        out_specs=(anywhere,) * 3 + (vmem, anywhere, vmem, vmem, vmem, anywhere, vmem, anywhere, vmem, vmem, vmem),
        scratch_shapes=[
            low_scratch(share, width),
            high_scratch(share, width),
            low_scratch(shares_per_row - 1, share, width),
            low_scratch(3, width, width),
            high_scratch(heads, 3 * head_dim, width),
            high_scratch(group_rows, width),
            high_scratch(2, width, width),
            dma((6,)),
            dma((6,)),
        ],
        compiler_params=pltpu.CompilerParams(vmem_limit_bytes=VMEM_LIMIT),
        name="finish",
    )(layer_output, partial, landed, summed, sums)
    return (layer_output, input_grad, grad_qkv.transpose(2, 0, 1), *rest)


def solution(mesh):
    return jax.shard_map(
        on_device,
        mesh=mesh,
        in_specs=(
            P("dp", None),
            P("dp"),
            P(None, "tensor", None),
            P("tensor", None),
            P("tensor", None),
            P(),
            P(),
            P(),
            P(None, "tensor"),
            P("tensor"),
            P("tensor", None),
            P(),
            P(),
            P(),
            P(("dp", "tensor"), None),
        ),
        out_specs=(
            P(("dp", "tensor"), None),
            P(("dp", "tensor"), None),
            P(None, "tensor", None),
            P("tensor", None),
            P("tensor", None),
            P(),
            P(),
            P(),
            P(None, "tensor"),
            P("tensor"),
            P("tensor", None),
            P(),
            P(),
            P(),
        ),
        check_vma=False,
    )
```

time: 189 us -> 170 us (0.90)
  Pallas kernels: 185 us -> 167 us
    pallas_call x2 -> x1, Pallas kernels: 178 us -> 160 us  [on_device(): pl.pallas_call(functools.partial(layer_kernel, n_tensor, heads, score_sca...]
where the time goes in v5:
time: 170 us
  Pallas kernels  167 us (98%)
  local copies, waits for them, and re-layouts  1.76 us (1%)
    pallas_call x1, Pallas kernels, on_device(): pl.pallas_call(functools.partial(layer_kernel, n_tensor, heads, score_sca...  160 us
    pallas_call x1, Pallas kernels, on_device(): pl.pallas_call(functools.partial(finish_kernel, heads), out_shape=(low(sh...  6.6 us

profile of v5, /device:TPU:0, one launch (start us, length us, event | category | flops | bytes accessed | tf_op | source)
XLA Modules:
  0.0 170.1 jit_solution(11494933296908807473)
XLA Ops:
  0.7 0.1 pad.12.clone
  0.7 0.8 fusion.7
  1.6 0.1 reshape.41
  1.6 0.1 reshape.42
  1.7 0.7 reshape.43
  2.4 0.7 fusion.6.local_small
  3.1 160.2 %layer.1 = (bf16[512,768]{1,0:T(8,128)(2,1)}, f32[512,768]{1,0:T(8,128)}, bf16[1,512,768]{2,1,0:T(8,128)(2,1)}, bf16[3,1,768,768]{3,2,1,0:T(8,128)(2,1)}, f32[8,768]{1,0:T(8,128)}) custom-call(bf16[2048,768]{1,0:T(8,128)(2,1)} %layer_input.1, s32[2048]{0:T(1024)} %segment_ids.1, bf16[576,768]{1,0:T(8,128)(2,1)} %bitcast.4, bf16[192,768]{1,0:T(8,128)(2,1)} %w_out.1, ...), custom_call_target="tpu_custom_call" | custom-call | tf_op jit(solution)/shard_map/layer/pallas_call | solution.py:1203
  163.3 6.6 %finish.1 = (bf16[512,768]{1,0:T(8,128)(2,1)}, f32[512,768]{1,0:T(8,128)}, f32[3,192,768]{2,1,0:T(8,128)}, f32[3,128]{1,0:T(4,128)}, f32[192,768]{1,0:T(8,128)},...) custom-call(bf16[512,768]{1,0:T(8,128)(2,1)} %get-tuple-element.33.i, ...), custom_call_target="tpu_custom_call" | custom-call | tf_op jit(solution)/shard_map/finish/pallas_call | solution.py:1294
  (1 shorter events, 0.0 us)

commit v6 on v5

--- a/solution.py
+++ b/solution.py
@@ -240,9 +240,10 @@
         33: (311,),
         34: (120,),
         40: (121, 212,),
-        41: (312, 122, 220, 221, 320,),
-        42: (222, 321,),
-        43: (322,),
+        41: (312, 122,),
+        46: (220, 221, 320,),
+        47: (222, 321,),
+        48: (322,),
     },
     {
         4: (0, 1,),
@@ -258,9 +259,10 @@
         33: (311,),
         35: (121,),
         40: (122, 212,),
-        41: (220, 312, 320,),
-        42: (221, 222, 321,),
-        43: (322,),
+        41: (220, 312,),
+        46: (320,),
+        47: (221, 222, 321,),
+        48: (322,),
     },
 )
 
@@ -518,66 +520,64 @@
 
 BACKWARD_PLAN = (
     {
-        11: (30,),
-        20: (20, 32,),
-        21: (22,),
+        11: (32, 22,),
+        20: (30,),
+        21: (20,),
         30: (31,),
         31: (21,),
-        50: (33,),
-        106: (130,),
-        103: (122,),
-        107: (23, 132,),
-        116: (131,),
-        110: (0,),
-        111: (10,),
-        112: (121,),
-        115: (133, 222,),
-        126: (230,),
-        121: (2, 12,),
-        122: (123, 232,),
-        125: (100, 231,),
-        136: (110, 221,),
-        131: (1, 11,),
-        132: (102, 233,),
-        134: (333, 223, 112, 323,),
-        137: (210, 200,),
-        200: (111, 101, 3, 202, 701, 13,),
-        201: (212, 433, 423, 201, 211, 702,),
-        202: (113, 103, 523, 533, 203, 213,),
-        203: (303, 313, 623, 703, 633, 403, 413,),
-        204: (503, 513, 603, 613,),
+        50: (132, 122, 33,),
+        104: (130, 131,),
+        107: (232, 23,),
+        116: (121,),
+        110: (2, 12,),
+        112: (222,),
+        113: (133,),
+        117: (231, 230, 221,),
+        120: (0,),
+        121: (123, 102, 10,),
+        124: (112,),
+        125: (100,),
+        127: (233, 223, 202, 323, 333,),
+        136: (212,),
+        130: (1, 110, 11,),
+        132: (200,),
+        135: (423,),
+        137: (210, 433,),
+        200: (111, 3, 101, 13, 523,),
+        201: (701, 533, 201, 623, 211,),
+        202: (633, 113, 103, 702, 703,),
+        203: (213, 313, 203, 303, 413, 403,),
+        204: (513, 503, 613, 603,),
     },
     {
-        11: (30,),
-        20: (20, 32,),
-        21: (22,),
+        11: (32, 22,),
+        20: (30,),
+        21: (20,),
         30: (31,),
         31: (21,),
-        50: (33,),
-        106: (130,),
-        101: (132,),
-        107: (23, 122, 121,),
-        110: (0,),
-        111: (10,),
-        112: (131,),
-        114: (133,),
-        115: (232,),
-        117: (230,),
-        121: (2, 12, 222,),
-        122: (123,),
-        123: (100,),
-        125: (221,),
-        127: (231,),
-        136: (110,),
-        130: (112,),
-        131: (1, 11, 233,),
-        133: (223,),
-        135: (102, 210,),
-        137: (101, 200, 212,),
-        200: (202, 333, 3, 13, 701, 111,),
-        201: (201, 323, 433, 113, 103, 702,),
-        202: (211, 423, 203, 303, 533, 213,),
-        203: (633, 523, 313, 703, 403, 623, 413,),
+        50: (132, 122, 33,),
+        105: (130, 121,),
+        107: (222, 23,),
+        110: (131, 2, 12,),
+        113: (232, 133,),
+        117: (221, 230,),
+        126: (231,),
+        120: (0,),
+        121: (123, 112, 10,),
+        124: (102,),
+        125: (100,),
+        127: (233, 223,),
+        136: (212, 202,),
+        130: (1,),
+        131: (110, 11, 323,),
+        132: (200,),
+        134: (333,),
+        135: (101,),
+        137: (210, 111,),
+        200: (423, 701, 3, 13, 433,),
+        201: (201, 211, 103, 523, 702,),
+        202: (703, 623, 533, 113, 203,),
+        203: (303, 633, 213, 313, 403, 413,),
         204: (503, 513, 603, 613,),
     },
 )
@@ -594,7 +594,8 @@
     w_up,
     w_down,
     in_cotangent,
-    local_small,
+    qv_bias,
+    up_bias,
     out_bias,
     norm1_gain,
     norm1_bias,
@@ -606,6 +607,7 @@
     out_landed,
     out_summed,
     out_sums,
+    local_small,
     small,
     weights,
     core_land,
@@ -697,6 +699,12 @@
     load_cotangent.start()
     partners = [(flip, place.z) for flip in flips] + [(place.dp, z) for z in place.others]
     greet(partners)
+    biases = qv_bias[...].astype(HIGH)
+    local_small[...] = jnp.zeros(local_small.shape, HIGH)
+    for row in range(2):
+        parts = [biases[head : head + 1, row * size : (row + 1) * size] for head in range(heads)]
+        local_small[row : row + 1, :group_rows] = jnp.concatenate(parts, axis=1)
+    local_small[2:3] = as_row(up_bias)
     meet(partners)
     gathers = [Gather(place, weights, gather_send, gather_recv, group, (group, 0, width)) for group in range(3)]
     gather_a, gather_b, gather_c = gathers
@@ -824,13 +832,15 @@
         value, rise = gelu_parts(raw)
         activation[z] = value.astype(LOW)
         slope[z] = rise.astype(LOW)
+        for index in range(n_tensor):
+            pass_pieces(45 + index, at == index)
         accum[...] += dot_nn(activation[z], weights[2, z])
         return carry
 
     lax.fori_loop(0, n_tensor, feed_forward, 0)
     gather_c.finish()
 
-    order = [near, far, middle, place.z]
+    order = [far, near, middle, place.z]
     lands = (core_land, first_land, second_land, far_land)
     wide = (flips[3:], wide_out, wide_land, wide_send, wide_recv)
     blocks = [(0, 0, width // 2), (0, width // 2, width // 2), (1, 0, width), (2, 0, width)]
@@ -1172,15 +1182,6 @@
     group_rows = heads * head_dim
 
     local_qkv = w_qkv.transpose(1, 2, 0).reshape(3 * group_rows, width)
-    local_small = jnp.concatenate(
-        [
-            jnp.pad(qv_bias[:, :head_dim].reshape(1, -1), ((0, 0), (0, width - group_rows))),
-            jnp.pad(qv_bias[:, head_dim:].reshape(1, -1), ((0, 0), (0, width - group_rows))),
-            up_bias.reshape(1, -1),
-            jnp.zeros((5, width), LOW),
-        ]
-    ).astype(HIGH)
-
     vmem = pl.BlockSpec(memory_space=pltpu.VMEM)
     anywhere = pl.BlockSpec(memory_space=pl.ANY)
 
@@ -1209,9 +1210,10 @@
             low(3, 1, width, width),
             high(8, width),
         ),
-        in_specs=[anywhere, vmem] + [anywhere] * 5 + [vmem] * 7,
+        in_specs=[anywhere, vmem] + [anywhere] * 5 + [vmem] * 8,
         out_specs=(anywhere,) * 4 + (vmem,),
         scratch_shapes=[
+            high_scratch(8, width),
             high_scratch(n_tensor, 8, width),
             low_scratch(3, n_tensor, width, width),
             low_scratch(2, n_tensor, width, side),
@@ -1280,7 +1282,8 @@
         w_up,
         w_down,
         out_cotangent,
-        local_small,
+        qv_bias,
+        up_bias,
         out_bias,
         norm1_gain,
         norm1_bias,

time: 170 us -> 167 us (0.982)
  local copies, waits for them, and re-layouts: 1.76 us -> 0 us
where the time goes in v6:
time: 167 us
  Pallas kernels  166 us (99%)
    pallas_call x1, Pallas kernels, on_device(): pl.pallas_call(functools.partial(layer_kernel, n_tensor, heads, score_sca...  159 us
    pallas_call x1, Pallas kernels, on_device(): pl.pallas_call(functools.partial(finish_kernel, heads), out_shape=(low(sh...  6.6 us

profile of v6, /device:TPU:0, one launch (start us, length us, event | category | flops | bytes accessed | tf_op | source)
XLA Modules:
  0.0 166.5 jit_solution(8134264946134289839)
XLA Ops:
  0.7 159.1 %layer.1 = (bf16[512,768]{1,0:T(8,128)(2,1)}, f32[512,768]{1,0:T(8,128)}, bf16[1,512,768]{2,1,0:T(8,128)(2,1)}, bf16[3,1,768,768]{3,2,1,0:T(8,128)(2,1)}, f32[8,768]{1,0:T(8,128)}) custom-call(bf16[2048,768]{1,0:T(8,128)(2,1)} %layer_input.1, s32[2048]{0:T(1024)} %segment_ids.1, bf16[576,768]{1,0:T(8,128)(2,1)} %bitcast.4, bf16[192,768]{1,0:T(8,128)(2,1)} %w_out.1, ...), custom_call_target="tpu_custom_call" | custom-call | tf_op jit(solution)/shard_map/layer/pallas_call | solution.py:1204
  159.8 6.6 %finish.1 = (bf16[512,768]{1,0:T(8,128)(2,1)}, f32[512,768]{1,0:T(8,128)}, f32[3,192,768]{2,1,0:T(8,128)}, f32[3,128]{1,0:T(4,128)}, f32[192,768]{1,0:T(8,128)},...) custom-call(bf16[512,768]{1,0:T(8,128)(2,1)} %get-tuple-element.33.i, ...), custom_call_target="tpu_custom_call" | custom-call | tf_op jit(solution)/shard_map/finish/pallas_call | solution.py:1297

commit v7 on v6

--- a/solution.py
+++ b/solution.py
@@ -800,7 +800,7 @@
     pass_pieces(39)
     attend_forward(3, far)
 
-    band = min(128, share)
+    band = min(256, share)
     own_first = my_share * share
     out_shift, gain_first, shift_first = as_row(out_bias), as_row(norm1_gain), as_row(norm1_bias)
     down_shift = as_row(down_bias)
@@ -1028,13 +1028,13 @@
         for step in range(1, shares_per_row):
             terms[step] += share_term(step)
         pl.when(at == n_tensor - 1)(send_terms)
-        accum[...] += share_term(0) + dot_nn(dq, q_rows)
         for kind, (left, right) in enumerate(((dq.T, row_input[in_row]), (dk, x_row), (dv, x_row))):
             grad = dot_nn(left, right).astype(LOW)
             for head in range(heads):
                 weights[0, z, pl.ds((3 * head + kind) * size, size)] = grad[head * size : (head + 1) * size]
         first_half.start(z)
         second_half.start(z)
+        accum[...] += share_term(0) + dot_nn(dq, q_rows)
         ones = jnp.ones((8, length), LOW)
         q_sums, v_sums = dot_nn(ones[:, :share], dq)[0:1], dot_nt(ones, dv)[0:1]
         for head in range(heads):
@@ -1057,6 +1057,9 @@
         if bit < 3:
             serve(200 + bit)
         late_fold.fold(bit)
+    for reduce in reduces[2:]:
+        reduce.finish()
+    fold.finish()
     serve(203)
     for step in range(1, shares_per_row):
         for part in range(parts):
@@ -1066,11 +1069,10 @@
     late_total = late_fold.total()
     for z in range(n_tensor):
         pl.when(place.z == z)(functools.partial(keep_row, late_total, z))
-    fold.finish()
+    serve(204)
     late_fold.finish()
-    for reduce in reduces:
+    for reduce in reduces[:2]:
         reduce.finish()
-    serve(204)
     for part in returns:
         part.sent(0)
     for z in place.others:

time: 167 us -> 167 us (level)
  no operation moved by 1% of the time
where the time goes in v7:
time: 167 us; the launch traced here: 166 us
  Pallas kernels  166 us (99%)
    pallas_call x1, Pallas kernels, on_device(): pl.pallas_call(functools.partial(layer_kernel, n_tensor, heads, score_sca...  159 us
    pallas_call x1, Pallas kernels, on_device(): pl.pallas_call(functools.partial(finish_kernel, heads), out_shape=(low(sh...  6.6 us

profile of v7, /device:TPU:0, one launch (start us, length us, event | category | flops | bytes accessed | tf_op | source)
XLA Modules:
  0.0 166.4 jit_solution(8663429963860174128)
XLA Ops:
  0.7 158.9 %layer.1 = (bf16[512,768]{1,0:T(8,128)(2,1)}, f32[512,768]{1,0:T(8,128)}, bf16[1,512,768]{2,1,0:T(8,128)(2,1)}, bf16[3,1,768,768]{3,2,1,0:T(8,128)(2,1)}, f32[8,768]{1,0:T(8,128)}) custom-call(bf16[2048,768]{1,0:T(8,128)(2,1)} %layer_input.1, s32[2048]{0:T(1024)} %segment_ids.1, bf16[576,768]{1,0:T(8,128)(2,1)} %bitcast.4, bf16[192,768]{1,0:T(8,128)(2,1)} %w_out.1, ...), custom_call_target="tpu_custom_call" | custom-call | tf_op jit(solution)/shard_map/layer/pallas_call | solution.py:1206
  159.6 6.6 %finish.1 = (bf16[512,768]{1,0:T(8,128)(2,1)}, f32[512,768]{1,0:T(8,128)}, f32[3,192,768]{2,1,0:T(8,128)}, f32[3,128]{1,0:T(4,128)}, f32[192,768]{1,0:T(8,128)},...) custom-call(bf16[512,768]{1,0:T(8,128)(2,1)} %get-tuple-element.33.i, ...), custom_call_target="tpu_custom_call" | custom-call | tf_op jit(solution)/shard_map/finish/pallas_call | solution.py:1299
